TPU v7x, 512 devices: a whole 4x8x8 slice. The times are simulated.
512 devices in a mesh: seq: 512 (over x, y, z, core).
Axes of the slice: x: 4, y: 8, z: 8, core: 2. Of those that a mesh axis runs over, the one named last changes fastest.
Arguments:
- right_side: bfloat16 [262144, 384], P('seq'), may hold values from -6 to 6
- leaf_inverse: bfloat16 [512, 512, 512], P('seq'), may hold values from -1 to 2
- project_rows: bfloat16 [9, 262144, 128], P(None, 'seq'), may hold values from -3 to 3, as said below
- spread_rows: bfloat16 [9, 262144, 128], P(None, 'seq'), may hold values from -0.119628906 to 0.119628906
- capacity: bfloat16 [9, 65536, 256], P(None, 'seq'), may hold values from -1 to 2, as said below
Outputs:
- solution: float32 [262144, 384], P('seq')
Inputs may be any that keep to these rules, and one draw needn't show every extreme that they name: Rows of project_rows of level l have a scale falling as (2 ** l * 512) ** -0.5. `capacity`: at level l the 128 x 2 * 128 blocks of all devices in one half of a node of 2 ** (l + 1) devices are equal.
All inputs are finite; a program needn't handle non-finite values.
Results may differ from a plain program's by a relative error of at most 0.0095.
Values may be sent and summed in bfloat16 or wider, within the bound.
No kernel may reach another device: no remote copies, remote signals or barrier semaphores. Data moves between devices by JAX's collectives and lax.ppermute only.
A program may use at most 64 MiB of HBM per device.

v0:
```python
import jax
import jax.numpy as jnp
from jax import lax
from jax.sharding import PartitionSpec as P


def partner(value, axis, bit):
    mask = 2**bit
    pairs = [(source, source ^ mask) for source in range(lax.axis_size(axis))]
    return lax.ppermute(value, axis, pairs)


def pair_sums(partial_sum, tree_level, half_side):
    for bit_index in range(tree_level):
        partial_sum = partial_sum + partner(partial_sum, "seq", bit_index)
    own_sums = partial_sum.astype(jnp.bfloat16)
    partner_sums = partner(own_sums, "seq", tree_level)
    return jnp.where(
        half_side == 0,
        jnp.concatenate([own_sums, partner_sums], 0),
        jnp.concatenate([partner_sums, own_sums], 0),
    )


def on_device(right_side, leaf_inverse, project_rows, spread_rows, capacity):
    solution = jnp.dot(leaf_inverse[0], right_side, preferred_element_type=jnp.float32)
    device_index = lax.axis_index("seq")
    level_count = project_rows.shape[0]
    for tree_level in range(level_count):
        rounded = solution.astype(jnp.bfloat16)
        partial_sum = jnp.einsum(
            "sr,sk->rk", project_rows[tree_level], rounded, preferred_element_type=jnp.float32
        )
        half_side = device_index >> tree_level & 1
        stacked = pair_sums(partial_sum, tree_level, half_side)
        coefficients = jnp.dot(
            capacity[tree_level], stacked, preferred_element_type=jnp.float32
        ).astype(jnp.bfloat16)
        solution = solution - jnp.dot(
            spread_rows[tree_level], coefficients, preferred_element_type=jnp.float32
        )
    return solution


def solution(mesh):
    return jax.shard_map(
        on_device,
        mesh=mesh,
        in_specs=(
            P("seq", None),
            P("seq", None, None),
            P(None, "seq", None),
            P(None, "seq", None),
            P(None, "seq", None),
        ),
        out_specs=P("seq", None),
        check_vma=False,
    )
```

profile of v0, /device:TPU:1, one launch (start us, length us, event | category | flops | bytes accessed | tf_op | source)
XLA Modules:
  0.0 468.1 jit_solution(15777062063967980020)
XLA Ops:
  3.7 8.8 %collective-permute-start = (bf16[128,384]{1,0:T(8,128)(2,1)S(1)}, bf16[128,384]{1,0:T(8,128)(2,1)S(1)}, u32[]{:S(2)}, u32[]{:S(2)}) collective-permute-start(bf16[128,384]{1,0:T(8,128)(2,1)S(1)} %fusion.9), channel_id=1, source_target_pairs={{0,1},{1,0},{2,3},{3,2},{4,5},{5,4},{6,7},{7,6},{8,9},{9,8},{10,11... | collective-permute-start | bytes 294920 | tf_op jit(solution)/shard_map/ppermute | solution.py:10
  33.8 6.1 %collective-permute-done.4 = f32[128,384]{1,0:T(8,128)S(1)} collective-permute-done((f32[128,384]{1,0:T(8,128)S(1)}, f32[128,384]{1,0:T(8,128)S(1)}, u32[]{:S(2)}, u32[]{:S(2)}) %collective-permute-start.4) | collective-permute-done | bytes 196640 | tf_op jit(solution)/shard_map/ppermute | solution.py:10
  41.9 6.7 %collective-permute-done.5 = bf16[128,384]{1,0:T(8,128)(2,1)S(1)} collective-permute-done((bf16[128,384]{1,0:T(8,128)(2,1)S(1)}, bf16[128,384]{1,0:T(8,128)(2,1)S(1)}, u32[]{:S(2)}, u32[]{:S(2)}) %collective-permute-start.5) | collective-permute-done | bytes 98336 | tf_op jit(solution)/shard_map/ppermute | solution.py:10
  57.2 6.1 %collective-permute-done.7 = f32[128,384]{1,0:T(8,128)S(1)} collective-permute-done((f32[128,384]{1,0:T(8,128)S(1)}, f32[128,384]{1,0:T(8,128)S(1)}, u32[]{:S(2)}, u32[]{:S(2)}) %collective-permute-start.7) | collective-permute-done | bytes 196640 | tf_op jit(solution)/shard_map/ppermute | solution.py:10
  65.3 11.9 %collective-permute-done.8 = f32[128,384]{1,0:T(8,128)S(1)} collective-permute-done((f32[128,384]{1,0:T(8,128)S(1)}, f32[128,384]{1,0:T(8,128)S(1)}, u32[]{:S(2)}, u32[]{:S(2)}) %collective-permute-start.8) | collective-permute-done | bytes 196640 | tf_op jit(solution)/shard_map/ppermute | solution.py:10
  82.0 7.6 %collective-permute-done.9 = bf16[128,384]{1,0:T(8,128)(2,1)S(1)} collective-permute-done((bf16[128,384]{1,0:T(8,128)(2,1)S(1)}, bf16[128,384]{1,0:T(8,128)(2,1)S(1)}, u32[]{:S(2)}, u32[]{:S(2)}) %collective-permute-start.9) | collective-permute-done | bytes 98336 | tf_op jit(solution)/shard_map/ppermute | solution.py:10
  97.6 6.1 %collective-permute-done.11 = f32[128,384]{1,0:T(8,128)S(1)} collective-permute-done((f32[128,384]{1,0:T(8,128)S(1)}, f32[128,384]{1,0:T(8,128)S(1)}, u32[]{:S(2)}, u32[]{:S(2)}) %collective-permute-start.11) | collective-permute-done | bytes 196640 | tf_op jit(solution)/shard_map/ppermute | solution.py:10
  105.6 11.9 %collective-permute-done.12 = f32[128,384]{1,0:T(8,128)S(1)} collective-permute-done((f32[128,384]{1,0:T(8,128)S(1)}, f32[128,384]{1,0:T(8,128)S(1)}, u32[]{:S(2)}, u32[]{:S(2)}) %collective-permute-start.12) | collective-permute-done | bytes 196640 | tf_op jit(solution)/shard_map/ppermute | solution.py:10
  121.8 11.8 %collective-permute-done.13 = f32[128,384]{1,0:T(8,128)S(1)} collective-permute-done((f32[128,384]{1,0:T(8,128)S(1)}, f32[128,384]{1,0:T(8,128)S(1)}, u32[]{:S(2)}, u32[]{:S(2)}) %collective-permute-start.13) | collective-permute-done | bytes 196640 | tf_op jit(solution)/shard_map/ppermute | solution.py:10
  148.2 6.1 %collective-permute-done.16 = f32[128,384]{1,0:T(8,128)S(1)} collective-permute-done((f32[128,384]{1,0:T(8,128)S(1)}, f32[128,384]{1,0:T(8,128)S(1)}, u32[]{:S(2)}, u32[]{:S(2)}) %collective-permute-start.16) | collective-permute-done | bytes 196640 | tf_op jit(solution)/shard_map/ppermute | solution.py:10
  156.3 11.9 %collective-permute-done.17 = f32[128,384]{1,0:T(8,128)S(1)} collective-permute-done((f32[128,384]{1,0:T(8,128)S(1)}, f32[128,384]{1,0:T(8,128)S(1)}, u32[]{:S(2)}, u32[]{:S(2)}) %collective-permute-start.17) | collective-permute-done | bytes 196640 | tf_op jit(solution)/shard_map/ppermute | solution.py:10
  173.0 11.8 %collective-permute-done.18 = f32[128,384]{1,0:T(8,128)S(1)} collective-permute-done((f32[128,384]{1,0:T(8,128)S(1)}, f32[128,384]{1,0:T(8,128)S(1)}, u32[]{:S(2)}, u32[]{:S(2)}) %collective-permute-start.18) | collective-permute-done | bytes 196640 | tf_op jit(solution)/shard_map/ppermute | solution.py:10
  194.7 6.6 %collective-permute-done.20 = bf16[128,384]{1,0:T(8,128)(2,1)S(1)} collective-permute-done((bf16[128,384]{1,0:T(8,128)(2,1)S(1)}, bf16[128,384]{1,0:T(8,128)(2,1)S(1)}, u32[]{:S(2)}, u32[]{:S(2)}) %collective-permute-start.20) | collective-permute-done | bytes 98336 | tf_op jit(solution)/shard_map/ppermute | solution.py:10
  210.1 6.1 %collective-permute-done.22 = f32[128,384]{1,0:T(8,128)S(1)} collective-permute-done((f32[128,384]{1,0:T(8,128)S(1)}, f32[128,384]{1,0:T(8,128)S(1)}, u32[]{:S(2)}, u32[]{:S(2)}) %collective-permute-start.22) | collective-permute-done | bytes 196640 | tf_op jit(solution)/shard_map/ppermute | solution.py:10
  218.1 11.9 %collective-permute-done.23 = f32[128,384]{1,0:T(8,128)S(1)} collective-permute-done((f32[128,384]{1,0:T(8,128)S(1)}, f32[128,384]{1,0:T(8,128)S(1)}, u32[]{:S(2)}, u32[]{:S(2)}) %collective-permute-start.23) | collective-permute-done | bytes 196640 | tf_op jit(solution)/shard_map/ppermute | solution.py:10
  234.3 11.8 %collective-permute-done.24 = f32[128,384]{1,0:T(8,128)S(1)} collective-permute-done((f32[128,384]{1,0:T(8,128)S(1)}, f32[128,384]{1,0:T(8,128)S(1)}, u32[]{:S(2)}, u32[]{:S(2)}) %collective-permute-start.24) | collective-permute-done | bytes 196640 | tf_op jit(solution)/shard_map/ppermute | solution.py:10
  248.1 5.9 %collective-permute-done.25 = f32[128,384]{1,0:T(8,128)S(1)} collective-permute-done((f32[128,384]{1,0:T(8,128)S(1)}, f32[128,384]{1,0:T(8,128)S(1)}, u32[]{:S(2)}, u32[]{:S(2)}) %collective-permute-start.25) | collective-permute-done | bytes 196640 | tf_op jit(solution)/shard_map/ppermute | solution.py:10
  256.0 11.9 %collective-permute-done.26 = f32[128,384]{1,0:T(8,128)S(1)} collective-permute-done((f32[128,384]{1,0:T(8,128)S(1)}, f32[128,384]{1,0:T(8,128)S(1)}, u32[]{:S(2)}, u32[]{:S(2)}) %collective-permute-start.26) | collective-permute-done | bytes 196640 | tf_op jit(solution)/shard_map/ppermute | solution.py:10
  272.0 7.6 %collective-permute-done.27 = bf16[128,384]{1,0:T(8,128)(2,1)S(1)} collective-permute-done((bf16[128,384]{1,0:T(8,128)(2,1)S(1)}, bf16[128,384]{1,0:T(8,128)(2,1)S(1)}, u32[]{:S(2)}, u32[]{:S(2)}) %collective-permute-start.27) | collective-permute-done | bytes 98336 | tf_op jit(solution)/shard_map/ppermute | solution.py:10
  287.5 6.1 %collective-permute-done.29 = f32[128,384]{1,0:T(8,128)S(1)} collective-permute-done((f32[128,384]{1,0:T(8,128)S(1)}, f32[128,384]{1,0:T(8,128)S(1)}, u32[]{:S(2)}, u32[]{:S(2)}) %collective-permute-start.29) | collective-permute-done | bytes 196640 | tf_op jit(solution)/shard_map/ppermute | solution.py:10
  295.6 11.9 %collective-permute-done.30 = f32[128,384]{1,0:T(8,128)S(1)} collective-permute-done((f32[128,384]{1,0:T(8,128)S(1)}, f32[128,384]{1,0:T(8,128)S(1)}, u32[]{:S(2)}, u32[]{:S(2)}) %collective-permute-start.30) | collective-permute-done | bytes 196640 | tf_op jit(solution)/shard_map/ppermute | solution.py:10
  312.4 11.8 %collective-permute-done.31 = f32[128,384]{1,0:T(8,128)S(1)} collective-permute-done((f32[128,384]{1,0:T(8,128)S(1)}, f32[128,384]{1,0:T(8,128)S(1)}, u32[]{:S(2)}, u32[]{:S(2)}) %collective-permute-start.31) | collective-permute-done | bytes 196640 | tf_op jit(solution)/shard_map/ppermute | solution.py:10
  326.2 5.9 %collective-permute-done.32 = f32[128,384]{1,0:T(8,128)S(1)} collective-permute-done((f32[128,384]{1,0:T(8,128)S(1)}, f32[128,384]{1,0:T(8,128)S(1)}, u32[]{:S(2)}, u32[]{:S(2)}) %collective-permute-start.32) | collective-permute-done | bytes 196640 | tf_op jit(solution)/shard_map/ppermute | solution.py:10
  334.1 11.9 %collective-permute-done.33 = f32[128,384]{1,0:T(8,128)S(1)} collective-permute-done((f32[128,384]{1,0:T(8,128)S(1)}, f32[128,384]{1,0:T(8,128)S(1)}, u32[]{:S(2)}, u32[]{:S(2)}) %collective-permute-start.33) | collective-permute-done | bytes 196640 | tf_op jit(solution)/shard_map/ppermute | solution.py:10
  351.0 11.8 %collective-permute-done.34 = f32[128,384]{1,0:T(8,128)S(1)} collective-permute-done((f32[128,384]{1,0:T(8,128)S(1)}, f32[128,384]{1,0:T(8,128)S(1)}, u32[]{:S(2)}, u32[]{:S(2)}) %collective-permute-start.34) | collective-permute-done | bytes 196640 | tf_op jit(solution)/shard_map/ppermute | solution.py:10
  377.4 6.1 %collective-permute-done.37 = f32[128,384]{1,0:T(8,128)S(1)} collective-permute-done((f32[128,384]{1,0:T(8,128)S(1)}, f32[128,384]{1,0:T(8,128)S(1)}, u32[]{:S(2)}, u32[]{:S(2)}) %collective-permute-start.37) | collective-permute-done | bytes 196640 | tf_op jit(solution)/shard_map/ppermute | solution.py:10
  385.4 11.9 %collective-permute-done.38 = f32[128,384]{1,0:T(8,128)S(1)} collective-permute-done((f32[128,384]{1,0:T(8,128)S(1)}, f32[128,384]{1,0:T(8,128)S(1)}, u32[]{:S(2)}, u32[]{:S(2)}) %collective-permute-start.38) | collective-permute-done | bytes 196640 | tf_op jit(solution)/shard_map/ppermute | solution.py:10
  401.5 11.8 %collective-permute-done.39 = f32[128,384]{1,0:T(8,128)S(1)} collective-permute-done((f32[128,384]{1,0:T(8,128)S(1)}, f32[128,384]{1,0:T(8,128)S(1)}, u32[]{:S(2)}, u32[]{:S(2)}) %collective-permute-start.39) | collective-permute-done | bytes 196640 | tf_op jit(solution)/shard_map/ppermute | solution.py:10
  415.3 5.9 %collective-permute-done.40 = f32[128,384]{1,0:T(8,128)S(1)} collective-permute-done((f32[128,384]{1,0:T(8,128)S(1)}, f32[128,384]{1,0:T(8,128)S(1)}, u32[]{:S(2)}, u32[]{:S(2)}) %collective-permute-start.40) | collective-permute-done | bytes 196640 | tf_op jit(solution)/shard_map/ppermute | solution.py:10
  423.2 11.9 %collective-permute-done.41 = f32[128,384]{1,0:T(8,128)S(1)} collective-permute-done((f32[128,384]{1,0:T(8,128)S(1)}, f32[128,384]{1,0:T(8,128)S(1)}, u32[]{:S(2)}, u32[]{:S(2)}) %collective-permute-start.41) | collective-permute-done | bytes 196640 | tf_op jit(solution)/shard_map/ppermute | solution.py:10
  439.3 11.8 %collective-permute-done.42 = f32[128,384]{1,0:T(8,128)S(1)} collective-permute-done((f32[128,384]{1,0:T(8,128)S(1)}, f32[128,384]{1,0:T(8,128)S(1)}, u32[]{:S(2)}, u32[]{:S(2)}) %collective-permute-start.42) | collective-permute-done | bytes 196640 | tf_op jit(solution)/shard_map/ppermute | solution.py:10
  453.0 5.9 %collective-permute-done.43 = f32[128,384]{1,0:T(8,128)S(1)} collective-permute-done((f32[128,384]{1,0:T(8,128)S(1)}, f32[128,384]{1,0:T(8,128)S(1)}, u32[]{:S(2)}, u32[]{:S(2)}) %collective-permute-start.43) | collective-permute-done | bytes 196640 | tf_op jit(solution)/shard_map/ppermute | solution.py:10
  (117 shorter events, 174.4 us)
Async XLA Ops:
  3.7 9.7 %collective-permute-start = (bf16[128,384]{1,0:T(8,128)(2,1)S(1)}, bf16[128,384]{1,0:T(8,128)(2,1)S(1)}, u32[]{:S(2)}, u32[]{:S(2)}) collective-permute-start(bf16[128,384]{1,0:T(8,128)(2,1)S(1)} %fusion.9), channel_id=1, source_target_pairs={{0,1},{1,0},{2,3},{3,2},{4,5},{5,4},{6,7},{7,6},{8,9},{9,8},{10,11... | collective-permute-start | bytes 294920 | tf_op jit(solution)/shard_map/ppermute | solution.py:10
  31.9 8.0 %collective-permute-start.4 = (f32[128,384]{1,0:T(8,128)S(1)}, f32[128,384]{1,0:T(8,128)S(1)}, u32[]{:S(2)}, u32[]{:S(2)}) collective-permute-start(f32[128,384]{1,0:T(8,128)S(1)} %add.109), channel_id=1, source_target_pairs={{0,2},{1,3},{2,0},{3,1},{4,6},{5,7},{6,4},{7,5},{8,10},{9,11},{10,... | collective-permute-start | bytes 589832 | tf_op jit(solution)/shard_map/ppermute | solution.py:10
  39.9 8.7 %collective-permute-start.5 = (bf16[128,384]{1,0:T(8,128)(2,1)S(1)}, bf16[128,384]{1,0:T(8,128)(2,1)S(1)}, u32[]{:S(2)}, u32[]{:S(2)}) collective-permute-start(bf16[128,384]{1,0:T(8,128)(2,1)S(1)} %add_convert_fusion.6), channel_id=1, source_target_pairs={{0,4},{1,5},{2,6},{3,7},{4,0},{5,1},{6,2},{7,3},{8,12},{9,13},{10,... | collective-permute-start | bytes 294920 | tf_op jit(solution)/shard_map/ppermute | solution.py:10
  55.3 8.0 %collective-permute-start.7 = (f32[128,384]{1,0:T(8,128)S(1)}, f32[128,384]{1,0:T(8,128)S(1)}, u32[]{:S(2)}, u32[]{:S(2)}) collective-permute-start(f32[128,384]{1,0:T(8,128)S(1)} %add.111), channel_id=1, source_target_pairs={{0,2},{1,3},{2,0},{3,1},{4,6},{5,7},{6,4},{7,5},{8,10},{9,11},{10,... | collective-permute-start | bytes 589832 | tf_op jit(solution)/shard_map/ppermute | solution.py:10
  63.3 13.8 %collective-permute-start.8 = (f32[128,384]{1,0:T(8,128)S(1)}, f32[128,384]{1,0:T(8,128)S(1)}, u32[]{:S(2)}, u32[]{:S(2)}) collective-permute-start(f32[128,384]{1,0:T(8,128)S(1)} %add.112), channel_id=1, source_target_pairs={{0,4},{1,5},{2,6},{3,7},{4,0},{5,1},{6,2},{7,3},{8,12},{9,13},{10,... | collective-permute-start | bytes 589832 | tf_op jit(solution)/shard_map/ppermute | solution.py:10
  77.1 12.5 %collective-permute-start.9 = (bf16[128,384]{1,0:T(8,128)(2,1)S(1)}, bf16[128,384]{1,0:T(8,128)(2,1)S(1)}, u32[]{:S(2)}, u32[]{:S(2)}) collective-permute-start(bf16[128,384]{1,0:T(8,128)(2,1)S(1)} %add_convert_fusion.5), channel_id=1, source_target_pairs={{0,8},{1,9},{2,10},{3,11},{4,12},{5,13},{6,14},{7,15},{8,0},{9,1},... | collective-permute-start | bytes 294920 | tf_op jit(solution)/shard_map/ppermute | solution.py:10
  95.7 8.0 %collective-permute-start.11 = (f32[128,384]{1,0:T(8,128)S(1)}, f32[128,384]{1,0:T(8,128)S(1)}, u32[]{:S(2)}, u32[]{:S(2)}) collective-permute-start(f32[128,384]{1,0:T(8,128)S(1)} %add.114), channel_id=1, source_target_pairs={{0,2},{1,3},{2,0},{3,1},{4,6},{5,7},{6,4},{7,5},{8,10},{9,11},{10,... | collective-permute-start | bytes 589832 | tf_op jit(solution)/shard_map/ppermute | solution.py:10
  103.7 13.8 %collective-permute-start.12 = (f32[128,384]{1,0:T(8,128)S(1)}, f32[128,384]{1,0:T(8,128)S(1)}, u32[]{:S(2)}, u32[]{:S(2)}) collective-permute-start(f32[128,384]{1,0:T(8,128)S(1)} %add.115), channel_id=1, source_target_pairs={{0,4},{1,5},{2,6},{3,7},{4,0},{5,1},{6,2},{7,3},{8,12},{9,13},{10,... | collective-permute-start | bytes 589832 | tf_op jit(solution)/shard_map/ppermute | solution.py:10
  117.5 16.2 %collective-permute-start.13 = (f32[128,384]{1,0:T(8,128)S(1)}, f32[128,384]{1,0:T(8,128)S(1)}, u32[]{:S(2)}, u32[]{:S(2)}) collective-permute-start(f32[128,384]{1,0:T(8,128)S(1)} %add.116), channel_id=1, source_target_pairs={{0,8},{1,9},{2,10},{3,11},{4,12},{5,13},{6,14},{7,15},{8,0},{9,1},... | collective-permute-start | bytes 589832 | tf_op jit(solution)/shard_map/ppermute | solution.py:10
  146.3 8.0 %collective-permute-start.16 = (f32[128,384]{1,0:T(8,128)S(1)}, f32[128,384]{1,0:T(8,128)S(1)}, u32[]{:S(2)}, u32[]{:S(2)}) collective-permute-start(f32[128,384]{1,0:T(8,128)S(1)} %add.118), channel_id=1, source_target_pairs={{0,2},{1,3},{2,0},{3,1},{4,6},{5,7},{6,4},{7,5},{8,10},{9,11},{10,... | collective-permute-start | bytes 589832 | tf_op jit(solution)/shard_map/ppermute | solution.py:10
  154.3 13.8 %collective-permute-start.17 = (f32[128,384]{1,0:T(8,128)S(1)}, f32[128,384]{1,0:T(8,128)S(1)}, u32[]{:S(2)}, u32[]{:S(2)}) collective-permute-start(f32[128,384]{1,0:T(8,128)S(1)} %add.119), channel_id=1, source_target_pairs={{0,4},{1,5},{2,6},{3,7},{4,0},{5,1},{6,2},{7,3},{8,12},{9,13},{10,... | collective-permute-start | bytes 589832 | tf_op jit(solution)/shard_map/ppermute | solution.py:10
  168.1 16.7 %collective-permute-start.18 = (f32[128,384]{1,0:T(8,128)S(1)}, f32[128,384]{1,0:T(8,128)S(1)}, u32[]{:S(2)}, u32[]{:S(2)}) collective-permute-start(f32[128,384]{1,0:T(8,128)S(1)} %add.120), channel_id=1, source_target_pairs={{0,8},{1,9},{2,10},{3,11},{4,12},{5,13},{6,14},{7,15},{8,0},{9,1},... | collective-permute-start | bytes 589832 | tf_op jit(solution)/shard_map/ppermute | solution.py:10
  184.9 7.9 %collective-permute-start.19 = (f32[128,384]{1,0:T(8,128)S(1)}, f32[128,384]{1,0:T(8,128)S(1)}, u32[]{:S(2)}, u32[]{:S(2)}) collective-permute-start(f32[128,384]{1,0:T(8,128)S(1)} %add.121), channel_id=1, source_target_pairs={{0,16},{1,17},{2,18},{3,19},{4,20},{5,21},{6,22},{7,23},{8,24},{9,... | collective-permute-start | bytes 589832 | tf_op jit(solution)/shard_map/ppermute | solution.py:10
  192.8 8.5 %collective-permute-start.20 = (bf16[128,384]{1,0:T(8,128)(2,1)S(1)}, bf16[128,384]{1,0:T(8,128)(2,1)S(1)}, u32[]{:S(2)}, u32[]{:S(2)}) collective-permute-start(bf16[128,384]{1,0:T(8,128)(2,1)S(1)} %add_convert_fusion.3), channel_id=1, source_target_pairs={{0,32},{1,33},{2,34},{3,35},{4,36},{5,37},{6,38},{7,39},{8,40},{9,... | collective-permute-start | bytes 294920 | tf_op jit(solution)/shard_map/ppermute | solution.py:10
  208.1 8.0 %collective-permute-start.22 = (f32[128,384]{1,0:T(8,128)S(1)}, f32[128,384]{1,0:T(8,128)S(1)}, u32[]{:S(2)}, u32[]{:S(2)}) collective-permute-start(f32[128,384]{1,0:T(8,128)S(1)} %add.123), channel_id=1, source_target_pairs={{0,2},{1,3},{2,0},{3,1},{4,6},{5,7},{6,4},{7,5},{8,10},{9,11},{10,... | collective-permute-start | bytes 589832 | tf_op jit(solution)/shard_map/ppermute | solution.py:10
  216.2 13.8 %collective-permute-start.23 = (f32[128,384]{1,0:T(8,128)S(1)}, f32[128,384]{1,0:T(8,128)S(1)}, u32[]{:S(2)}, u32[]{:S(2)}) collective-permute-start(f32[128,384]{1,0:T(8,128)S(1)} %add.124), channel_id=1, source_target_pairs={{0,4},{1,5},{2,6},{3,7},{4,0},{5,1},{6,2},{7,3},{8,12},{9,13},{10,... | collective-permute-start | bytes 589832 | tf_op jit(solution)/shard_map/ppermute | solution.py:10
  230.0 16.2 %collective-permute-start.24 = (f32[128,384]{1,0:T(8,128)S(1)}, f32[128,384]{1,0:T(8,128)S(1)}, u32[]{:S(2)}, u32[]{:S(2)}) collective-permute-start(f32[128,384]{1,0:T(8,128)S(1)} %add.125), channel_id=1, source_target_pairs={{0,8},{1,9},{2,10},{3,11},{4,12},{5,13},{6,14},{7,15},{8,0},{9,1},... | collective-permute-start | bytes 589832 | tf_op jit(solution)/shard_map/ppermute | solution.py:10
  246.2 7.9 %collective-permute-start.25 = (f32[128,384]{1,0:T(8,128)S(1)}, f32[128,384]{1,0:T(8,128)S(1)}, u32[]{:S(2)}, u32[]{:S(2)}) collective-permute-start(f32[128,384]{1,0:T(8,128)S(1)} %add.126), channel_id=1, source_target_pairs={{0,16},{1,17},{2,18},{3,19},{4,20},{5,21},{6,22},{7,23},{8,24},{9,... | collective-permute-start | bytes 589832 | tf_op jit(solution)/shard_map/ppermute | solution.py:10
  254.1 13.8 %collective-permute-start.26 = (f32[128,384]{1,0:T(8,128)S(1)}, f32[128,384]{1,0:T(8,128)S(1)}, u32[]{:S(2)}, u32[]{:S(2)}) collective-permute-start(f32[128,384]{1,0:T(8,128)S(1)} %add.127), channel_id=1, source_target_pairs={{0,32},{1,33},{2,34},{3,35},{4,36},{5,37},{6,38},{7,39},{8,40},{9,... | collective-permute-start | bytes 589832 | tf_op jit(solution)/shard_map/ppermute | solution.py:10
  267.9 11.7 %collective-permute-start.27 = (bf16[128,384]{1,0:T(8,128)(2,1)S(1)}, bf16[128,384]{1,0:T(8,128)(2,1)S(1)}, u32[]{:S(2)}, u32[]{:S(2)}) collective-permute-start(bf16[128,384]{1,0:T(8,128)(2,1)S(1)} %add_convert_fusion.2), channel_id=1, source_target_pairs={{0,64},{1,65},{2,66},{3,67},{4,68},{5,69},{6,70},{7,71},{8,72},{9,... | collective-permute-start | bytes 294920 | tf_op jit(solution)/shard_map/ppermute | solution.py:10
  285.6 8.0 %collective-permute-start.29 = (f32[128,384]{1,0:T(8,128)S(1)}, f32[128,384]{1,0:T(8,128)S(1)}, u32[]{:S(2)}, u32[]{:S(2)}) collective-permute-start(f32[128,384]{1,0:T(8,128)S(1)} %add.129), channel_id=1, source_target_pairs={{0,2},{1,3},{2,0},{3,1},{4,6},{5,7},{6,4},{7,5},{8,10},{9,11},{10,... | collective-permute-start | bytes 589832 | tf_op jit(solution)/shard_map/ppermute | solution.py:10
  293.6 13.8 %collective-permute-start.30 = (f32[128,384]{1,0:T(8,128)S(1)}, f32[128,384]{1,0:T(8,128)S(1)}, u32[]{:S(2)}, u32[]{:S(2)}) collective-permute-start(f32[128,384]{1,0:T(8,128)S(1)} %add.130), channel_id=1, source_target_pairs={{0,4},{1,5},{2,6},{3,7},{4,0},{5,1},{6,2},{7,3},{8,12},{9,13},{10,... | collective-permute-start | bytes 589832 | tf_op jit(solution)/shard_map/ppermute | solution.py:10
  307.4 16.8 %collective-permute-start.31 = (f32[128,384]{1,0:T(8,128)S(1)}, f32[128,384]{1,0:T(8,128)S(1)}, u32[]{:S(2)}, u32[]{:S(2)}) collective-permute-start(f32[128,384]{1,0:T(8,128)S(1)} %add.131), channel_id=1, source_target_pairs={{0,8},{1,9},{2,10},{3,11},{4,12},{5,13},{6,14},{7,15},{8,0},{9,1},... | collective-permute-start | bytes 589832 | tf_op jit(solution)/shard_map/ppermute | solution.py:10
  324.3 7.9 %collective-permute-start.32 = (f32[128,384]{1,0:T(8,128)S(1)}, f32[128,384]{1,0:T(8,128)S(1)}, u32[]{:S(2)}, u32[]{:S(2)}) collective-permute-start(f32[128,384]{1,0:T(8,128)S(1)} %add.132), channel_id=1, source_target_pairs={{0,16},{1,17},{2,18},{3,19},{4,20},{5,21},{6,22},{7,23},{8,24},{9,... | collective-permute-start | bytes 589832 | tf_op jit(solution)/shard_map/ppermute | solution.py:10
  332.2 13.8 %collective-permute-start.33 = (f32[128,384]{1,0:T(8,128)S(1)}, f32[128,384]{1,0:T(8,128)S(1)}, u32[]{:S(2)}, u32[]{:S(2)}) collective-permute-start(f32[128,384]{1,0:T(8,128)S(1)} %add.133), channel_id=1, source_target_pairs={{0,32},{1,33},{2,34},{3,35},{4,36},{5,37},{6,38},{7,39},{8,40},{9,... | collective-permute-start | bytes 589832 | tf_op jit(solution)/shard_map/ppermute | solution.py:10
  346.0 16.8 %collective-permute-start.34 = (f32[128,384]{1,0:T(8,128)S(1)}, f32[128,384]{1,0:T(8,128)S(1)}, u32[]{:S(2)}, u32[]{:S(2)}) collective-permute-start(f32[128,384]{1,0:T(8,128)S(1)} %add.134), channel_id=1, source_target_pairs={{0,64},{1,65},{2,66},{3,67},{4,68},{5,69},{6,70},{7,71},{8,72},{9,... | collective-permute-start | bytes 589832 | tf_op jit(solution)/shard_map/ppermute | solution.py:10
  375.4 8.0 %collective-permute-start.37 = (f32[128,384]{1,0:T(8,128)S(1)}, f32[128,384]{1,0:T(8,128)S(1)}, u32[]{:S(2)}, u32[]{:S(2)}) collective-permute-start(f32[128,384]{1,0:T(8,128)S(1)} %add.136), channel_id=1, source_target_pairs={{0,2},{1,3},{2,0},{3,1},{4,6},{5,7},{6,4},{7,5},{8,10},{9,11},{10,... | collective-permute-start | bytes 589832 | tf_op jit(solution)/shard_map/ppermute | solution.py:10
  383.5 13.8 %collective-permute-start.38 = (f32[128,384]{1,0:T(8,128)S(1)}, f32[128,384]{1,0:T(8,128)S(1)}, u32[]{:S(2)}, u32[]{:S(2)}) collective-permute-start(f32[128,384]{1,0:T(8,128)S(1)} %add.137), channel_id=1, source_target_pairs={{0,4},{1,5},{2,6},{3,7},{4,0},{5,1},{6,2},{7,3},{8,12},{9,13},{10,... | collective-permute-start | bytes 589832 | tf_op jit(solution)/shard_map/ppermute | solution.py:10
  397.3 16.1 %collective-permute-start.39 = (f32[128,384]{1,0:T(8,128)S(1)}, f32[128,384]{1,0:T(8,128)S(1)}, u32[]{:S(2)}, u32[]{:S(2)}) collective-permute-start(f32[128,384]{1,0:T(8,128)S(1)} %add.138), channel_id=1, source_target_pairs={{0,8},{1,9},{2,10},{3,11},{4,12},{5,13},{6,14},{7,15},{8,0},{9,1},... | collective-permute-start | bytes 589832 | tf_op jit(solution)/shard_map/ppermute | solution.py:10
  413.4 7.9 %collective-permute-start.40 = (f32[128,384]{1,0:T(8,128)S(1)}, f32[128,384]{1,0:T(8,128)S(1)}, u32[]{:S(2)}, u32[]{:S(2)}) collective-permute-start(f32[128,384]{1,0:T(8,128)S(1)} %add.139), channel_id=1, source_target_pairs={{0,16},{1,17},{2,18},{3,19},{4,20},{5,21},{6,22},{7,23},{8,24},{9,... | collective-permute-start | bytes 589832 | tf_op jit(solution)/shard_map/ppermute | solution.py:10
  421.3 13.8 %collective-permute-start.41 = (f32[128,384]{1,0:T(8,128)S(1)}, f32[128,384]{1,0:T(8,128)S(1)}, u32[]{:S(2)}, u32[]{:S(2)}) collective-permute-start(f32[128,384]{1,0:T(8,128)S(1)} %add.140), channel_id=1, source_target_pairs={{0,32},{1,33},{2,34},{3,35},{4,36},{5,37},{6,38},{7,39},{8,40},{9,... | collective-permute-start | bytes 589832 | tf_op jit(solution)/shard_map/ppermute | solution.py:10
  435.1 16.0 %collective-permute-start.42 = (f32[128,384]{1,0:T(8,128)S(1)}, f32[128,384]{1,0:T(8,128)S(1)}, u32[]{:S(2)}, u32[]{:S(2)}) collective-permute-start(f32[128,384]{1,0:T(8,128)S(1)} %add.141), channel_id=1, source_target_pairs={{0,64},{1,65},{2,66},{3,67},{4,68},{5,69},{6,70},{7,71},{8,72},{9,... | collective-permute-start | bytes 589832 | tf_op jit(solution)/shard_map/ppermute | solution.py:10
  (15 other events, 78.0 us)
where the time goes:
time: 470 us; the launch traced here: 468 us
  waiting for transfers between devices  316 us (67%)
  starting transfers between devices  124 us (26%)
  matrix products  25 us (5%)
    ppermute x45, waiting for transfers between devices, partner(): return lax.ppermute(value, axis, pairs)  316 us
    ppermute x45, starting transfers between devices, partner(): return lax.ppermute(value, axis, pairs)  124 us
    dot_general x9, matrix products, on_device(): jnp.dot(spread_rows[tree_level], coefficients, preferred_element_type=jnp...  13 us
    dot_general x9, matrix products, on_device(): jnp.einsum('sr,sk->rk', project_rows[tree_level], rounded, preferred_elem...  10.6 us
  transfers between devices with their start and end apart: 45, of which 45 were waited for; matrix products, arithmetic and copies ran while one was open for 0% of the time, Pallas kernels for 0%

commit v1 on v0

v1 whole, which is shorter than its diff:
```python
import jax
import jax.numpy as jnp
from jax import lax
from jax.experimental import pallas as pl
from jax.experimental.pallas import tpu as pltpu
from jax.sharding import PartitionSpec as P

BF = jnp.bfloat16
F32 = jnp.float32
AXIS = "seq"
MASKS = {3: 12, 6: 96, 8: 384}


def mask_of(level):
    return MASKS.get(level, 1 << level)


def swap(value, mask, core):
    pairs = [(d, d ^ mask) for d in range(lax.axis_size(AXIS)) if d & 1 == core]
    return lax.ppermute(value, AXIS, pairs)


def to_core(value, core):
    pairs = [(d ^ 1, d) for d in range(lax.axis_size(AXIS)) if d & 1 == core]
    return lax.ppermute(value, AXIS, pairs)


def dot(a, b, dims):
    return lax.dot_general(a, b, (dims, ((), ())), preferred_element_type=F32)


NN = ((1,), (0,))
NT = ((1,), (1,))
TN = ((0,), (0,))


def call(body, out_shape, args, in_specs=None, flops=0):
    if in_specs is None:
        in_specs = [None] * len(args)
    specs = [s if s is not None else pl.BlockSpec(memory_space=pltpu.VMEM) for s in in_specs]
    single = not isinstance(out_shape, (list, tuple))
    outs = pl.BlockSpec(memory_space=pltpu.VMEM)
    size = sum(a.size * a.dtype.itemsize for a in args)
    return pl.pallas_call(
        body,
        out_shape=out_shape,
        grid=(1,),
        in_specs=specs,
        out_specs=outs if single else [outs] * len(out_shape),
        compiler_params=pltpu.CompilerParams(vmem_limit_bytes=32 * 2**20),
        cost_estimate=pl.CostEstimate(flops=flops, bytes_accessed=size, transcendentals=0),
    )(*args)


SCALAR = pl.BlockSpec(memory_space=pltpu.SMEM)


def sds(shape, dtype):
    return jax.ShapeDtypeStruct(shape, dtype)


def static_body(project_ref, spread_ref, out_ref):
    levels = project_ref.shape[0]
    at = 0
    for low in range(1, levels - 1):
        spread = spread_ref[low]
        for high in range(low + 1, levels):
            block = dot(spread, project_ref[high], TN)
            out_ref[:, at : at + block.shape[1]] = block.astype(BF)
            at += block.shape[1]


def leaf_body(inverse_ref, right_ref, project_ref, state_ref, sums_ref):
    state = dot(inverse_ref[0], right_ref[...], NN)
    state_ref[...] = state
    sums_ref[...] = dot(project_ref[0], state.astype(BF), TN).astype(BF)


def first_body(state_ref, stacked_ref, capacity_ref, spread_ref, project_ref, next_ref, sums_ref):
    coefficients = dot(capacity_ref[0], stacked_ref[...], NN).astype(BF)
    state = state_ref[...] - dot(spread_ref[0], coefficients, NN)
    next_ref[...] = state
    rounded = state.astype(BF)
    for level in range(1, project_ref.shape[0]):
        block = dot(rounded, project_ref[level], TN)
        rank = block.shape[1]
        sums_ref[:, (level - 1) * rank : level * rank] = block.astype(BF)


def step_body(half_ref, own_ref, other_ref, static_ref, *out_refs):
    rank = static_ref.shape[0] // 2
    width = own_ref.shape[1] - rank
    lower = half_ref[0] == 0
    own, other = own_ref[:, :rank], other_ref[:, :rank]
    stacked = jnp.concatenate([jnp.where(lower, own, other), jnp.where(lower, other, own)], 1)
    capacity = static_ref[:, width : width + 2 * rank]
    coefficients = dot(stacked, capacity, NT).astype(BF)
    out_refs[0][...] = coefficients[:, : out_refs[0].shape[1]]
    if width:
        both = own_ref[:, rank:].astype(F32) + other_ref[:, rank:].astype(F32)
        out_refs[1][...] = (both - dot(coefficients, static_ref[:, :width], NN)).astype(BF)


def last_body(where_ref, state_ref, spread_ref, own_ref, got_ref, out_ref):
    is_first = where_ref[0] == 0
    total = state_ref[...]
    for level in range(1, spread_ref.shape[0]):
        rows = jnp.where(is_first, own_ref[level - 1], got_ref[level - 1])
        total = total - dot(spread_ref[level], rows, NT)
    out_ref[...] = total


def on_device(right_side, leaf_inverse, project_rows, spread_rows, capacity):
    levels, samples, rank = project_rows.shape
    columns = right_side.shape[1]
    device = lax.axis_index(AXIS)

    def bit(level):
        return (device >> level & 1).astype(jnp.int32)

    def level_block(array, level):
        return pl.BlockSpec((1,) + array.shape[1:], lambda i: (level, 0, 0))

    pairs = (levels - 1) * (levels - 2) // 2
    static = call(static_body, sds((rank, pairs * rank), BF), [project_rows, spread_rows])
    static = static + to_core(static, 1)

    state, sums = call(
        leaf_body,
        [sds((samples, columns), F32), sds((rank, columns), BF)],
        [leaf_inverse, right_side, project_rows],
        [None, None, level_block(project_rows, 0)],
    )
    size = lax.axis_size(AXIS)
    stacked = lax.all_gather(
        sums, AXIS, axis_index_groups=[[d, d + 1] for d in range(0, size, 2)], tiled=True
    )
    state, sums = call(
        first_body,
        [sds((samples, columns), F32), sds((columns, (levels - 1) * rank), BF)],
        [state, stacked, capacity, spread_rows, project_rows],
        [None, None, level_block(capacity, 0), level_block(spread_rows, 0), None],
    )
    sums = sums + to_core(sums, 0)
    half = columns // 2
    side = bit(1)
    own = lax.dynamic_slice_in_dim(sums, side * half, half, 0)
    send = lax.dynamic_slice_in_dim(sums, (1 - side) * half, half, 0)

    gathered = []
    for level in range(1, levels):
        other = swap(send, mask_of(level), 0)

        width = (levels - 1 - level) * rank
        block = jnp.concatenate([static[:, :width], capacity[level]], 1)
        if level < levels - 1:
            message = jnp.concatenate([block, static[:, width:]], 1)
        else:
            message = block
        got = swap(message, mask_of(level), 1)
        cut = width + 2 * rank
        both = jnp.concatenate([block, got[:, :cut]], 0)
        static = static[:, width:] + got[:, cut:]
        both = to_core(both, 0)

        outs = [sds((half, 2 * rank if level == 1 else rank), BF)]
        if width:
            outs.append(sds((half, width), BF))
        results = call(
            step_body, outs, [bit(level)[None], own, other, both], [SCALAR, None, None, None]
        )
        gathered.append(results[0])
        if width:
            own = send = results[1]

    mine = jnp.stack([gathered[0][:, :rank]] + gathered[1:])
    theirs = swap(jnp.stack([gathered[0][:, rank:]] + gathered[1:]), 2, 0)
    both = jnp.where(
        side == 0, jnp.concatenate([mine, theirs], 1), jnp.concatenate([theirs, mine], 1)
    )
    got = to_core(both, 1)
    return call(
        last_body,
        sds((samples, columns), F32),
        [bit(0)[None], state, spread_rows, both, got],
        [SCALAR, None, None, None, None],
    )


def solution(mesh):
    return jax.shard_map(
        on_device,
        mesh=mesh,
        in_specs=(
            P(AXIS, None),
            P(AXIS, None, None),
            P(None, AXIS, None),
            P(None, AXIS, None),
            P(None, AXIS, None),
        ),
        out_specs=P(AXIS, None),
        check_vma=False,
    )
```

time: 470 us -> 149 us (0.32)
  waiting for transfers between devices: 316 us -> 71.8 us
  starting transfers between devices: 124 us -> 49.9 us
  matrix products: 25 us -> 0 us
  Pallas kernels: 0 us -> 8.05 us
  other arithmetic: 0.81 us -> 8.11 us
  local copies, waits for them, and re-layouts: 1.04 us -> 7.4 us
    ppermute x45 -> x28, waiting for transfers between devices: 316 us -> 71.8 us  [the longest x11 39.6 us: to_core(): return lax.ppermute(value, AXIS, pairs)]
    ppermute x45 -> x28, starting transfers between devices: 124 us -> 49.9 us  [the longest x17 32.4 us: swap(): return lax.ppermute(value, AXIS, pairs)]
    dot_general x19 -> x0, matrix products: 25 us -> none  [the longest x9 13 us: on_device(): jnp.dot(spread_rows[tree_level], coefficients, preferred_element_type=jnp...]
    pallas_call x0 -> x12, Pallas kernels: none -> 8.05 us  [call(): pl.pallas_call(body, out_shape=out_shape, grid=(1,), in_specs=specs, out_...]
  transfers between devices with their start and end apart: 45 -> 28, of which waited for: 45 -> 9; matrix products, arithmetic and copies ran while one was open for 0% -> 8% of each run, Pallas kernels for 0% -> 3%
where the time goes in v1:
time: 149 us; the launch traced here: 148 us
  waiting for transfers between devices  71.8 us (48%)
  starting transfers between devices  49.9 us (33%)
  other arithmetic  8.11 us (5%)
  Pallas kernels  8.05 us (5%)
  local copies, waits for them, and re-layouts  7.4 us (5%)
  blocking collectives  1.95 us (1%)
    ppermute x11, waiting for transfers between devices, to_core(): return lax.ppermute(value, AXIS, pairs)  39.6 us
    ppermute x17, starting transfers between devices, swap(): return lax.ppermute(value, AXIS, pairs)  32.4 us
    ppermute x17, waiting for transfers between devices, swap(): return lax.ppermute(value, AXIS, pairs)  32.1 us
    ppermute x11, starting transfers between devices, to_core(): return lax.ppermute(value, AXIS, pairs)  17.5 us
    pallas_call x12, Pallas kernels, call(): pl.pallas_call(body, out_shape=out_shape, grid=(1,), in_specs=specs, out_...  8.05 us
    unnamed x51, local copies, waits for them, and re-layouts  3.63 us
  transfers between devices with their start and end apart: 28, of which 9 were waited for; matrix products, arithmetic and copies ran while one was open for 8% of the time, Pallas kernels for 3%

profile of v1, /device:TPU:1, one launch (start us, length us, event | category | flops | bytes accessed | tf_op | source)
XLA Modules:
  0.0 148.1 jit_solution(1081629710206902725)
XLA Ops:
  0.0 1.3 copy-done
  3.7 1.3 collective-permute-start.2
  5.8 8.1 %collective-permute-done.2 = bf16[128,3584]{1,0:T(8,128)(2,1)S(1)} collective-permute-done((bf16[128,3584]{1,0:T(8,128)(2,1)S(1)}, bf16[128,3584]{1,0:T(8,128)(2,1)S(1)}, u32[]{:S(2)}, u32[]{:S(2)}) %collective-permute-start.2) | collective-permute-done | bytes 917536 | tf_op jit(solution)/shard_map/ppermute | solution.py:25
  14.3 2.2 %collective-permute-start.3 = (bf16[128,3840]{1,0:T(8,128)(2,1)S(1)}, bf16[128,3840]{1,0:T(8,128)(2,1)S(1)}, u32[]{:S(2)}, u32[]{:S(2)}) collective-permute-start(bf16[128,3840]{1,0:T(8,128)(2,1)S(1)} %pad_maximum_fusion), channel_id=1, source_target_pairs={{1,3},{3,1},{5,7},{7,5},{9,11},{11,9},{13,15},{15,13},{17,19},{19,... | collective-permute-start | bytes 2949128 | tf_op jit(solution)/shard_map/ppermute | solution.py:20
  17.1 1.9 %all_gather.3.stacked_ref = bf16[256,384]{1,0:T(8,128)(2,1)S(1)} all-gather(bf16[128,384]{1,0:T(8,128)(2,1)S(1)} %get-tuple-element.24), channel_id=1, replica_groups={{0,1},{2,3},{4,5},{6,7},{8,9},{10,11},{12,13},{14,15},{16,17},{18,19},{..., dimensions={0}, use_global_device_ids=true | all-gather | bytes 294912 | tf_op jit(solution)/shard_map/all_gather | solution.py:135
  19.0 1.4 shard_map.56
  20.4 3.0 %collective-permute-start = (bf16[384,1024]{1,0:T(8,128)(2,1)S(1)}, bf16[384,1024]{1,0:T(8,128)(2,1)}, u32[]{:S(2)}, u32[]{:S(2)}) collective-permute-start(bf16[384,1024]{1,0:T(8,128)(2,1)S(1)} %get-tuple-element.26), channel_id=1, source_target_pairs={{1,0},{3,2},{5,4},{7,6},{9,8},{11,10},{13,12},{15,14},{17,16},{19,... | collective-permute-start | bytes 2359304 | tf_op jit(solution)/shard_map/ppermute | solution.py:25
  23.4 6.0 %collective-permute-done.3 = bf16[128,3840]{1,0:T(8,128)(2,1)S(1)} collective-permute-done((bf16[128,3840]{1,0:T(8,128)(2,1)S(1)}, bf16[128,3840]{1,0:T(8,128)(2,1)S(1)}, u32[]{:S(2)}, u32[]{:S(2)}) %collective-permute-start.3) | collective-permute-done | bytes 983072 | tf_op jit(solution)/shard_map/ppermute | solution.py:20
  31.3 1.9 %collective-permute-start.6 = (bf16[128,2944]{1,0:T(8,128)(2,1)}, bf16[128,2944]{1,0:T(8,128)(2,1)}, u32[]{:S(2)}, u32[]{:S(2)}) collective-permute-start(bf16[128,2944]{1,0:T(8,128)(2,1)} %pad_maximum_fusion.1), channel_id=1, source_target_pairs={{1,5},{3,7},{5,1},{7,3},{9,13},{11,15},{13,9},{15,11},{17,21},{19,... | collective-permute-start | bytes 2261000 | tf_op jit(solution)/shard_map/ppermute | solution.py:20
  33.3 1.5 add.30
  35.7 1.3 collective-permute-start.4
  37.0 15.7 %collective-permute-done.6 = bf16[128,2944]{1,0:T(8,128)(2,1)} collective-permute-done((bf16[128,2944]{1,0:T(8,128)(2,1)}, bf16[128,2944]{1,0:T(8,128)(2,1)}, u32[]{:S(2)}, u32[]{:S(2)}) %collective-permute-start.6) | collective-permute-done | bytes 753696 | tf_op jit(solution)/shard_map/ppermute | solution.py:20
  54.8 3.5 %collective-permute-start.9 = (bf16[128,2176]{1,0:T(8,128)(2,1)}, bf16[128,2176]{1,0:T(8,128)(2,1)}, u32[]{:S(2)}, u32[]{:S(2)}) collective-permute-start(bf16[128,2176]{1,0:T(8,128)(2,1)} %pad_maximum_fusion.3), channel_id=1, source_target_pairs={{1,13},{3,15},{5,9},{7,11},{9,5},{11,7},{13,1},{15,3},{17,29},{19,... | collective-permute-start | bytes 1671176 | tf_op jit(solution)/shard_map/ppermute | solution.py:20
  59.8 4.4 %collective-permute-start.24 = (bf16[128,256]{1,0:T(8,128)(2,1)}, bf16[128,256]{1,0:T(8,128)(2,1)}, u32[]{:S(2)}, u32[]{:S(2)}) collective-permute-start(bf16[128,256]{1,0:T(8,128)(2,1)} %get-tuple-element.43), channel_id=1, source_target_pairs={{1,385},{3,387},{5,389},{7,391},{9,393},{11,395},{13,397},{15,399}... | collective-permute-start | bytes 196616 | tf_op jit(solution)/shard_map/ppermute | solution.py:20
  64.2 2.1 %collective-permute-done.24 = bf16[128,256]{1,0:T(8,128)(2,1)} collective-permute-done((bf16[128,256]{1,0:T(8,128)(2,1)}, bf16[128,256]{1,0:T(8,128)(2,1)}, u32[]{:S(2)}, u32[]{:S(2)}) %collective-permute-start.24) | collective-permute-done | bytes 65568 | tf_op jit(solution)/shard_map/ppermute | solution.py:20
  67.2 1.3 collective-permute-start.25
  70.8 1.3 collective-permute-start.7
  73.2 3.3 %collective-permute-start.12 = (bf16[128,1536]{1,0:T(8,128)(2,1)S(1)}, bf16[128,1536]{1,0:T(8,128)(2,1)S(1)}, u32[]{:S(2)}, u32[]{:S(2)}) collective-permute-start(bf16[128,1536]{1,0:T(8,128)(2,1)S(1)} %pad_maximum_fusion.6), channel_id=1, source_target_pairs={{1,17},{3,19},{5,21},{7,23},{9,25},{11,27},{13,29},{15,31},{17,1},... | collective-permute-start | bytes 1179656 | tf_op jit(solution)/shard_map/ppermute | solution.py:20
  78.8 2.8 %collective-permute-start.10 = (bf16[256,896]{1,0:T(8,128)(2,1)S(1)}, bf16[256,896]{1,0:T(8,128)(2,1)S(1)}, u32[]{:S(2)}, u32[]{:S(2)}) collective-permute-start(bf16[256,896]{1,0:T(8,128)(2,1)S(1)} %pad_maximum_fusion.5), channel_id=1, source_target_pairs={{1,0},{3,2},{5,4},{7,6},{9,8},{11,10},{13,12},{15,14},{17,16},{19,... | collective-permute-start | bytes 1376264 | tf_op jit(solution)/shard_map/ppermute | solution.py:25
  82.3 4.2 %collective-permute-start.15 = (bf16[128,1024]{1,0:T(8,128)(2,1)S(1)}, bf16[128,1024]{1,0:T(8,128)(2,1)S(1)}, u32[]{:S(2)}, u32[]{:S(2)}) collective-permute-start(bf16[128,1024]{1,0:T(8,128)(2,1)S(1)} %pad_maximum_fusion.9), channel_id=1, source_target_pairs={{1,33},{3,35},{5,37},{7,39},{9,41},{11,43},{13,45},{15,47},{17,49}... | collective-permute-start | bytes 786440 | tf_op jit(solution)/shard_map/ppermute | solution.py:20
  86.6 1.3 collective-permute-start.13
  89.1 4.2 %collective-permute-done.15 = bf16[128,1024]{1,0:T(8,128)(2,1)S(1)} collective-permute-done((bf16[128,1024]{1,0:T(8,128)(2,1)S(1)}, bf16[128,1024]{1,0:T(8,128)(2,1)S(1)}, u32[]{:S(2)}, u32[]{:S(2)}) %collective-permute-start.15) | collective-permute-done | bytes 262176 | tf_op jit(solution)/shard_map/ppermute | solution.py:20
  93.3 4.9 %collective-permute-start.18 = (bf16[128,640]{1,0:T(8,128)(2,1)S(1)}, bf16[128,640]{1,0:T(8,128)(2,1)S(1)}, u32[]{:S(2)}, u32[]{:S(2)}) collective-permute-start(bf16[128,640]{1,0:T(8,128)(2,1)S(1)} %pad_maximum_fusion.12), channel_id=1, source_target_pairs={{1,97},{3,99},{5,101},{7,103},{9,105},{11,107},{13,109},{15,111},{... | collective-permute-start | bytes 491528 | tf_op jit(solution)/shard_map/ppermute | solution.py:20
  98.3 1.3 collective-permute-start.16
  100.7 1.5 collective-permute-done.18
  102.2 1.9 %collective-permute-start.21 = (bf16[128,384]{1,0:T(8,128)(2,1)S(1)}, bf16[128,384]{1,0:T(8,128)(2,1)S(1)}, u32[]{:S(2)}, u32[]{:S(2)}) collective-permute-start(bf16[128,384]{1,0:T(8,128)(2,1)S(1)} %pad_maximum_fusion.14), channel_id=1, source_target_pairs={{1,129},{3,131},{5,133},{7,135},{9,137},{11,139},{13,141},{15,143}... | collective-permute-start | bytes 294920 | tf_op jit(solution)/shard_map/ppermute | solution.py:20
  104.2 1.3 collective-permute-start.19
  105.5 2.1 %collective-permute-done.21 = bf16[128,384]{1,0:T(8,128)(2,1)S(1)} collective-permute-done((bf16[128,384]{1,0:T(8,128)(2,1)S(1)}, bf16[128,384]{1,0:T(8,128)(2,1)S(1)}, u32[]{:S(2)}, u32[]{:S(2)}) %collective-permute-start.21) | collective-permute-done | bytes 98336 | tf_op jit(solution)/shard_map/ppermute | solution.py:20
  107.6 1.3 collective-permute-start.22
  113.4 1.3 collective-permute-start.27
  114.7 31.5 %collective-permute-done.27.got_ref = bf16[8,384,128]{2,1,0:T(8,128)(2,1)S(1)} collective-permute-done((bf16[8,384,128]{2,1,0:T(8,128)(2,1)S(1)}, bf16[8,384,128]{2,1,0:T(8,128)(2,1)S(1)}, u32[]{:S(2)}, u32[]{:S(2)}) %collective-permute-start.27) | collective-permute-done | bytes 786464 | tf_op jit(solution)/shard_map/ppermute | solution.py:25
  146.2 1.9 %shard_map.66 = f32[512,384]{1,0:T(8,128)} custom-call(s32[1]{0:T(128)} %bitcast.where_ref, f32[512,384]{1,0:T(8,128)S(1)} %get-tuple-element.25.state_ref, bf16[9,512,128]{2,1,0:T(8,128)(2,1)S(1)} %copy-done.1, bf16[8,384,128]{2,1,0:T(8,128)(2,1)S(1)} %maximum_select_fusion.own_ref, bf16[8,384,128]{2,1,0:T(8,128)(2,1)S(1)} %collective-permute-done.27.got_ref), custom_call_target="tpu_custom_call" | custom-call | bytes 3538948 | tf_op jit(solution)/shard_map/pallas_call | solution.py:44
  (132 shorter events, 24.3 us)
Async XLA Ops:
  3.7 10.1 %collective-permute-start.2 = (bf16[128,3584]{1,0:T(8,128)(2,1)S(1)}, bf16[128,3584]{1,0:T(8,128)(2,1)S(1)}, u32[]{:S(2)}, u32[]{:S(2)}) collective-permute-start(bf16[128,3584]{1,0:T(8,128)(2,1)S(1)} %shard_map.57), channel_id=1, source_target_pairs={{0,1},{2,3},{4,5},{6,7},{8,9},{10,11},{12,13},{14,15},{16,17},{18,... | collective-permute-start | bytes 2752520 | tf_op jit(solution)/shard_map/ppermute | solution.py:25
  5.8 24.6 %copy-start.17 = (bf16[128,256]{1,0:T(8,128)(2,1)}, bf16[128,256]{1,0:T(8,128)(2,1)S(1)}, u32[]{:S(2)}) copy-start(bf16[128,256]{1,0:T(8,128)(2,1)S(1)} %get-tuple-element.48) | copy-start | bytes 196612
  5.8 48.1 %copy-start.14 = (bf16[128,256]{1,0:T(8,128)(2,1)}, bf16[128,256]{1,0:T(8,128)(2,1)S(1)}, u32[]{:S(2)}) copy-start(bf16[128,256]{1,0:T(8,128)(2,1)S(1)} %get-tuple-element.47) | copy-start | bytes 196612
  14.3 15.1 %collective-permute-start.3 = (bf16[128,3840]{1,0:T(8,128)(2,1)S(1)}, bf16[128,3840]{1,0:T(8,128)(2,1)S(1)}, u32[]{:S(2)}, u32[]{:S(2)}) collective-permute-start(bf16[128,3840]{1,0:T(8,128)(2,1)S(1)} %pad_maximum_fusion), channel_id=1, source_target_pairs={{1,3},{3,1},{5,7},{7,5},{9,11},{11,9},{13,15},{15,13},{17,19},{19,... | collective-permute-start | bytes 2949128 | tf_op jit(solution)/shard_map/ppermute | solution.py:20
  20.4 12.9 %collective-permute-start = (bf16[384,1024]{1,0:T(8,128)(2,1)S(1)}, bf16[384,1024]{1,0:T(8,128)(2,1)}, u32[]{:S(2)}, u32[]{:S(2)}) collective-permute-start(bf16[384,1024]{1,0:T(8,128)(2,1)S(1)} %get-tuple-element.26), channel_id=1, source_target_pairs={{1,0},{3,2},{5,4},{7,6},{9,8},{11,10},{13,12},{15,14},{17,16},{19,... | collective-permute-start | bytes 2359304 | tf_op jit(solution)/shard_map/ppermute | solution.py:25
  31.3 21.4 %collective-permute-start.6 = (bf16[128,2944]{1,0:T(8,128)(2,1)}, bf16[128,2944]{1,0:T(8,128)(2,1)}, u32[]{:S(2)}, u32[]{:S(2)}) collective-permute-start(bf16[128,2944]{1,0:T(8,128)(2,1)} %pad_maximum_fusion.1), channel_id=1, source_target_pairs={{1,5},{3,7},{5,1},{7,3},{9,13},{11,15},{13,9},{15,11},{17,21},{19,... | collective-permute-start | bytes 2261000 | tf_op jit(solution)/shard_map/ppermute | solution.py:20
  34.8 18.0 %copy-start.8 = (bf16[128,2688]{1,0:T(8,128)(2,1)S(1)}, bf16[128,2688]{1,0:T(8,128)(2,1)}, u32[]{:S(2)}) copy-start(bf16[128,2688]{1,0:T(8,128)(2,1)} %copy-done.7) | copy-start | bytes 2064388
  35.7 32.9 %collective-permute-start.4 = (bf16[256,1152]{1,0:T(8,128)(2,1)}, bf16[256,1152]{1,0:T(8,128)(2,1)S(1)}, u32[]{:S(2)}, u32[]{:S(2)}) collective-permute-start(bf16[256,1152]{1,0:T(8,128)(2,1)} %pad_maximum_fusion.2), channel_id=1, source_target_pairs={{1,0},{3,2},{5,4},{7,6},{9,8},{11,10},{13,12},{15,14},{17,16},{19,... | collective-permute-start | bytes 1769480 | tf_op jit(solution)/shard_map/ppermute | solution.py:25
  54.8 17.3 %collective-permute-start.9 = (bf16[128,2176]{1,0:T(8,128)(2,1)}, bf16[128,2176]{1,0:T(8,128)(2,1)}, u32[]{:S(2)}, u32[]{:S(2)}) collective-permute-start(bf16[128,2176]{1,0:T(8,128)(2,1)} %pad_maximum_fusion.3), channel_id=1, source_target_pairs={{1,13},{3,15},{5,9},{7,11},{9,5},{11,7},{13,1},{15,3},{17,29},{19,... | collective-permute-start | bytes 1671176 | tf_op jit(solution)/shard_map/ppermute | solution.py:20
  59.1 9.4 %collective-permute-start.1 = (bf16[192,1024]{1,0:T(8,128)(2,1)}, bf16[192,1024]{1,0:T(8,128)(2,1)S(1)}, u32[]{:S(2)}, u32[]{:S(2)}) collective-permute-start(bf16[192,1024]{1,0:T(8,128)(2,1)} %get-tuple-element.41), channel_id=1, source_target_pairs={{0,2},{2,0},{4,6},{6,4},{8,10},{10,8},{12,14},{14,12},{16,18},{18,... | collective-permute-start | bytes 1179656 | tf_op jit(solution)/shard_map/ppermute | solution.py:20
  59.8 6.5 %collective-permute-start.24 = (bf16[128,256]{1,0:T(8,128)(2,1)}, bf16[128,256]{1,0:T(8,128)(2,1)}, u32[]{:S(2)}, u32[]{:S(2)}) collective-permute-start(bf16[128,256]{1,0:T(8,128)(2,1)} %get-tuple-element.43), channel_id=1, source_target_pairs={{1,385},{3,387},{5,389},{7,391},{9,393},{11,395},{13,397},{15,399}... | collective-permute-start | bytes 196616 | tf_op jit(solution)/shard_map/ppermute | solution.py:20
  67.2 45.0 %collective-permute-start.25 = (bf16[256,256]{1,0:T(8,128)(2,1)S(1)}, bf16[256,256]{1,0:T(8,128)(2,1)S(1)}, u32[]{:S(2)}, u32[]{:S(2)}) collective-permute-start(bf16[256,256]{1,0:T(8,128)(2,1)S(1)} %pad_maximum_fusion.13), channel_id=1, source_target_pairs={{1,0},{3,2},{5,4},{7,6},{9,8},{11,10},{13,12},{15,14},{17,16},{19,... | collective-permute-start | bytes 393224 | tf_op jit(solution)/shard_map/ppermute | solution.py:25
  69.0 7.6 %collective-permute-start.5 = (bf16[192,896]{1,0:T(8,128)(2,1)S(1)}, bf16[192,896]{1,0:T(8,128)(2,1)S(1)}, u32[]{:S(2)}, u32[]{:S(2)}) collective-permute-start(bf16[192,896]{1,0:T(8,128)(2,1)S(1)} %get-tuple-element.28.own_ref), channel_id=1, source_target_pairs={{0,4},{2,6},{4,0},{6,2},{8,12},{10,14},{12,8},{14,10},{16,20},{18,... | collective-permute-start | bytes 1032200 | tf_op jit(solution)/shard_map/ppermute | solution.py:20
  70.8 5.8 %collective-permute-start.7 = (bf16[256,1024]{1,0:T(8,128)(2,1)S(1)}, bf16[256,1024]{1,0:T(8,128)(2,1)S(1)}, u32[]{:S(2)}, u32[]{:S(2)}) collective-permute-start(bf16[256,1024]{1,0:T(8,128)(2,1)S(1)} %pad_maximum_fusion.4), channel_id=1, source_target_pairs={{1,0},{3,2},{5,4},{7,6},{9,8},{11,10},{13,12},{15,14},{17,16},{19,... | collective-permute-start | bytes 1572872 | tf_op jit(solution)/shard_map/ppermute | solution.py:25
  73.2 8.9 %collective-permute-start.12 = (bf16[128,1536]{1,0:T(8,128)(2,1)S(1)}, bf16[128,1536]{1,0:T(8,128)(2,1)S(1)}, u32[]{:S(2)}, u32[]{:S(2)}) collective-permute-start(bf16[128,1536]{1,0:T(8,128)(2,1)S(1)} %pad_maximum_fusion.6), channel_id=1, source_target_pairs={{1,17},{3,19},{5,21},{7,23},{9,25},{11,27},{13,29},{15,31},{17,1},... | collective-permute-start | bytes 1179656 | tf_op jit(solution)/shard_map/ppermute | solution.py:20
  77.1 10.8 %collective-permute-start.8 = (bf16[192,768]{1,0:T(8,128)(2,1)S(1)}, bf16[192,768]{1,0:T(8,128)(2,1)S(1)}, u32[]{:S(2)}, u32[]{:S(2)}) collective-permute-start(bf16[192,768]{1,0:T(8,128)(2,1)S(1)} %get-tuple-element.30.own_ref), channel_id=1, source_target_pairs={{0,12},{2,14},{4,8},{6,10},{8,4},{10,6},{12,0},{14,2},{16,28},{18,... | collective-permute-start | bytes 884744 | tf_op jit(solution)/shard_map/ppermute | solution.py:20
  78.8 9.1 %collective-permute-start.10 = (bf16[256,896]{1,0:T(8,128)(2,1)S(1)}, bf16[256,896]{1,0:T(8,128)(2,1)S(1)}, u32[]{:S(2)}, u32[]{:S(2)}) collective-permute-start(bf16[256,896]{1,0:T(8,128)(2,1)S(1)} %pad_maximum_fusion.5), channel_id=1, source_target_pairs={{1,0},{3,2},{5,4},{7,6},{9,8},{11,10},{13,12},{15,14},{17,16},{19,... | collective-permute-start | bytes 1376264 | tf_op jit(solution)/shard_map/ppermute | solution.py:25
  82.3 10.9 %collective-permute-start.15 = (bf16[128,1024]{1,0:T(8,128)(2,1)S(1)}, bf16[128,1024]{1,0:T(8,128)(2,1)S(1)}, u32[]{:S(2)}, u32[]{:S(2)}) collective-permute-start(bf16[128,1024]{1,0:T(8,128)(2,1)S(1)} %pad_maximum_fusion.9), channel_id=1, source_target_pairs={{1,33},{3,35},{5,37},{7,39},{9,41},{11,43},{13,45},{15,47},{17,49}... | collective-permute-start | bytes 786440 | tf_op jit(solution)/shard_map/ppermute | solution.py:20
  86.6 13.0 %collective-permute-start.13 = (bf16[256,768]{1,0:T(8,128)(2,1)S(1)}, bf16[256,768]{1,0:T(8,128)(2,1)S(1)}, u32[]{:S(2)}, u32[]{:S(2)}) collective-permute-start(bf16[256,768]{1,0:T(8,128)(2,1)S(1)} %pad_maximum_fusion.7), channel_id=1, source_target_pairs={{1,0},{3,2},{5,4},{7,6},{9,8},{11,10},{13,12},{15,14},{17,16},{19,... | collective-permute-start | bytes 1179656 | tf_op jit(solution)/shard_map/ppermute | solution.py:25
  88.4 11.2 %collective-permute-start.11 = (bf16[192,640]{1,0:T(8,128)(2,1)S(1)}, bf16[192,640]{1,0:T(8,128)(2,1)S(1)}, u32[]{:S(2)}, u32[]{:S(2)}) collective-permute-start(bf16[192,640]{1,0:T(8,128)(2,1)S(1)} %get-tuple-element.32.own_ref), channel_id=1, source_target_pairs={{0,16},{2,18},{4,20},{6,22},{8,24},{10,26},{12,28},{14,30},{16,0},... | collective-permute-start | bytes 737288 | tf_op jit(solution)/shard_map/ppermute | solution.py:20
  93.3 8.9 %copy-start.19 = (bf16[128,256]{1,0:T(8,128)(2,1)S(1)}, bf16[128,256]{1,0:T(8,128)(2,1)}, u32[]{:S(2)}) copy-start(bf16[128,256]{1,0:T(8,128)(2,1)} %get-tuple-element.50) | copy-start | bytes 196612
  93.3 8.9 %collective-permute-start.18 = (bf16[128,640]{1,0:T(8,128)(2,1)S(1)}, bf16[128,640]{1,0:T(8,128)(2,1)S(1)}, u32[]{:S(2)}, u32[]{:S(2)}) collective-permute-start(bf16[128,640]{1,0:T(8,128)(2,1)S(1)} %pad_maximum_fusion.12), channel_id=1, source_target_pairs={{1,97},{3,99},{5,101},{7,103},{9,105},{11,107},{13,109},{15,111},{... | collective-permute-start | bytes 491528 | tf_op jit(solution)/shard_map/ppermute | solution.py:20
  98.3 10.7 %collective-permute-start.16 = (bf16[256,640]{1,0:T(8,128)(2,1)S(1)}, bf16[256,640]{1,0:T(8,128)(2,1)S(1)}, u32[]{:S(2)}, u32[]{:S(2)}) collective-permute-start(bf16[256,640]{1,0:T(8,128)(2,1)S(1)} %pad_maximum_fusion.8), channel_id=1, source_target_pairs={{1,0},{3,2},{5,4},{7,6},{9,8},{11,10},{13,12},{15,14},{17,16},{19,... | collective-permute-start | bytes 983048 | tf_op jit(solution)/shard_map/ppermute | solution.py:25
  100.0 8.9 %collective-permute-start.14 = (bf16[192,512]{1,0:T(8,128)(2,1)S(1)}, bf16[192,512]{1,0:T(8,128)(2,1)S(1)}, u32[]{:S(2)}, u32[]{:S(2)}) collective-permute-start(bf16[192,512]{1,0:T(8,128)(2,1)S(1)} %get-tuple-element.34.own_ref), channel_id=1, source_target_pairs={{0,32},{2,34},{4,36},{6,38},{8,40},{10,42},{12,44},{14,46},{16,48}... | collective-permute-start | bytes 589832 | tf_op jit(solution)/shard_map/ppermute | solution.py:20
  102.2 5.4 %collective-permute-start.21 = (bf16[128,384]{1,0:T(8,128)(2,1)S(1)}, bf16[128,384]{1,0:T(8,128)(2,1)S(1)}, u32[]{:S(2)}, u32[]{:S(2)}) collective-permute-start(bf16[128,384]{1,0:T(8,128)(2,1)S(1)} %pad_maximum_fusion.14), channel_id=1, source_target_pairs={{1,129},{3,131},{5,133},{7,135},{9,137},{11,139},{13,141},{15,143}... | collective-permute-start | bytes 294920 | tf_op jit(solution)/shard_map/ppermute | solution.py:20
  104.2 5.9 %collective-permute-start.19 = (bf16[256,512]{1,0:T(8,128)(2,1)S(1)}, bf16[256,512]{1,0:T(8,128)(2,1)S(1)}, u32[]{:S(2)}, u32[]{:S(2)}) collective-permute-start(bf16[256,512]{1,0:T(8,128)(2,1)S(1)} %pad_maximum_fusion.10), channel_id=1, source_target_pairs={{1,0},{3,2},{5,4},{7,6},{9,8},{11,10},{13,12},{15,14},{17,16},{19,... | collective-permute-start | bytes 786440 | tf_op jit(solution)/shard_map/ppermute | solution.py:25
  107.6 3.5 %collective-permute-start.22 = (bf16[256,384]{1,0:T(8,128)(2,1)S(1)}, bf16[256,384]{1,0:T(8,128)(2,1)S(1)}, u32[]{:S(2)}, u32[]{:S(2)}) collective-permute-start(bf16[256,384]{1,0:T(8,128)(2,1)S(1)} %pad_maximum_fusion.11), channel_id=1, source_target_pairs={{1,0},{3,2},{5,4},{7,6},{9,8},{11,10},{13,12},{15,14},{17,16},{19,... | collective-permute-start | bytes 589832 | tf_op jit(solution)/shard_map/ppermute | solution.py:25
  109.4 0.7 collective-permute-start.17
  110.4 0.7 collective-permute-start.20
  111.5 0.7 collective-permute-start.23
  112.5 0.7 collective-permute-start.26
  113.4 32.8 %collective-permute-start.27 = (bf16[8,384,128]{2,1,0:T(8,128)(2,1)S(1)}, bf16[8,384,128]{2,1,0:T(8,128)(2,1)S(1)}, u32[]{:S(2)}, u32[]{:S(2)}) collective-permute-start(bf16[8,384,128]{2,1,0:T(8,128)(2,1)S(1)} %maximum_select_fusion.own_ref), channel_id=1, source_target_pairs={{0,1},{2,3},{4,5},{6,7},{8,9},{10,11},{12,13},{14,15},{16,17},{18,... | collective-permute-start | bytes 2359304 | tf_op jit(solution)/shard_map/ppermute | solution.py:25
  (19 other events, 61.3 us)

commit v2 on v1

v2 whole, which is shorter than its diff:
```python
import jax
import jax.numpy as jnp
from jax import lax
from jax.experimental import pallas as pl
from jax.experimental.pallas import tpu as pltpu
from jax.sharding import PartitionSpec as P

BF = jnp.bfloat16
F32 = jnp.float32
AXIS = "seq"
MASKS = {3: 12, 6: 96, 8: 384}


def mask_of(level):
    return MASKS.get(level, 1 << level)


def swap(value, mask, core):
    pairs = [(d, d ^ mask) for d in range(lax.axis_size(AXIS)) if d & 1 == core]
    return lax.ppermute(value, AXIS, pairs)


def to_core(value, core, mask=1):
    pairs = [(d ^ mask, d) for d in range(lax.axis_size(AXIS)) if d & 1 == core]
    return lax.ppermute(value, AXIS, pairs)


def dot(a, b, dims):
    return lax.dot_general(a, b, (dims, ((), ())), preferred_element_type=F32)


NN = ((1,), (0,))
NT = ((1,), (1,))
TN = ((0,), (0,))


def call(body, out_shape, args, in_specs=None, flops=0):
    if in_specs is None:
        in_specs = [None] * len(args)
    specs = [s if s is not None else pl.BlockSpec(memory_space=pltpu.VMEM) for s in in_specs]
    single = not isinstance(out_shape, (list, tuple))
    outs = pl.BlockSpec(memory_space=pltpu.VMEM)
    size = sum(a.size * a.dtype.itemsize for a in args)
    return pl.pallas_call(
        body,
        out_shape=out_shape,
        grid=(1,),
        in_specs=specs,
        out_specs=outs if single else [outs] * len(out_shape),
        compiler_params=pltpu.CompilerParams(vmem_limit_bytes=32 * 2**20),
        cost_estimate=pl.CostEstimate(flops=flops, bytes_accessed=size, transcendentals=0),
    )(*args)


SCALAR = pl.BlockSpec(memory_space=pltpu.SMEM)


def sds(shape, dtype):
    return jax.ShapeDtypeStruct(shape, dtype)


def front_body(inverse_ref, right_ref, project_ref, spread_ref, static_ref, state_ref, sums_ref):
    levels = project_ref.shape[0]
    at = 0
    for low in range(1, levels - 1):
        spread = spread_ref[low]
        for high in range(low + 1, levels):
            block = dot(spread, project_ref[high], TN)
            static_ref[:, at : at + block.shape[1]] = block.astype(BF)
            at += block.shape[1]
    state = dot(inverse_ref[0], right_ref[...], NN)
    state_ref[...] = state
    sums_ref[...] = dot(project_ref[0], state.astype(BF), TN).astype(BF)


def first_body(state_ref, stacked_ref, capacity_ref, spread_ref, project_ref, next_ref, sums_ref):
    coefficients = dot(capacity_ref[0], stacked_ref[...], NN).astype(BF)
    state = state_ref[...] - dot(spread_ref[0], coefficients, NN)
    next_ref[...] = state
    rounded = state.astype(BF)
    for level in range(1, project_ref.shape[0]):
        block = dot(rounded, project_ref[level], TN)
        rank = block.shape[1]
        sums_ref[:, (level - 1) * rank : level * rank] = block.astype(BF)


def rows_of(part, count):
    return pl.ds(pl.multiple_of(part * count, count), count)


def merge_body(side_ref, own_ref, other_ref, keep_ref, send_ref):
    side = side_ref[0]
    count = keep_ref.shape[0]
    for part, out_ref in ((side, keep_ref), (1 - side, send_ref)):
        rows = rows_of(part, count)
        total = own_ref[rows, :].astype(F32) + other_ref[rows, :].astype(F32)
        out_ref[...] = total.astype(BF)


def cut_body(side_ref, own_ref, other_ref, capacity_ref, first_ref, keep_ref, send_ref):
    side = side_ref[0]
    width = first_ref.shape[1] - capacity_ref.shape[2]
    first = own_ref[:, :width].astype(F32) + other_ref[:, :width].astype(F32)
    first_ref[:, :width] = first.astype(BF)
    first_ref[:, width:] = capacity_ref[0]
    count = keep_ref.shape[0]
    for part, out_ref in ((side, keep_ref), (1 - side, send_ref)):
        rows = rows_of(part, count)
        total = own_ref[rows, width:].astype(F32) + other_ref[rows, width:].astype(F32)
        out_ref[...] = total.astype(BF)


def static_body(side_ref, own_ref, other_ref, capacity_ref, *out_refs, cut, width):
    message_ref = out_refs[0]
    count = own_ref.shape[0]
    inner = capacity_ref.shape[2]
    if width:
        total = own_ref[:, cut : cut + width].astype(F32) + other_ref[:, cut : cut + width].astype(F32)
        message_ref[:, :width] = total.astype(BF)
    message_ref[:, width : width + inner] = capacity_ref[0, rows_of(side_ref[0], count), :]
    if own_ref.shape[1] > cut + width:
        rest = own_ref[:, cut + width :].astype(F32) + other_ref[:, cut + width :].astype(F32)
        message_ref[:, width + inner :] = rest.astype(BF)
    if cut:
        out_refs[1][:count, :] = own_ref[:, :cut]
        out_refs[1][count:, :] = other_ref[:, :cut]


def step_body(place_ref, own_ref, other_ref, near_ref, far_ref, *out_refs):
    rank = near_ref.shape[0]
    width = own_ref.shape[1] - rank
    lower = place_ref[0] == 0
    own, other = own_ref[:, :rank], other_ref[:, :rank]
    stacked = jnp.concatenate([jnp.where(lower, own, other), jnp.where(lower, other, own)], 1)
    near = dot(stacked, near_ref[:, width:], NT).astype(BF)
    far = dot(stacked, far_ref[:, width:], NT).astype(BF)
    if out_refs[0].shape[1] > rank:
        out_refs[0][:, :rank] = near
        out_refs[0][:, rank:] = far
    else:
        first = place_ref[1] == 0
        part = rank // 2
        near_own, far_own = near[:, :part], far[:, :part]
        out_refs[0][...] = jnp.concatenate(
            [jnp.where(first, near_own, far_own), jnp.where(first, far_own, near_own)], 1
        )
    if width:
        total = own_ref[:, rank:].astype(F32) + other_ref[:, rank:].astype(F32)
        total = total - dot(near, near_ref[:, :width], NN)
        total = total - dot(far, far_ref[:, :width], NN)
        out_refs[1][...] = total.astype(BF)


def spread_body(place_ref, state_ref, spread_ref, near0_ref, far0_ref, near1_ref, far1_ref, out_ref, *, base):
    zero_core = place_ref[0] == 0
    first = place_ref[1] == 0
    total = state_ref[...]
    for index in range(near0_ref.shape[0]):
        near = jnp.where(zero_core, near0_ref[index], near1_ref[index])
        far = jnp.where(zero_core, far0_ref[index], far1_ref[index])
        spread = spread_ref[base + index]
        rows = jnp.concatenate([jnp.where(first, near, far), jnp.where(first, far, near)], 0)
        total = total - dot(spread, rows, NT)
    out_ref[...] = total


def on_device(right_side, leaf_inverse, project_rows, spread_rows, capacity):
    levels, samples, rank = project_rows.shape
    columns = right_side.shape[1]
    inner = capacity.shape[2]
    size = lax.axis_size(AXIS)
    device = lax.axis_index(AXIS)

    def bit(level):
        return (device >> level & 1).astype(jnp.int32)

    def level_block(array, level):
        return pl.BlockSpec((1,) + array.shape[1:], lambda i: (level, 0, 0))

    core, side = bit(0), bit(1)
    pairs = (levels - 1) * (levels - 2) // 2
    static, state, sums = call(
        front_body,
        [sds((rank, pairs * rank), BF), sds((samples, columns), F32), sds((rank, columns), BF)],
        [leaf_inverse, right_side, project_rows, spread_rows],
    )
    static_other = to_core(static, 1)
    stacked = lax.all_gather(
        sums, AXIS, axis_index_groups=[[d, d + 1] for d in range(0, size, 2)], tiled=True
    )
    width = (levels - 2) * rank
    part = rank // 2
    first, keep, send = call(
        cut_body,
        [
            sds((rank, width + inner), BF),
            sds((part, pairs * rank - width), BF),
            sds((part, pairs * rank - width), BF),
        ],
        [side[None], static, static_other, capacity],
        [SCALAR, None, None, level_block(capacity, 1)],
    )
    static_got = swap(send, 2, 1)
    near, far = to_core(first, 0), to_core(first, 0, 3)

    state, sums = call(
        first_body,
        [sds((samples, columns), F32), sds((columns, (levels - 1) * rank), BF)],
        [state, stacked, capacity, spread_rows, project_rows],
        [None, None, level_block(capacity, 0), level_block(spread_rows, 0), None],
    )
    half = columns // 2
    own, send = call(
        merge_body,
        [sds((half, (levels - 1) * rank), BF)] * 2,
        [side[None], sums, to_core(sums, 0)],
        [SCALAR, None, None],
    )

    def spread_out(state, mine, base):
        near0 = jnp.stack([c[:, :rank] for c in mine])
        theirs = jnp.stack([c[:, -rank:] for c in mine])
        far0 = swap(theirs, 2, 0)
        near1 = to_core(near0, 1)
        far1 = to_core(theirs, 1, 3)
        return call(
            lambda *refs: spread_body(*refs, base=base),
            sds((samples, columns), F32),
            [jnp.stack([core, side]), state, spread_rows, near0, far0, near1, far1],
            [SCALAR] + [None] * 6,
        )

    gathered = []
    early = levels - 3
    message, cut = keep, 0
    for level in range(1, levels):
        other = swap(send, mask_of(level), 0)
        if level < levels - 1:
            width = (levels - 2 - level) * rank
            total = message.shape[1] - cut + inner
            outs = [sds((part, total), BF)] + ([sds((rank, cut), BF)] if cut else [])
            results = call(
                lambda *refs, c=cut, w=width: static_body(*refs, cut=c, width=w),
                outs,
                [side[None], message, static_got, capacity],
                [SCALAR, None, None, level_block(capacity, level + 1)],
            )
            message = results[0]
            static_got = swap(message, mask_of(level + 1), 1)
            both = results[1] if cut else None
            cut = width + inner
        else:
            both = jnp.concatenate([message, static_got], 0)
        if level > 1:
            near, far = to_core(both, 0), to_core(both, 0, 3)

        width = (levels - 1 - level) * rank
        outs = [sds((half, 2 * rank if level == 1 else rank), BF)]
        if width:
            outs.append(sds((half, width), BF))
        results = call(
            step_body,
            outs,
            [jnp.stack([bit(level), side]), own, other, near, far],
            [SCALAR, None, None, None, None],
        )
        gathered.append(results[0])
        if width:
            own = send = results[1]
        if level == early:
            state = spread_out(state, gathered, 1)
    return spread_out(state, gathered[early:], early + 1)


def solution(mesh):
    return jax.shard_map(
        on_device,
        mesh=mesh,
        in_specs=(
            P(AXIS, None),
            P(AXIS, None, None),
            P(None, AXIS, None),
            P(None, AXIS, None),
            P(None, AXIS, None),
        ),
        out_specs=P(AXIS, None),
        check_vma=False,
    )
```

time: 149 us -> 156 us (1.047)
  waiting for transfers between devices: 71.8 us -> 33.2 us
  starting transfers between devices: 49.9 us -> 79.7 us
  Pallas kernels: 8.05 us -> 20.6 us
  blocking collectives: 1.95 us -> 9.44 us
  other arithmetic: 8.11 us -> 0.7 us
  local copies, waits for them, and re-layouts: 7.4 us -> 9.85 us
    ppermute x11 -> x22, starting transfers between devices: 17.5 us -> 49.1 us  [to_core(): return lax.ppermute(value, AXIS, pairs)]
    ppermute x11 -> x22, waiting for transfers between devices: 39.6 us -> 14.4 us  [to_core(): return lax.ppermute(value, AXIS, pairs)]
    ppermute x17 -> x18, waiting for transfers between devices: 32.1 us -> 18.8 us  [swap(): return lax.ppermute(value, AXIS, pairs)]
    pallas_call x12 -> x21, Pallas kernels: 8.05 us -> 20.6 us  [call(): pl.pallas_call(body, out_shape=out_shape, grid=(1,), in_specs=specs, out_...]
    all_gather x1, blocking collectives: 1.95 us -> 9.44 us  [on_device(): lax.all_gather(sums, AXIS, axis_index_groups=[[d, d + 1] for d in range(0...]
    unnamed x51 -> x28, local copies, waits for them, and re-layouts: 3.63 us -> 9.22 us
    concatenate x15 -> x0, other arithmetic: 3.98 us -> none  [the longest x6 2 us: on_device(): message = jnp.concatenate([block, static[:, width:]], 1)]
    add x8 -> x0, other arithmetic: 3.92 us -> none  [the longest x6 2.23 us: on_device(): static = static[:, width:] + got[:, cut:]]
  transfers between devices with their start and end apart: 28 -> 40, of which waited for: 9 -> 7; matrix products, arithmetic and copies ran while one was open for 8% -> 3% of each run, Pallas kernels for 3% -> 11%
where the time goes in v2:
time: 156 us; the launch traced here: 154 us
  starting transfers between devices  79.7 us (51%)
  waiting for transfers between devices  33.2 us (21%)
  Pallas kernels  20.6 us (13%)
  local copies, waits for them, and re-layouts  9.85 us (6%)
  blocking collectives  9.44 us (6%)
    ppermute x22, starting transfers between devices, to_core(): return lax.ppermute(value, AXIS, pairs)  49.1 us
    ppermute x18, starting transfers between devices, swap(): return lax.ppermute(value, AXIS, pairs)  30.6 us
    pallas_call x21, Pallas kernels, call(): pl.pallas_call(body, out_shape=out_shape, grid=(1,), in_specs=specs, out_...  20.6 us
    ppermute x18, waiting for transfers between devices, swap(): return lax.ppermute(value, AXIS, pairs)  18.8 us
    ppermute x22, waiting for transfers between devices, to_core(): return lax.ppermute(value, AXIS, pairs)  14.4 us
    all_gather x1, blocking collectives, on_device(): lax.all_gather(sums, AXIS, axis_index_groups=[[d, d + 1] for d in range(0...  9.44 us
    unnamed x28, local copies, waits for them, and re-layouts  9.22 us
  transfers between devices with their start and end apart: 40, of which 7 were waited for; matrix products, arithmetic and copies ran while one was open for 3% of the time, Pallas kernels for 11%

profile of v2, /device:TPU:1, one launch (start us, length us, event | category | flops | bytes accessed | tf_op | source)
XLA Modules:
  0.0 154.1 jit_solution(655934906087037562)
XLA Ops:
  4.6 1.6 %shard_map.55 = (bf16[128,3584]{1,0:T(8,128)(2,1)S(1)}, f32[512,384]{1,0:T(8,128)S(1)}, bf16[128,384]{1,0:T(8,128)(2,1)S(1)}) custom-call(bf16[1,512,512]{2,1,0:T(8,128)(2,1)S(1)} %copy-done.6, bf16[512,384]{1,0:T(8,128)(2,1)S(1)} %copy-done.7, bf16[9,512,128]{2,1,0:T(8,128)(2,1)S(1)} %copy-done.3, bf16[9,512,128]{2,1,0:T(8,128)(2,1)S(1)} %copy-done.1), custom_call_target="tpu_custom_call" | custom-call | bytes 3276800 | tf_op jit(solution)/shard_map/pallas_call | solution.py:44
  7.5 9.4 %all_gather.3.stacked_ref = bf16[256,384]{1,0:T(8,128)(2,1)S(1)} all-gather(bf16[128,384]{1,0:T(8,128)(2,1)S(1)} %get-tuple-element.42), channel_id=1, replica_groups={{0,1},{2,3},{4,5},{6,7},{8,9},{10,11},{12,13},{14,15},{16,17},{18,19},{..., dimensions={0}, use_global_device_ids=true | all-gather | bytes 294912 | tf_op jit(solution)/shard_map/all_gather | solution.py:188
  16.9 1.4 shard_map.56
  19.2 3.2 %collective-permute-start = (bf16[384,1024]{1,0:T(8,128)(2,1)S(1)}, bf16[384,1024]{1,0:T(8,128)(2,1)}, u32[]{:S(2)}, u32[]{:S(2)}) collective-permute-start(bf16[384,1024]{1,0:T(8,128)(2,1)S(1)} %get-tuple-element.44.own_ref), channel_id=1, source_target_pairs={{1,0},{3,2},{5,4},{7,6},{9,8},{11,10},{13,12},{15,14},{17,16},{19,... | collective-permute-start | bytes 2359304 | tf_op jit(solution)/shard_map/ppermute | solution.py:25
  22.3 2.1 %shard_map.58 = (bf16[128,1152]{1,0:T(8,128)(2,1)}, bf16[64,2688]{1,0:T(8,128)(2,1)S(1)}, bf16[64,2688]{1,0:T(8,128)(2,1)S(1)}) custom-call(s32[1]{0:T(128)} %bitcast.1.side_ref.refs_0_, bf16[128,3584]{1,0:T(8,128)(2,1)S(1)} %get-tuple-element.47.own_ref, bf16[128,3584]{1,0:T(8,128)(2,1)} %collective-permute-done.2.other_ref, bf16[9,128,256]{2,1,0:T(8,128)(2,1)S(1)} %copy-done), custom_call_target="tpu_custom_call" | custom-call | bytes 2424836 | tf_op jit(solution)/shard_map/pallas_call | solution.py:44
  24.4 1.9 %collective-permute-start.6 = (bf16[64,2688]{1,0:T(8,128)(2,1)S(1)}, bf16[64,2688]{1,0:T(8,128)(2,1)S(1)}, u32[]{:S(2)}, u32[]{:S(2)}) collective-permute-start(bf16[64,2688]{1,0:T(8,128)(2,1)S(1)} %get-tuple-element.52), channel_id=1, source_target_pairs={{1,3},{3,1},{5,7},{7,5},{9,11},{11,9},{13,15},{15,13},{17,19},{19,... | collective-permute-start | bytes 1032200 | tf_op jit(solution)/shard_map/ppermute | solution.py:20
  26.3 6.6 %collective-permute-done.6.refs_2_ = bf16[64,2688]{1,0:T(8,128)(2,1)S(1)} collective-permute-done((bf16[64,2688]{1,0:T(8,128)(2,1)S(1)}, bf16[64,2688]{1,0:T(8,128)(2,1)S(1)}, u32[]{:S(2)}, u32[]{:S(2)}) %collective-permute-start.6) | collective-permute-done | bytes 344096 | tf_op jit(solution)/shard_map/ppermute | solution.py:20
  33.0 1.9 %collective-permute-start.7 = (bf16[64,2944]{1,0:T(8,128)(2,1)S(1)}, bf16[64,2944]{1,0:T(8,128)(2,1)}, u32[]{:S(2)}, u32[]{:S(2)}) collective-permute-start(bf16[64,2944]{1,0:T(8,128)(2,1)S(1)} %shard_map.60.refs_1_), channel_id=1, source_target_pairs={{1,5},{3,7},{5,1},{7,3},{9,13},{11,15},{13,9},{15,11},{17,21},{19,... | collective-permute-start | bytes 1130504 | tf_op jit(solution)/shard_map/ppermute | solution.py:20
  35.0 2.0 %shard_map.57 = (bf16[192,1024]{1,0:T(8,128)(2,1)S(1)}, bf16[192,1024]{1,0:T(8,128)(2,1)}) custom-call(s32[1]{0:T(128)} %bitcast.1.side_ref.refs_0_, bf16[384,1024]{1,0:T(8,128)(2,1)S(1)} %get-tuple-element.44.own_ref, bf16[384,1024]{1,0:T(8,128)(2,1)} %collective-permute-done.other_ref), custom_call_target="tpu_custom_call" | custom-call | bytes 1572868 | tf_op jit(solution)/shard_map/pallas_call | solution.py:44
  37.7 1.3 collective-permute-start.3
  40.4 6.2 %collective-permute-done.7.refs_2_ = bf16[64,2944]{1,0:T(8,128)(2,1)} collective-permute-done((bf16[64,2944]{1,0:T(8,128)(2,1)S(1)}, bf16[64,2944]{1,0:T(8,128)(2,1)}, u32[]{:S(2)}, u32[]{:S(2)}) %collective-permute-start.7) | collective-permute-done | bytes 376864 | tf_op jit(solution)/shard_map/ppermute | solution.py:20
  46.5 1.8 %shard_map.61 = (bf16[64,2176]{1,0:T(8,128)(2,1)}, bf16[128,1024]{1,0:T(8,128)(2,1)S(1)}) custom-call(s32[1]{0:T(128)} %bitcast.1.side_ref.refs_0_, bf16[64,2944]{1,0:T(8,128)(2,1)S(1)} %shard_map.60.refs_1_, bf16[64,2944]{1,0:T(8,128)(2,1)} %collective-permute-done.7.refs_2_, bf16[9,128,256]{2,1,0:T(8,128)(2,1)S(1)} %copy-done), custom_call_target="tpu_custom_call" | custom-call | bytes 1343492 | tf_op jit(solution)/shard_map/pallas_call | solution.py:44
  48.3 3.0 %collective-permute-start.11 = (bf16[64,2176]{1,0:T(8,128)(2,1)}, bf16[64,2176]{1,0:T(8,128)(2,1)}, u32[]{:S(2)}, u32[]{:S(2)}) collective-permute-start(bf16[64,2176]{1,0:T(8,128)(2,1)} %get-tuple-element.56.refs_1_), channel_id=1, source_target_pairs={{1,13},{3,15},{5,9},{7,11},{9,5},{11,7},{13,1},{15,3},{17,29},{19,... | collective-permute-start | bytes 835592 | tf_op jit(solution)/shard_map/ppermute | solution.py:20
  53.8 1.9 %collective-permute-start.8 = (bf16[128,1024]{1,0:T(8,128)(2,1)}, bf16[128,1024]{1,0:T(8,128)(2,1)S(1)}, u32[]{:S(2)}, u32[]{:S(2)}) collective-permute-start(bf16[128,1024]{1,0:T(8,128)(2,1)} %copy-done.10), channel_id=1, source_target_pairs={{1,0},{3,2},{5,4},{7,6},{9,8},{11,10},{13,12},{15,14},{17,16},{19,... | collective-permute-start | bytes 786440 | tf_op jit(solution)/shard_map/ppermute | solution.py:25
  55.7 2.5 %collective-permute-start.9 = (bf16[128,1024]{1,0:T(8,128)(2,1)}, bf16[128,1024]{1,0:T(8,128)(2,1)S(1)}, u32[]{:S(2)}, u32[]{:S(2)}) collective-permute-start(bf16[128,1024]{1,0:T(8,128)(2,1)} %copy-done.10), channel_id=1, source_target_pairs={{3,0},{1,2},{7,4},{5,6},{11,8},{9,10},{15,12},{13,14},{19,16},{17,... | collective-permute-start | bytes 786440 | tf_op jit(solution)/shard_map/ppermute | solution.py:25
  59.4 2.7 %collective-permute-start.15 = (bf16[64,1536]{1,0:T(8,128)(2,1)S(1)}, bf16[64,1536]{1,0:T(8,128)(2,1)S(1)}, u32[]{:S(2)}, u32[]{:S(2)}) collective-permute-start(bf16[64,1536]{1,0:T(8,128)(2,1)S(1)} %get-tuple-element.60.refs_1_), channel_id=1, source_target_pairs={{1,17},{3,19},{5,21},{7,23},{9,25},{11,27},{13,29},{15,31},{17,1},... | collective-permute-start | bytes 589832 | tf_op jit(solution)/shard_map/ppermute | solution.py:20
  62.3 1.7 %collective-permute-done.9.far_ref = bf16[128,1024]{1,0:T(8,128)(2,1)S(1)} collective-permute-done((bf16[128,1024]{1,0:T(8,128)(2,1)}, bf16[128,1024]{1,0:T(8,128)(2,1)S(1)}, u32[]{:S(2)}, u32[]{:S(2)}) %collective-permute-start.9) | collective-permute-done | bytes 262176 | tf_op jit(solution)/shard_map/ppermute | solution.py:25
  65.7 6.8 %collective-permute-start.12 = (bf16[128,896]{1,0:T(8,128)(2,1)S(1)}, bf16[128,896]{1,0:T(8,128)(2,1)S(1)}, u32[]{:S(2)}, u32[]{:S(2)}) collective-permute-start(bf16[128,896]{1,0:T(8,128)(2,1)S(1)} %get-tuple-element.57), channel_id=1, source_target_pairs={{1,0},{3,2},{5,4},{7,6},{9,8},{11,10},{13,12},{15,14},{17,16},{19,... | collective-permute-start | bytes 688136 | tf_op jit(solution)/shard_map/ppermute | solution.py:25
  72.5 4.1 %collective-permute-start.13 = (bf16[128,896]{1,0:T(8,128)(2,1)S(1)}, bf16[128,896]{1,0:T(8,128)(2,1)S(1)}, u32[]{:S(2)}, u32[]{:S(2)}) collective-permute-start(bf16[128,896]{1,0:T(8,128)(2,1)S(1)} %get-tuple-element.57), channel_id=1, source_target_pairs={{3,0},{1,2},{7,4},{5,6},{11,8},{9,10},{15,12},{13,14},{19,16},{17,... | collective-permute-start | bytes 688136 | tf_op jit(solution)/shard_map/ppermute | solution.py:25
  76.7 3.2 %collective-permute-start.19 = (bf16[64,1024]{1,0:T(8,128)(2,1)S(1)}, bf16[64,1024]{1,0:T(8,128)(2,1)S(1)}, u32[]{:S(2)}, u32[]{:S(2)}) collective-permute-start(bf16[64,1024]{1,0:T(8,128)(2,1)S(1)} %get-tuple-element.64.refs_1_), channel_id=1, source_target_pairs={{1,33},{3,35},{5,37},{7,39},{9,41},{11,43},{13,45},{15,47},{17,49}... | collective-permute-start | bytes 393224 | tf_op jit(solution)/shard_map/ppermute | solution.py:20
  80.6 4.1 %collective-permute-done.19.refs_2_ = bf16[64,1024]{1,0:T(8,128)(2,1)S(1)} collective-permute-done((bf16[64,1024]{1,0:T(8,128)(2,1)S(1)}, bf16[64,1024]{1,0:T(8,128)(2,1)S(1)}, u32[]{:S(2)}, u32[]{:S(2)}) %collective-permute-start.19) | collective-permute-done | bytes 131104 | tf_op jit(solution)/shard_map/ppermute | solution.py:20
  84.7 4.0 %collective-permute-start.23 = (bf16[64,640]{1,0:T(8,128)(2,1)S(1)}, bf16[64,640]{1,0:T(8,128)(2,1)S(1)}, u32[]{:S(2)}, u32[]{:S(2)}) collective-permute-start(bf16[64,640]{1,0:T(8,128)(2,1)S(1)} %get-tuple-element.68.refs_1_), channel_id=1, source_target_pairs={{1,97},{3,99},{5,101},{7,103},{9,105},{11,107},{13,109},{15,111},{... | collective-permute-start | bytes 245768 | tf_op jit(solution)/shard_map/ppermute | solution.py:20
  93.6 3.1 %collective-permute-start.30 = (bf16[64,384]{1,0:T(8,128)(2,1)S(1)}, bf16[64,384]{1,0:T(8,128)(2,1)S(1)}, u32[]{:S(2)}, u32[]{:S(2)}) collective-permute-start(bf16[64,384]{1,0:T(8,128)(2,1)S(1)} %get-tuple-element.72.refs_1_), channel_id=1, source_target_pairs={{1,129},{3,131},{5,133},{7,135},{9,137},{11,139},{13,141},{15,143}... | collective-permute-start | bytes 147464 | tf_op jit(solution)/shard_map/ppermute | solution.py:20
  98.7 4.2 %collective-permute-start.34 = (bf16[64,256]{1,0:T(8,128)(2,1)S(1)}, bf16[64,256]{1,0:T(8,128)(2,1)S(1)}, u32[]{:S(2)}, u32[]{:S(2)}) collective-permute-start(bf16[64,256]{1,0:T(8,128)(2,1)S(1)} %get-tuple-element.76), channel_id=1, source_target_pairs={{1,385},{3,387},{5,389},{7,391},{9,393},{11,395},{13,397},{15,399}... | collective-permute-start | bytes 98312 | tf_op jit(solution)/shard_map/ppermute | solution.py:20
  102.9 1.8 %collective-permute-done.34 = bf16[64,256]{1,0:T(8,128)(2,1)S(1)} collective-permute-done((bf16[64,256]{1,0:T(8,128)(2,1)S(1)}, bf16[64,256]{1,0:T(8,128)(2,1)S(1)}, u32[]{:S(2)}, u32[]{:S(2)}) %collective-permute-start.34) | collective-permute-done | bytes 32800 | tf_op jit(solution)/shard_map/ppermute | solution.py:20
  110.9 1.4 collective-permute-start.31
  115.9 1.7 %collective-permute-start.35 = (bf16[128,256]{1,0:T(8,128)(2,1)S(1)}, bf16[128,256]{1,0:T(8,128)(2,1)S(1)}, u32[]{:S(2)}, u32[]{:S(2)}) collective-permute-start(bf16[128,256]{1,0:T(8,128)(2,1)S(1)} %constant_dynamic-update-slice_fusion), channel_id=1, source_target_pairs={{1,0},{3,2},{5,4},{7,6},{9,8},{11,10},{13,12},{15,14},{17,16},{19,... | collective-permute-start | bytes 196616 | tf_op jit(solution)/shard_map/ppermute | solution.py:25
  120.6 9.2 %collective-permute-start.36 = (bf16[128,256]{1,0:T(8,128)(2,1)S(1)}, bf16[128,256]{1,0:T(8,128)(2,1)S(1)}, u32[]{:S(2)}, u32[]{:S(2)}) collective-permute-start(bf16[128,256]{1,0:T(8,128)(2,1)S(1)} %constant_dynamic-update-slice_fusion), channel_id=1, source_target_pairs={{3,0},{1,2},{7,4},{5,6},{11,8},{9,10},{15,12},{13,14},{19,16},{17,... | collective-permute-start | bytes 196616 | tf_op jit(solution)/shard_map/ppermute | solution.py:25
  138.3 1.3 shard_map.71.refs_1_
  139.7 8.5 %collective-permute-done.38.refs_5_ = bf16[2,192,128]{2,1,0:T(8,128)(2,1)S(1)} collective-permute-done((bf16[2,192,128]{2,1,0:T(8,128)(2,1)S(1)}, bf16[2,192,128]{2,1,0:T(8,128)(2,1)S(1)}, u32[]{:S(2)}, u32[]{:S(2)}) %collective-permute-start.38) | collective-permute-done | bytes 98336 | tf_op jit(solution)/shard_map/ppermute | solution.py:25
  148.2 4.1 %collective-permute-done.39.refs_6_ = bf16[2,192,128]{2,1,0:T(8,128)(2,1)S(1)} collective-permute-done((bf16[2,192,128]{2,1,0:T(8,128)(2,1)S(1)}, bf16[2,192,128]{2,1,0:T(8,128)(2,1)S(1)}, u32[]{:S(2)}, u32[]{:S(2)}) %collective-permute-start.39) | collective-permute-done | bytes 98336 | tf_op jit(solution)/shard_map/ppermute | solution.py:25
  152.3 1.8 %shard_map.75 = f32[512,384]{1,0:T(8,128)} custom-call(s32[2]{0:T(128)S(1)} %pad_add_fusion.refs_0_, f32[512,384]{1,0:T(8,128)S(1)} %shard_map.71.refs_1_, bf16[9,512,128]{2,1,0:T(8,128)(2,1)S(1)} %copy-done.2, bf16[2,192,128]{2,1,0:T(8,128)(2,1)S(1)} %pad_maximum_fusion.refs_3_, bf16[2,192,128]{2,1,0:T(8,128)(2,1)S(1)} %collective-permute-done.37.refs_4_, ...), custom_call_target="tpu_custom_call" | custom-call | bytes 2359304 | tf_op jit(solution)/shard_map/pallas_call | solution.py:44
  (110 shorter events, 42.9 us)
Async XLA Ops:
  6.2 16.2 %collective-permute-start.2 = (bf16[128,3584]{1,0:T(8,128)(2,1)S(1)}, bf16[128,3584]{1,0:T(8,128)(2,1)}, u32[]{:S(2)}, u32[]{:S(2)}) collective-permute-start(bf16[128,3584]{1,0:T(8,128)(2,1)S(1)} %get-tuple-element.47.own_ref), channel_id=1, source_target_pairs={{0,1},{2,3},{4,5},{6,7},{8,9},{10,11},{12,13},{14,15},{16,17},{18,... | collective-permute-start | bytes 2752520 | tf_op jit(solution)/shard_map/ppermute | solution.py:25
  19.2 15.8 %collective-permute-start = (bf16[384,1024]{1,0:T(8,128)(2,1)S(1)}, bf16[384,1024]{1,0:T(8,128)(2,1)}, u32[]{:S(2)}, u32[]{:S(2)}) collective-permute-start(bf16[384,1024]{1,0:T(8,128)(2,1)S(1)} %get-tuple-element.44.own_ref), channel_id=1, source_target_pairs={{1,0},{3,2},{5,4},{7,6},{9,8},{11,10},{13,12},{15,14},{17,16},{19,... | collective-permute-start | bytes 2359304 | tf_op jit(solution)/shard_map/ppermute | solution.py:25
  24.4 8.5 %collective-permute-start.6 = (bf16[64,2688]{1,0:T(8,128)(2,1)S(1)}, bf16[64,2688]{1,0:T(8,128)(2,1)S(1)}, u32[]{:S(2)}, u32[]{:S(2)}) collective-permute-start(bf16[64,2688]{1,0:T(8,128)(2,1)S(1)} %get-tuple-element.52), channel_id=1, source_target_pairs={{1,3},{3,1},{5,7},{7,5},{9,11},{11,9},{13,15},{15,13},{17,19},{19,... | collective-permute-start | bytes 1032200 | tf_op jit(solution)/shard_map/ppermute | solution.py:20
  33.0 13.5 %collective-permute-start.7 = (bf16[64,2944]{1,0:T(8,128)(2,1)S(1)}, bf16[64,2944]{1,0:T(8,128)(2,1)}, u32[]{:S(2)}, u32[]{:S(2)}) collective-permute-start(bf16[64,2944]{1,0:T(8,128)(2,1)S(1)} %shard_map.60.refs_1_), channel_id=1, source_target_pairs={{1,5},{3,7},{5,1},{7,3},{9,13},{11,15},{13,9},{15,11},{17,21},{19,... | collective-permute-start | bytes 1130504 | tf_op jit(solution)/shard_map/ppermute | solution.py:20
  37.0 14.4 %collective-permute-start.1 = (bf16[192,1024]{1,0:T(8,128)(2,1)}, bf16[192,1024]{1,0:T(8,128)(2,1)S(1)}, u32[]{:S(2)}, u32[]{:S(2)}) collective-permute-start(bf16[192,1024]{1,0:T(8,128)(2,1)} %get-tuple-element.46), channel_id=1, source_target_pairs={{0,2},{2,0},{4,6},{6,4},{8,10},{10,8},{12,14},{14,12},{16,18},{18,... | collective-permute-start | bytes 1179656 | tf_op jit(solution)/shard_map/ppermute | solution.py:20
  37.7 13.7 %collective-permute-start.3 = (bf16[128,1152]{1,0:T(8,128)(2,1)}, bf16[128,1152]{1,0:T(8,128)(2,1)S(1)}, u32[]{:S(2)}, u32[]{:S(2)}) collective-permute-start(bf16[128,1152]{1,0:T(8,128)(2,1)} %get-tuple-element.48), channel_id=1, source_target_pairs={{1,0},{3,2},{5,4},{7,6},{9,8},{11,10},{13,12},{15,14},{17,16},{19,... | collective-permute-start | bytes 884744 | tf_op jit(solution)/shard_map/ppermute | solution.py:25
  39.0 12.4 %collective-permute-start.4 = (bf16[128,1152]{1,0:T(8,128)(2,1)}, bf16[128,1152]{1,0:T(8,128)(2,1)S(1)}, u32[]{:S(2)}, u32[]{:S(2)}) collective-permute-start(bf16[128,1152]{1,0:T(8,128)(2,1)} %get-tuple-element.48), channel_id=1, source_target_pairs={{3,0},{1,2},{7,4},{5,6},{11,8},{9,10},{15,12},{13,14},{19,16},{17,... | collective-permute-start | bytes 884744 | tf_op jit(solution)/shard_map/ppermute | solution.py:25
  48.3 10.0 %collective-permute-start.11 = (bf16[64,2176]{1,0:T(8,128)(2,1)}, bf16[64,2176]{1,0:T(8,128)(2,1)}, u32[]{:S(2)}, u32[]{:S(2)}) collective-permute-start(bf16[64,2176]{1,0:T(8,128)(2,1)} %get-tuple-element.56.refs_1_), channel_id=1, source_target_pairs={{1,13},{3,15},{5,9},{7,11},{9,5},{11,7},{13,1},{15,3},{17,29},{19,... | collective-permute-start | bytes 835592 | tf_op jit(solution)/shard_map/ppermute | solution.py:20
  53.0 9.2 %collective-permute-start.5 = (bf16[192,896]{1,0:T(8,128)(2,1)S(1)}, bf16[192,896]{1,0:T(8,128)(2,1)S(1)}, u32[]{:S(2)}, u32[]{:S(2)}) collective-permute-start(bf16[192,896]{1,0:T(8,128)(2,1)S(1)} %get-tuple-element.50.own_ref), channel_id=1, source_target_pairs={{0,4},{2,6},{4,0},{6,2},{8,12},{10,14},{12,8},{14,10},{16,20},{18,... | collective-permute-start | bytes 1032200 | tf_op jit(solution)/shard_map/ppermute | solution.py:20
  53.8 8.5 %collective-permute-start.8 = (bf16[128,1024]{1,0:T(8,128)(2,1)}, bf16[128,1024]{1,0:T(8,128)(2,1)S(1)}, u32[]{:S(2)}, u32[]{:S(2)}) collective-permute-start(bf16[128,1024]{1,0:T(8,128)(2,1)} %copy-done.10), channel_id=1, source_target_pairs={{1,0},{3,2},{5,4},{7,6},{9,8},{11,10},{13,12},{15,14},{17,16},{19,... | collective-permute-start | bytes 786440 | tf_op jit(solution)/shard_map/ppermute | solution.py:25
  55.7 8.3 %collective-permute-start.9 = (bf16[128,1024]{1,0:T(8,128)(2,1)}, bf16[128,1024]{1,0:T(8,128)(2,1)S(1)}, u32[]{:S(2)}, u32[]{:S(2)}) collective-permute-start(bf16[128,1024]{1,0:T(8,128)(2,1)} %copy-done.10), channel_id=1, source_target_pairs={{3,0},{1,2},{7,4},{5,6},{11,8},{9,10},{15,12},{13,14},{19,16},{17,... | collective-permute-start | bytes 786440 | tf_op jit(solution)/shard_map/ppermute | solution.py:25
  59.4 17.2 %collective-permute-start.15 = (bf16[64,1536]{1,0:T(8,128)(2,1)S(1)}, bf16[64,1536]{1,0:T(8,128)(2,1)S(1)}, u32[]{:S(2)}, u32[]{:S(2)}) collective-permute-start(bf16[64,1536]{1,0:T(8,128)(2,1)S(1)} %get-tuple-element.60.refs_1_), channel_id=1, source_target_pairs={{1,17},{3,19},{5,21},{7,23},{9,25},{11,27},{13,29},{15,31},{17,1},... | collective-permute-start | bytes 589832 | tf_op jit(solution)/shard_map/ppermute | solution.py:20
  65.0 27.0 %collective-permute-start.10 = (bf16[192,768]{1,0:T(8,128)(2,1)S(1)}, bf16[192,768]{1,0:T(8,128)(2,1)S(1)}, u32[]{:S(2)}, u32[]{:S(2)}) collective-permute-start(bf16[192,768]{1,0:T(8,128)(2,1)S(1)} %get-tuple-element.55.own_ref), channel_id=1, source_target_pairs={{0,12},{2,14},{4,8},{6,10},{8,4},{10,6},{12,0},{14,2},{16,28},{18,... | collective-permute-start | bytes 884744 | tf_op jit(solution)/shard_map/ppermute | solution.py:20
  65.7 24.9 %collective-permute-start.12 = (bf16[128,896]{1,0:T(8,128)(2,1)S(1)}, bf16[128,896]{1,0:T(8,128)(2,1)S(1)}, u32[]{:S(2)}, u32[]{:S(2)}) collective-permute-start(bf16[128,896]{1,0:T(8,128)(2,1)S(1)} %get-tuple-element.57), channel_id=1, source_target_pairs={{1,0},{3,2},{5,4},{7,6},{9,8},{11,10},{13,12},{15,14},{17,16},{19,... | collective-permute-start | bytes 688136 | tf_op jit(solution)/shard_map/ppermute | solution.py:25
  72.5 19.5 %collective-permute-start.13 = (bf16[128,896]{1,0:T(8,128)(2,1)S(1)}, bf16[128,896]{1,0:T(8,128)(2,1)S(1)}, u32[]{:S(2)}, u32[]{:S(2)}) collective-permute-start(bf16[128,896]{1,0:T(8,128)(2,1)S(1)} %get-tuple-element.57), channel_id=1, source_target_pairs={{3,0},{1,2},{7,4},{5,6},{11,8},{9,10},{15,12},{13,14},{19,16},{17,... | collective-permute-start | bytes 688136 | tf_op jit(solution)/shard_map/ppermute | solution.py:25
  76.7 8.0 %collective-permute-start.19 = (bf16[64,1024]{1,0:T(8,128)(2,1)S(1)}, bf16[64,1024]{1,0:T(8,128)(2,1)S(1)}, u32[]{:S(2)}, u32[]{:S(2)}) collective-permute-start(bf16[64,1024]{1,0:T(8,128)(2,1)S(1)} %get-tuple-element.64.refs_1_), channel_id=1, source_target_pairs={{1,33},{3,35},{5,37},{7,39},{9,41},{11,43},{13,45},{15,47},{17,49}... | collective-permute-start | bytes 393224 | tf_op jit(solution)/shard_map/ppermute | solution.py:20
  84.7 8.9 %collective-permute-start.23 = (bf16[64,640]{1,0:T(8,128)(2,1)S(1)}, bf16[64,640]{1,0:T(8,128)(2,1)S(1)}, u32[]{:S(2)}, u32[]{:S(2)}) collective-permute-start(bf16[64,640]{1,0:T(8,128)(2,1)S(1)} %get-tuple-element.68.refs_1_), channel_id=1, source_target_pairs={{1,97},{3,99},{5,101},{7,103},{9,105},{11,107},{13,109},{15,111},{... | collective-permute-start | bytes 245768 | tf_op jit(solution)/shard_map/ppermute | solution.py:20
  89.3 16.7 %collective-permute-start.16 = (bf16[128,768]{1,0:T(8,128)(2,1)S(1)}, bf16[128,768]{1,0:T(8,128)(2,1)S(1)}, u32[]{:S(2)}, u32[]{:S(2)}) collective-permute-start(bf16[128,768]{1,0:T(8,128)(2,1)S(1)} %get-tuple-element.61), channel_id=1, source_target_pairs={{1,0},{3,2},{5,4},{7,6},{9,8},{11,10},{13,12},{15,14},{17,16},{19,... | collective-permute-start | bytes 589832 | tf_op jit(solution)/shard_map/ppermute | solution.py:25
  90.6 16.7 %collective-permute-start.17 = (bf16[128,768]{1,0:T(8,128)(2,1)S(1)}, bf16[128,768]{1,0:T(8,128)(2,1)S(1)}, u32[]{:S(2)}, u32[]{:S(2)}) collective-permute-start(bf16[128,768]{1,0:T(8,128)(2,1)S(1)} %get-tuple-element.61), channel_id=1, source_target_pairs={{3,0},{1,2},{7,4},{5,6},{11,8},{9,10},{15,12},{13,14},{19,16},{17,... | collective-permute-start | bytes 589832 | tf_op jit(solution)/shard_map/ppermute | solution.py:25
  92.9 15.7 %collective-permute-start.14 = (bf16[192,640]{1,0:T(8,128)(2,1)S(1)}, bf16[192,640]{1,0:T(8,128)(2,1)S(1)}, u32[]{:S(2)}, u32[]{:S(2)}) collective-permute-start(bf16[192,640]{1,0:T(8,128)(2,1)S(1)} %get-tuple-element.59.own_ref), channel_id=1, source_target_pairs={{0,16},{2,18},{4,20},{6,22},{8,24},{10,26},{12,28},{14,30},{16,0},... | collective-permute-start | bytes 737288 | tf_op jit(solution)/shard_map/ppermute | solution.py:20
  97.4 13.5 %collective-permute-start.20 = (bf16[128,640]{1,0:T(8,128)(2,1)S(1)}, bf16[128,640]{1,0:T(8,128)(2,1)S(1)}, u32[]{:S(2)}, u32[]{:S(2)}) collective-permute-start(bf16[128,640]{1,0:T(8,128)(2,1)S(1)} %get-tuple-element.65), channel_id=1, source_target_pairs={{1,0},{3,2},{5,4},{7,6},{9,8},{11,10},{13,12},{15,14},{17,16},{19,... | collective-permute-start | bytes 491528 | tf_op jit(solution)/shard_map/ppermute | solution.py:25
  106.0 9.9 %collective-permute-start.24 = (bf16[128,512]{1,0:T(8,128)(2,1)S(1)}, bf16[128,512]{1,0:T(8,128)(2,1)S(1)}, u32[]{:S(2)}, u32[]{:S(2)}) collective-permute-start(bf16[128,512]{1,0:T(8,128)(2,1)S(1)} %get-tuple-element.69), channel_id=1, source_target_pairs={{1,0},{3,2},{5,4},{7,6},{9,8},{11,10},{13,12},{15,14},{17,16},{19,... | collective-permute-start | bytes 393224 | tf_op jit(solution)/shard_map/ppermute | solution.py:25
  107.4 10.3 %collective-permute-start.25 = (bf16[128,512]{1,0:T(8,128)(2,1)S(1)}, bf16[128,512]{1,0:T(8,128)(2,1)S(1)}, u32[]{:S(2)}, u32[]{:S(2)}) collective-permute-start(bf16[128,512]{1,0:T(8,128)(2,1)S(1)} %get-tuple-element.69), channel_id=1, source_target_pairs={{3,0},{1,2},{7,4},{5,6},{11,8},{9,10},{15,12},{13,14},{19,16},{17,... | collective-permute-start | bytes 393224 | tf_op jit(solution)/shard_map/ppermute | solution.py:25
  110.9 9.7 %collective-permute-start.31 = (bf16[128,384]{1,0:T(8,128)(2,1)S(1)}, bf16[128,384]{1,0:T(8,128)(2,1)S(1)}, u32[]{:S(2)}, u32[]{:S(2)}) collective-permute-start(bf16[128,384]{1,0:T(8,128)(2,1)S(1)} %get-tuple-element.73), channel_id=1, source_target_pairs={{1,0},{3,2},{5,4},{7,6},{9,8},{11,10},{13,12},{15,14},{17,16},{19,... | collective-permute-start | bytes 294920 | tf_op jit(solution)/shard_map/ppermute | solution.py:25
  112.4 17.5 %collective-permute-start.32 = (bf16[128,384]{1,0:T(8,128)(2,1)S(1)}, bf16[128,384]{1,0:T(8,128)(2,1)S(1)}, u32[]{:S(2)}, u32[]{:S(2)}) collective-permute-start(bf16[128,384]{1,0:T(8,128)(2,1)S(1)} %get-tuple-element.73), channel_id=1, source_target_pairs={{3,0},{1,2},{7,4},{5,6},{11,8},{9,10},{15,12},{13,14},{19,16},{17,... | collective-permute-start | bytes 294920 | tf_op jit(solution)/shard_map/ppermute | solution.py:25
  115.9 17.4 %collective-permute-start.35 = (bf16[128,256]{1,0:T(8,128)(2,1)S(1)}, bf16[128,256]{1,0:T(8,128)(2,1)S(1)}, u32[]{:S(2)}, u32[]{:S(2)}) collective-permute-start(bf16[128,256]{1,0:T(8,128)(2,1)S(1)} %constant_dynamic-update-slice_fusion), channel_id=1, source_target_pairs={{1,0},{3,2},{5,4},{7,6},{9,8},{11,10},{13,12},{15,14},{17,16},{19,... | collective-permute-start | bytes 196616 | tf_op jit(solution)/shard_map/ppermute | solution.py:25
  119.2 17.8 %collective-permute-start.26 = (bf16[6,192,128]{2,1,0:T(8,128)(2,1)}, bf16[6,192,128]{2,1,0:T(8,128)(2,1)S(1)}, u32[]{:S(2)}, u32[]{:S(2)}) collective-permute-start(bf16[6,192,128]{2,1,0:T(8,128)(2,1)} %get-tuple-element.79), channel_id=1, source_target_pairs={{0,2},{2,0},{4,6},{6,4},{8,10},{10,8},{12,14},{14,12},{16,18},{18,... | collective-permute-start | bytes 884744 | tf_op jit(solution)/shard_map/ppermute | solution.py:20
  119.9 11.3 %collective-permute-start.29 = (bf16[192,256]{1,0:T(8,128)(2,1)S(1)}, bf16[192,256]{1,0:T(8,128)(2,1)S(1)}, u32[]{:S(2)}, u32[]{:S(2)}) collective-permute-start(bf16[192,256]{1,0:T(8,128)(2,1)S(1)} %get-tuple-element.71.own_ref), channel_id=1, source_target_pairs={{0,128},{2,130},{4,132},{6,134},{8,136},{10,138},{12,140},{14,142}... | collective-permute-start | bytes 294920 | tf_op jit(solution)/shard_map/ppermute | solution.py:20
  120.6 13.5 %collective-permute-start.36 = (bf16[128,256]{1,0:T(8,128)(2,1)S(1)}, bf16[128,256]{1,0:T(8,128)(2,1)S(1)}, u32[]{:S(2)}, u32[]{:S(2)}) collective-permute-start(bf16[128,256]{1,0:T(8,128)(2,1)S(1)} %constant_dynamic-update-slice_fusion), channel_id=1, source_target_pairs={{3,0},{1,2},{7,4},{5,6},{11,8},{9,10},{15,12},{13,14},{19,16},{17,... | collective-permute-start | bytes 196616 | tf_op jit(solution)/shard_map/ppermute | solution.py:25
  129.9 8.5 %collective-permute-start.28 = (bf16[6,192,128]{2,1,0:T(8,128)(2,1)}, bf16[6,192,128]{2,1,0:T(8,128)(2,1)S(1)}, u32[]{:S(2)}, u32[]{:S(2)}) collective-permute-start(bf16[6,192,128]{2,1,0:T(8,128)(2,1)} %get-tuple-element.79), channel_id=1, source_target_pairs={{2,1},{0,3},{6,5},{4,7},{10,9},{8,11},{14,13},{12,15},{18,17},{16,... | collective-permute-start | bytes 884744 | tf_op jit(solution)/shard_map/ppermute | solution.py:25
  135.6 12.6 %collective-permute-start.38 = (bf16[2,192,128]{2,1,0:T(8,128)(2,1)S(1)}, bf16[2,192,128]{2,1,0:T(8,128)(2,1)S(1)}, u32[]{:S(2)}, u32[]{:S(2)}) collective-permute-start(bf16[2,192,128]{2,1,0:T(8,128)(2,1)S(1)} %pad_maximum_fusion.refs_3_), channel_id=1, source_target_pairs={{0,1},{2,3},{4,5},{6,7},{8,9},{10,11},{12,13},{14,15},{16,17},{18,... | collective-permute-start | bytes 294920 | tf_op jit(solution)/shard_map/ppermute | solution.py:25
  136.9 15.4 %collective-permute-start.39 = (bf16[2,192,128]{2,1,0:T(8,128)(2,1)S(1)}, bf16[2,192,128]{2,1,0:T(8,128)(2,1)S(1)}, u32[]{:S(2)}, u32[]{:S(2)}) collective-permute-start(bf16[2,192,128]{2,1,0:T(8,128)(2,1)S(1)} %pad_maximum_fusion.refs_3_), channel_id=1, source_target_pairs={{2,1},{0,3},{6,5},{4,7},{10,9},{8,11},{14,13},{12,15},{18,17},{16,... | collective-permute-start | bytes 294920 | tf_op jit(solution)/shard_map/ppermute | solution.py:25
  (19 other events, 120.1 us)

commit v3 on v2

v3 whole, which is shorter than its diff:
```python
import jax
import jax.numpy as jnp
from jax import lax
from jax.experimental import pallas as pl
from jax.experimental.pallas import tpu as pltpu
from jax.sharding import PartitionSpec as P

BF = jnp.bfloat16
F32 = jnp.float32
AXIS = "seq"
MASKS = {3: 12, 6: 96, 8: 384}


def mask_of(level):
    return MASKS.get(level, 1 << level)


def swap(value, mask, core):
    pairs = [(d, d ^ mask) for d in range(lax.axis_size(AXIS)) if d & 1 == core]
    return lax.ppermute(value, AXIS, pairs)


def to_core(value, core, mask=1):
    pairs = [(d ^ mask, d) for d in range(lax.axis_size(AXIS)) if d & 1 == core]
    return lax.ppermute(value, AXIS, pairs)


def dot(a, b, dims):
    return lax.dot_general(a, b, (dims, ((), ())), preferred_element_type=F32)


NN = ((1,), (0,))
NT = ((1,), (1,))
TN = ((0,), (0,))


SMEM = pl.BlockSpec(memory_space=pltpu.SMEM)
VMEM = pl.BlockSpec(memory_space=pltpu.VMEM)
HBM = pl.BlockSpec(memory_space=pltpu.HBM)
ANY = pl.BlockSpec(memory_space=pl.ANY)


def call(body, outs, args, specs, scratch=(), grid=(1,), out_specs=None, limit=40):
    return pl.pallas_call(
        body,
        out_shape=outs,
        grid=grid,
        in_specs=specs,
        out_specs=out_specs or [VMEM] * len(outs),
        scratch_shapes=list(scratch),
        compiler_params=pltpu.CompilerParams(vmem_limit_bytes=limit * 2**20),
        cost_estimate=pl.CostEstimate(
            flops=0, bytes_accessed=sum(a.size * a.dtype.itemsize for a in args), transcendentals=0
        ),
    )(*args)


def sds(shape, dtype):
    return jax.ShapeDtypeStruct(shape, dtype)


def like(array):
    return pltpu.VMEM(array.shape, array.dtype)


def rows_of(part, count):
    return pl.ds(pl.multiple_of(part * count, count), count)


def front_body(
    inverse_hbm, right_hbm, project_hbm, spread_hbm, static_ref, state_ref, sums_ref,
    inverse, right, project, spread, project_sems, spread_sems, inverse_sem, right_sem,
):
    levels = project.shape[0]
    copies = {}
    for level in range(1, levels):
        if level < levels - 1:
            copies["s", level] = pltpu.make_async_copy(spread_hbm.at[level], spread.at[level], spread_sems.at[level])
            copies["s", level].start()
        if level > 1:
            copies["p", level] = pltpu.make_async_copy(project_hbm.at[level], project.at[level], project_sems.at[level])
            copies["p", level].start()
    late = [
        pltpu.make_async_copy(inverse_hbm.at[0], inverse, inverse_sem),
        pltpu.make_async_copy(right_hbm, right, right_sem),
        pltpu.make_async_copy(project_hbm.at[0], project.at[0], project_sems.at[0]),
    ]
    for copy in late:
        copy.start()
    for copy in copies.values():
        copy.wait()
    at = 0
    for low in range(1, levels - 1):
        block = [dot(spread[low], project[high], TN) for high in range(low + 1, levels)]
        for part in block:
            static_ref[:, at : at + part.shape[1]] = part.astype(BF)
            at += part.shape[1]
    for copy in late:
        copy.wait()
    state = dot(inverse[...], right[...], NN)
    state_ref[...] = state
    sums_ref[...] = dot(project[0], state.astype(BF), TN).astype(BF)


def first_body(state_ref, stacked_ref, capacity_ref, spread_ref, project_ref, first_ref, sums_ref):
    coefficients = dot(capacity_ref[0], stacked_ref[...], NN).astype(BF)
    first_ref[...] = coefficients
    rounded = (state_ref[...] - dot(spread_ref[0], coefficients, NN)).astype(BF)
    for level in range(1, project_ref.shape[0]):
        block = dot(rounded, project_ref[level], TN)
        rank = block.shape[1]
        sums_ref[:, (level - 1) * rank : level * rank] = block.astype(BF)


def fetch(pairs, sems):
    copies = [pltpu.make_async_copy(a, b, sems.at[i]) for i, (a, b) in enumerate(pairs)]
    for copy in copies:
        copy.start()
    for copy in copies:
        copy.wait()


def merge_body(bits_ref, own_any, other_any, keep_ref, send_ref, own, other, sems):
    @pl.when(bits_ref[0] == 0)
    def _():
        fetch([(own_any, own), (other_any, other)], sems)
        side = bits_ref[1]
        count = keep_ref.shape[0]
        for part, out_ref in ((side, keep_ref), (1 - side, send_ref)):
            rows = rows_of(part, count)
            out_ref[...] = (own[rows, :].astype(F32) + other[rows, :].astype(F32)).astype(BF)


def cut_body(bits_ref, own_any, other_any, capacity_ref, first_ref, keep_ref, send_ref, own, other, sems):
    @pl.when(bits_ref[0] == 1)
    def _():
        fetch([(own_any, own), (other_any, other)], sems)
        side = bits_ref[1]
        width = first_ref.shape[1] - capacity_ref.shape[2]
        first_ref[:, :width] = (own[:, :width].astype(F32) + other[:, :width].astype(F32)).astype(BF)
        first_ref[:, width:] = capacity_ref[0]
        count = keep_ref.shape[0]
        for part, out_ref in ((side, keep_ref), (1 - side, send_ref)):
            rows = rows_of(part, count)
            total = own[rows, width:].astype(F32) + other[rows, width:].astype(F32)
            out_ref[...] = total.astype(BF)


def static_body(bits_ref, own_any, other_any, capacity_ref, *refs, cut, width, outs):
    out_refs, (own, other, sems) = refs[:outs], refs[outs:]

    @pl.when(bits_ref[0] == 1)
    def _():
        fetch([(own_any, own), (other_any, other)], sems)
        count = own.shape[0]
        inner = capacity_ref.shape[2]
        if cut:
            out_refs[0][:count, :] = own[:, :cut]
            out_refs[0][count:, :] = other[:, :cut]
        if outs == 1 and cut:
            return
        message_ref = out_refs[-1]
        if width:
            total = own[:, cut : cut + width].astype(F32) + other[:, cut : cut + width].astype(F32)
            message_ref[:, :width] = total.astype(BF)
        message_ref[:, width : width + inner] = capacity_ref[0, rows_of(bits_ref[1], count), :]
        if own.shape[1] > cut + width:
            rest = own[:, cut + width :].astype(F32) + other[:, cut + width :].astype(F32)
            message_ref[:, width + inner :] = rest.astype(BF)


def step_body(bits_ref, own_ref, other_ref, near_ref, far_ref, *out_refs, level):
    rank = near_ref.shape[0]
    width = own_ref.shape[1] - rank

    @pl.when(bits_ref[0] == 0)
    def _():
        lower = bits_ref[level] == 0
        own, other = own_ref[:, :rank], other_ref[:, :rank]
        stacked = jnp.concatenate([jnp.where(lower, own, other), jnp.where(lower, other, own)], 1)
        capacity = jnp.concatenate([near_ref[:, width:], far_ref[:, width:]], 0)
        both = dot(stacked, capacity, NT).astype(BF)
        if level == 1:
            out_refs[0][...] = both
        else:
            first = bits_ref[1] == 0
            part = rank // 2
            near, far = both[:, :part], both[:, rank : rank + part]
            out_refs[0][...] = jnp.concatenate([jnp.where(first, near, far), jnp.where(first, far, near)], 1)
        if width:
            total = own_ref[:, rank:].astype(F32) + other_ref[:, rank:].astype(F32)
            static = jnp.concatenate([near_ref[:, :width], far_ref[:, :width]], 0)
            out_refs[1][...] = (total - dot(both, static, NN)).astype(BF)


def spread_body(bits_ref, state_ref, *refs, count, zero):
    spreads, (near0_ref, far0_ref, near1_ref, far1_ref), rest = refs[:count], refs[count : count + 4], refs[count + 4 :]
    out_ref = rest[-1]
    zero_core = bits_ref[0] == 0
    first = bits_ref[1] == 0
    total = state_ref[...]
    if zero:
        total = total - dot(rest[0][0], rest[1][...], NN)
    for at in range(0, count, 2):
        left, right = [], []
        for index in range(at, min(at + 2, count)):
            near = jnp.where(zero_core, near0_ref[index], near1_ref[index])
            far = jnp.where(zero_core, far0_ref[index], far1_ref[index])
            left.append(spreads[index][0])
            right.append(jnp.concatenate([jnp.where(first, near, far), jnp.where(first, far, near)], 0))
        total = total - dot(jnp.concatenate(left, 1), jnp.concatenate(right, 1), NT)
    out_ref[...] = total


def on_device(right_side, leaf_inverse, project_rows, spread_rows, capacity):
    levels, samples, rank = project_rows.shape
    columns = right_side.shape[1]
    inner = capacity.shape[2]
    size = lax.axis_size(AXIS)
    device = lax.axis_index(AXIS)
    bits = (device >> jnp.arange(levels, dtype=jnp.int32) & 1).astype(jnp.int32)
    dma = pltpu.SemaphoreType.DMA

    def level_block(array, level):
        return pl.BlockSpec((1,) + array.shape[1:], lambda i: (level, 0, 0))

    pairs = (levels - 1) * (levels - 2) // 2
    static, state, sums = call(
        front_body,
        [sds((rank, pairs * rank), BF), sds((samples, columns), F32), sds((rank, columns), BF)],
        [leaf_inverse, right_side, project_rows, spread_rows],
        [HBM] * 4,
        [
            pltpu.VMEM(leaf_inverse.shape[1:], BF), like(right_side), like(project_rows), like(spread_rows),
            dma((levels,)), dma((levels,)), dma, dma,
        ],
        limit=60,
    )
    static_other = to_core(static, 1)
    stacked = lax.all_gather(
        sums, AXIS, axis_index_groups=[[d, d + 1] for d in range(0, size, 2)], tiled=True
    )
    width = (levels - 2) * rank
    part = rank // 2
    first, keep, send = call(
        cut_body,
        [
            sds((rank, width + inner), BF),
            sds((part, pairs * rank - width), BF),
            sds((part, pairs * rank - width), BF),
        ],
        [bits, static, static_other, capacity],
        [SMEM, ANY, ANY, level_block(capacity, 1)],
        [like(static), like(static), dma((2,))],
    )
    near, far = to_core(first, 0), to_core(first, 0, 3)

    stacked, send = lax.optimization_barrier((stacked, send))
    static_got = swap(send, 2, 1)
    zero, sums = call(
        first_body,
        [sds((rank, columns), BF), sds((columns, (levels - 1) * rank), BF)],
        [state, stacked, capacity, spread_rows, project_rows],
        [VMEM, VMEM, level_block(capacity, 0), level_block(spread_rows, 0), VMEM],
    )
    half = columns // 2
    own, send = call(
        merge_body,
        [sds((half, (levels - 1) * rank), BF)] * 2,
        [bits, sums, to_core(sums, 0)],
        [SMEM, ANY, ANY],
        [like(sums), like(sums), dma((2,))],
    )

    def spread_out(state, mine, base, zero):
        near0 = jnp.stack([c[:, :rank] for c in mine])
        theirs = jnp.stack([c[:, -rank:] for c in mine])
        far0 = swap(theirs, 2, 0)
        near1 = to_core(near0, 1)
        far1 = to_core(theirs, 1, 3)
        count = len(mine)
        tile = samples // 2

        def spread_block(level):
            return pl.BlockSpec((1, tile, rank), lambda i: (level, i, 0))

        whole = pl.BlockSpec((tile, columns), lambda i: (i, 0))
        args = [bits, state] + [spread_rows] * count + [near0, far0, near1, far1]
        specs = [SMEM, whole] + [spread_block(base + i) for i in range(count)] + [VMEM] * 4
        if zero is not None:
            args += [spread_rows, zero]
            specs += [spread_block(0), VMEM]
        return call(
            lambda *refs: spread_body(*refs, count=count, zero=zero is not None),
            [sds((samples, columns), F32)],
            args,
            specs,
            grid=(2,),
            out_specs=[whole],
        )[0]

    gathered = []
    early = levels - 3
    message, cut = keep, 0
    for level in range(1, levels):
        other = swap(send, mask_of(level), 0)
        if level == 1:
            static_got, near, far, other = lax.optimization_barrier((static_got, near, far, other))
        width = max(levels - 2 - level, 0) * rank
        total = message.shape[1] - cut + inner
        outs = [sds((rank, cut), BF)] if cut else []
        if level < levels - 1:
            outs.append(sds((part, total), BF))
        results = call(
            lambda *refs, c=cut, w=width, n=len(outs): static_body(*refs, cut=c, width=w, outs=n),
            outs,
            [bits, message, static_got, capacity],
            [SMEM, ANY, ANY, level_block(capacity, min(level + 1, levels - 1))],
            [like(message), like(message), dma((2,))],
        )
        if level < levels - 1:
            message = results[-1]
            static_got = swap(message, mask_of(level + 1), 1)
        if level > 1:
            near, far = to_core(results[0], 0), to_core(results[0], 0, 3)
        cut = width + inner

        width = (levels - 1 - level) * rank
        outs = [sds((half, 2 * rank if level == 1 else rank), BF)]
        if width:
            outs.append(sds((half, width), BF))
        results = call(
            lambda *refs, l=level: step_body(*refs, level=l),
            outs,
            [bits, own, other, near, far],
            [SMEM, VMEM, VMEM, VMEM, VMEM],
        )
        gathered.append(results[0])
        if width:
            own = send = results[1]
        if level == early:
            state = spread_out(state, gathered, 1, zero)
    return spread_out(state, gathered[early:], early + 1, None)


def solution(mesh):
    return jax.shard_map(
        on_device,
        mesh=mesh,
        in_specs=(
            P(AXIS, None),
            P(AXIS, None, None),
            P(None, AXIS, None),
            P(None, AXIS, None),
            P(None, AXIS, None),
        ),
        out_specs=P(AXIS, None),
        check_vma=False,
    )
```

time: 156 us -> 165 us (1.058)
  waiting for transfers between devices: 33.2 us -> 42.1 us
  starting transfers between devices: 79.7 us -> 87.1 us
  local copies, waits for them, and re-layouts: 9.85 us -> 2.57 us
    unnamed x28 -> x17, local copies, waits for them, and re-layouts: 9.22 us -> 2.56 us
    ppermute x18, waiting for transfers between devices: 18.8 us -> 24.1 us  [swap(): return lax.ppermute(value, AXIS, pairs)]
    ppermute x18, starting transfers between devices: 30.6 us -> 36 us  [swap(): return lax.ppermute(value, AXIS, pairs)]
    ppermute x22, waiting for transfers between devices: 14.4 us -> 18 us  [to_core(): return lax.ppermute(value, AXIS, pairs)]
    ppermute x22, starting transfers between devices: 49.1 us -> 51.2 us  [to_core(): return lax.ppermute(value, AXIS, pairs)]
    pallas_call x21 -> x22, Pallas kernels: 20.6 us -> 21.9 us  [call(): pl.pallas_call(body, out_shape=outs, grid=grid, in_specs=specs, out_specs...]
  transfers between devices with their start and end apart: 40 -> 40, of which waited for: 7 -> 10; matrix products, arithmetic and copies ran while one was open for 3% -> 0% of each run, Pallas kernels for 11% -> 7%
where the time goes in v3:
time: 165 us; the launch traced here: 164 us
  starting transfers between devices  87.1 us (53%)
  waiting for transfers between devices  42.1 us (26%)
  Pallas kernels  21.9 us (13%)
  blocking collectives  9.17 us (6%)
  local copies, waits for them, and re-layouts  2.57 us (2%)
    ppermute x22, starting transfers between devices, to_core(): return lax.ppermute(value, AXIS, pairs)  51.2 us
    ppermute x18, starting transfers between devices, swap(): return lax.ppermute(value, AXIS, pairs)  36 us
    ppermute x18, waiting for transfers between devices, swap(): return lax.ppermute(value, AXIS, pairs)  24.1 us
    pallas_call x22, Pallas kernels, call(): pl.pallas_call(body, out_shape=outs, grid=grid, in_specs=specs, out_specs...  21.9 us
    ppermute x22, waiting for transfers between devices, to_core(): return lax.ppermute(value, AXIS, pairs)  18 us
    all_gather x1, blocking collectives, on_device(): lax.all_gather(sums, AXIS, axis_index_groups=[[d, d + 1] for d in range(0...  9.17 us
  transfers between devices with their start and end apart: 40, of which 10 were waited for; matrix products, arithmetic and copies ran while one was open for 0% of the time, Pallas kernels for 7%

profile of v3, /device:TPU:1, one launch (start us, length us, event | category | flops | bytes accessed | tf_op | source)
XLA Modules:
  0.0 163.7 jit_solution(2804736226550624028)
XLA Ops:
  0.0 4.3 %shard_map.55 = (bf16[128,3584]{1,0:T(8,128)(2,1)}, f32[512,384]{1,0:T(8,128)}, bf16[128,384]{1,0:T(8,128)(2,1)}) custom-call(bf16[1,512,512]{2,1,0:T(8,128)(2,1)} %inverse_hbm.1, bf16[512,384]{1,0:T(8,128)(2,1)} %right_hbm.1, bf16[9,512,128]{2,1,0:T(8,128)(2,1)} %project_ref.1, bf16[9,512,128]{2,1,0:T(8,128)(2,1)} %refs_3_.19), custom_call_target="tpu_custom_call" | custom-call | bytes 3276800 | tf_op jit(solution)/shard_map/pallas_call | solution.py:44
  5.6 9.2 %all_gather.3.stacked_ref = bf16[256,384]{1,0:T(8,128)(2,1)S(1)} all-gather(bf16[128,384]{1,0:T(8,128)(2,1)} %get-tuple-element.48), channel_id=1, replica_groups={{0,1},{2,3},{4,5},{6,7},{8,9},{10,11},{12,13},{14,15},{16,17},{18,19},{..., dimensions={0}, use_global_device_ids=true | all-gather | bytes 294912 | tf_op jit(solution)/shard_map/all_gather | solution.py:240
  14.8 1.3 copy-done.5
  18.5 1.4 shard_map.57
  19.9 1.4 collective-permute-start.1
  21.3 1.8 %collective-permute-done.1.other_any = bf16[384,1024]{1,0:T(8,128)(2,1)S(1)} collective-permute-done((bf16[384,1024]{1,0:T(8,128)(2,1)S(1)}, bf16[384,1024]{1,0:T(8,128)(2,1)S(1)}, u32[]{:S(2)}, u32[]{:S(2)}) %collective-permute-start.1) | collective-permute-done | bytes 786464 | tf_op jit(solution)/shard_map/ppermute | solution.py:25
  24.4 1.9 %collective-permute-start.2 = (bf16[64,2688]{1,0:T(8,128)(2,1)S(1)}, bf16[64,2688]{1,0:T(8,128)(2,1)S(1)}, u32[]{:S(2)}, u32[]{:S(2)}) collective-permute-start(bf16[64,2688]{1,0:T(8,128)(2,1)S(1)} %get-tuple-element.54), channel_id=1, source_target_pairs={{1,3},{3,1},{5,7},{7,5},{9,11},{11,9},{13,15},{15,13},{17,19},{19,... | collective-permute-start | bytes 1032200 | tf_op jit(solution)/shard_map/ppermute | solution.py:20
  26.3 2.6 %collective-permute-start.3 = (bf16[128,1152]{1,0:T(8,128)(2,1)S(1)}, bf16[128,1152]{1,0:T(8,128)(2,1)S(1)}, u32[]{:S(2)}, u32[]{:S(2)}) collective-permute-start(bf16[128,1152]{1,0:T(8,128)(2,1)S(1)} %get-tuple-element.55), channel_id=1, source_target_pairs={{1,0},{3,2},{5,4},{7,6},{9,8},{11,10},{13,12},{15,14},{17,16},{19,... | collective-permute-start | bytes 884744 | tf_op jit(solution)/shard_map/ppermute | solution.py:25
  28.9 2.9 %collective-permute-start.4 = (bf16[128,1152]{1,0:T(8,128)(2,1)S(1)}, bf16[128,1152]{1,0:T(8,128)(2,1)S(1)}, u32[]{:S(2)}, u32[]{:S(2)}) collective-permute-start(bf16[128,1152]{1,0:T(8,128)(2,1)S(1)} %get-tuple-element.55), channel_id=1, source_target_pairs={{3,0},{1,2},{7,4},{5,6},{11,8},{9,10},{15,12},{13,14},{19,16},{17,... | collective-permute-start | bytes 884744 | tf_op jit(solution)/shard_map/ppermute | solution.py:25
  31.9 6.0 %collective-permute-done.4.refs_4_ = bf16[128,1152]{1,0:T(8,128)(2,1)S(1)} collective-permute-done((bf16[128,1152]{1,0:T(8,128)(2,1)S(1)}, bf16[128,1152]{1,0:T(8,128)(2,1)S(1)}, u32[]{:S(2)}, u32[]{:S(2)}) %collective-permute-start.4) | collective-permute-done | bytes 294944 | tf_op jit(solution)/shard_map/ppermute | solution.py:25
  38.8 3.0 %collective-permute-start.7 = (bf16[64,2944]{1,0:T(8,128)(2,1)S(1)}, bf16[64,2944]{1,0:T(8,128)(2,1)S(1)}, u32[]{:S(2)}, u32[]{:S(2)}) collective-permute-start(bf16[64,2944]{1,0:T(8,128)(2,1)S(1)} %shard_map.60.refs_1_), channel_id=1, source_target_pairs={{1,5},{3,7},{5,1},{7,3},{9,13},{11,15},{13,9},{15,11},{17,21},{19,... | collective-permute-start | bytes 1130504 | tf_op jit(solution)/shard_map/ppermute | solution.py:20
  41.8 16.9 %collective-permute-done.7.refs_2_ = bf16[64,2944]{1,0:T(8,128)(2,1)S(1)} collective-permute-done((bf16[64,2944]{1,0:T(8,128)(2,1)S(1)}, bf16[64,2944]{1,0:T(8,128)(2,1)S(1)}, u32[]{:S(2)}, u32[]{:S(2)}) %collective-permute-start.7) | collective-permute-done | bytes 376864 | tf_op jit(solution)/shard_map/ppermute | solution.py:20
  59.6 5.0 %collective-permute-start.11 = (bf16[64,2176]{1,0:T(8,128)(2,1)S(1)}, bf16[64,2176]{1,0:T(8,128)(2,1)S(1)}, u32[]{:S(2)}, u32[]{:S(2)}) collective-permute-start(bf16[64,2176]{1,0:T(8,128)(2,1)S(1)} %get-tuple-element.67.refs_1_), channel_id=1, source_target_pairs={{1,13},{3,15},{5,9},{7,11},{9,5},{11,7},{13,1},{15,3},{17,29},{19,... | collective-permute-start | bytes 835592 | tf_op jit(solution)/shard_map/ppermute | solution.py:20
  65.8 1.3 collective-permute-start.8
  67.1 1.3 collective-permute-start.9
  68.5 2.6 %collective-permute-done.11.refs_2_ = bf16[64,2176]{1,0:T(8,128)(2,1)S(1)} collective-permute-done((bf16[64,2176]{1,0:T(8,128)(2,1)S(1)}, bf16[64,2176]{1,0:T(8,128)(2,1)S(1)}, u32[]{:S(2)}, u32[]{:S(2)}) %collective-permute-start.11) | collective-permute-done | bytes 278560 | tf_op jit(solution)/shard_map/ppermute | solution.py:20
  71.8 3.2 %collective-permute-start.15 = (bf16[64,1536]{1,0:T(8,128)(2,1)S(1)}, bf16[64,1536]{1,0:T(8,128)(2,1)S(1)}, u32[]{:S(2)}, u32[]{:S(2)}) collective-permute-start(bf16[64,1536]{1,0:T(8,128)(2,1)S(1)} %get-tuple-element.71.refs_1_), channel_id=1, source_target_pairs={{1,17},{3,19},{5,21},{7,23},{9,25},{11,27},{13,29},{15,31},{17,1},... | collective-permute-start | bytes 589832 | tf_op jit(solution)/shard_map/ppermute | solution.py:20
  76.2 4.9 %collective-permute-start.12 = (bf16[128,896]{1,0:T(8,128)(2,1)S(1)}, bf16[128,896]{1,0:T(8,128)(2,1)S(1)}, u32[]{:S(2)}, u32[]{:S(2)}) collective-permute-start(bf16[128,896]{1,0:T(8,128)(2,1)S(1)} %get-tuple-element.68), channel_id=1, source_target_pairs={{1,0},{3,2},{5,4},{7,6},{9,8},{11,10},{13,12},{15,14},{17,16},{19,... | collective-permute-start | bytes 688136 | tf_op jit(solution)/shard_map/ppermute | solution.py:25
  81.2 1.5 collective-permute-start.13
  83.8 4.0 %collective-permute-start.19 = (bf16[64,1024]{1,0:T(8,128)(2,1)S(1)}, bf16[64,1024]{1,0:T(8,128)(2,1)S(1)}, u32[]{:S(2)}, u32[]{:S(2)}) collective-permute-start(bf16[64,1024]{1,0:T(8,128)(2,1)S(1)} %get-tuple-element.75.refs_1_), channel_id=1, source_target_pairs={{1,33},{3,35},{5,37},{7,39},{9,41},{11,43},{13,45},{15,47},{17,49}... | collective-permute-start | bytes 393224 | tf_op jit(solution)/shard_map/ppermute | solution.py:20
  89.1 2.7 %collective-permute-done.19.refs_2_ = bf16[64,1024]{1,0:T(8,128)(2,1)S(1)} collective-permute-done((bf16[64,1024]{1,0:T(8,128)(2,1)S(1)}, bf16[64,1024]{1,0:T(8,128)(2,1)S(1)}, u32[]{:S(2)}, u32[]{:S(2)}) %collective-permute-start.19) | collective-permute-done | bytes 131104 | tf_op jit(solution)/shard_map/ppermute | solution.py:20
  92.8 4.7 %collective-permute-start.23 = (bf16[64,640]{1,0:T(8,128)(2,1)S(1)}, bf16[64,640]{1,0:T(8,128)(2,1)S(1)}, u32[]{:S(2)}, u32[]{:S(2)}) collective-permute-start(bf16[64,640]{1,0:T(8,128)(2,1)S(1)} %get-tuple-element.79.refs_1_), channel_id=1, source_target_pairs={{1,97},{3,99},{5,101},{7,103},{9,105},{11,107},{13,109},{15,111},{... | collective-permute-start | bytes 245768 | tf_op jit(solution)/shard_map/ppermute | solution.py:20
  101.0 3.1 %collective-permute-start.30 = (bf16[64,384]{1,0:T(8,128)(2,1)S(1)}, bf16[64,384]{1,0:T(8,128)(2,1)S(1)}, u32[]{:S(2)}, u32[]{:S(2)}) collective-permute-start(bf16[64,384]{1,0:T(8,128)(2,1)S(1)} %get-tuple-element.84.refs_1_), channel_id=1, source_target_pairs={{1,129},{3,131},{5,133},{7,135},{9,137},{11,139},{13,141},{15,143}... | collective-permute-start | bytes 147464 | tf_op jit(solution)/shard_map/ppermute | solution.py:20
  111.7 2.7 %collective-permute-start.31 = (bf16[128,384]{1,0:T(8,128)(2,1)S(1)}, bf16[128,384]{1,0:T(8,128)(2,1)S(1)}, u32[]{:S(2)}, u32[]{:S(2)}) collective-permute-start(bf16[128,384]{1,0:T(8,128)(2,1)S(1)} %get-tuple-element.85), channel_id=1, source_target_pairs={{1,0},{3,2},{5,4},{7,6},{9,8},{11,10},{13,12},{15,14},{17,16},{19,... | collective-permute-start | bytes 294920 | tf_op jit(solution)/shard_map/ppermute | solution.py:25
  119.0 4.4 %collective-permute-start.34 = (bf16[64,256]{1,0:T(8,128)(2,1)S(1)}, bf16[64,256]{1,0:T(8,128)(2,1)S(1)}, u32[]{:S(2)}, u32[]{:S(2)}) collective-permute-start(bf16[64,256]{1,0:T(8,128)(2,1)S(1)} %get-tuple-element.88.refs_1_), channel_id=1, source_target_pairs={{1,385},{3,387},{5,389},{7,391},{9,393},{11,395},{13,397},{15,399}... | collective-permute-start | bytes 98312 | tf_op jit(solution)/shard_map/ppermute | solution.py:20
  123.4 1.5 collective-permute-done.34.refs_2_
  125.5 12.7 %collective-permute-start.35 = (bf16[128,256]{1,0:T(8,128)(2,1)S(1)}, bf16[128,256]{1,0:T(8,128)(2,1)S(1)}, u32[]{:S(2)}, u32[]{:S(2)}) collective-permute-start(bf16[128,256]{1,0:T(8,128)(2,1)S(1)} %shard_map.74), channel_id=1, source_target_pairs={{1,0},{3,2},{5,4},{7,6},{9,8},{11,10},{13,12},{15,14},{17,16},{19,... | collective-permute-start | bytes 196616 | tf_op jit(solution)/shard_map/ppermute | solution.py:25
  140.9 4.3 %collective-permute-start.36 = (bf16[128,256]{1,0:T(8,128)(2,1)S(1)}, bf16[128,256]{1,0:T(8,128)(2,1)S(1)}, u32[]{:S(2)}, u32[]{:S(2)}) collective-permute-start(bf16[128,256]{1,0:T(8,128)(2,1)S(1)} %shard_map.74), channel_id=1, source_target_pairs={{3,0},{1,2},{7,4},{5,6},{11,8},{9,10},{15,12},{13,14},{19,16},{17,... | collective-permute-start | bytes 196616 | tf_op jit(solution)/shard_map/ppermute | solution.py:25
  151.0 1.5 shard_map.71.refs_1_
  152.5 5.4 %collective-permute-done.38.refs_6_ = bf16[2,192,128]{2,1,0:T(8,128)(2,1)S(1)} collective-permute-done((bf16[2,192,128]{2,1,0:T(8,128)(2,1)S(1)}, bf16[2,192,128]{2,1,0:T(8,128)(2,1)S(1)}, u32[]{:S(2)}, u32[]{:S(2)}) %collective-permute-start.38) | collective-permute-done | bytes 98336 | tf_op jit(solution)/shard_map/ppermute | solution.py:25
  157.9 3.9 %collective-permute-done.39.refs_7_ = bf16[2,192,128]{2,1,0:T(8,128)(2,1)S(1)} collective-permute-done((bf16[2,192,128]{2,1,0:T(8,128)(2,1)S(1)}, bf16[2,192,128]{2,1,0:T(8,128)(2,1)S(1)}, u32[]{:S(2)}, u32[]{:S(2)}) %collective-permute-start.39) | collective-permute-done | bytes 98336 | tf_op jit(solution)/shard_map/ppermute | solution.py:25
  161.8 1.8 %shard_map.76 = f32[512,384]{1,0:T(8,128)} custom-call(s32[9]{0:T(128)S(1)} %shift-right-arithmetic_and_fusion.bits_ref.refs_0_, f32[512,384]{1,0:T(8,128)S(1)} %shard_map.71.refs_1_, bf16[9,512,128]{2,1,0:T(8,128)(2,1)S(1)} %copy-done, bf16[9,512,128]{2,1,0:T(8,128)(2,1)S(1)} %copy-done, bf16[2,192,128]{2,1,0:T(8,128)(2,1)S(1)} %pad_maximum_fusion.refs_4_, ...), custom_call_target="tpu_custom_call" | custom-call | bytes 3538980 | tf_op jit(solution)/shard_map/pallas_call | solution.py:44
  (91 shorter events, 37.8 us)
Async XLA Ops:
  4.3 10.5 %collective-permute-start = (bf16[128,3584]{1,0:T(8,128)(2,1)}, bf16[128,3584]{1,0:T(8,128)(2,1)S(1)}, u32[]{:S(2)}, u32[]{:S(2)}) collective-permute-start(bf16[128,3584]{1,0:T(8,128)(2,1)} %get-tuple-element.49.own_any), channel_id=1, source_target_pairs={{0,1},{2,3},{4,5},{6,7},{8,9},{10,11},{12,13},{14,15},{16,17},{18,... | collective-permute-start | bytes 2752520 | tf_op jit(solution)/shard_map/ppermute | solution.py:25
  23.7 14.2 %collective-permute-start.5 = (bf16[192,1024]{1,0:T(8,128)(2,1)S(1)}, bf16[192,1024]{1,0:T(8,128)(2,1)S(1)}, u32[]{:S(2)}, u32[]{:S(2)}) collective-permute-start(bf16[192,1024]{1,0:T(8,128)(2,1)S(1)} %get-tuple-element.56), channel_id=1, source_target_pairs={{0,2},{2,0},{4,6},{6,4},{8,10},{10,8},{12,14},{14,12},{16,18},{18,... | collective-permute-start | bytes 1179656 | tf_op jit(solution)/shard_map/ppermute | solution.py:20
  24.4 13.5 %collective-permute-start.2 = (bf16[64,2688]{1,0:T(8,128)(2,1)S(1)}, bf16[64,2688]{1,0:T(8,128)(2,1)S(1)}, u32[]{:S(2)}, u32[]{:S(2)}) collective-permute-start(bf16[64,2688]{1,0:T(8,128)(2,1)S(1)} %get-tuple-element.54), channel_id=1, source_target_pairs={{1,3},{3,1},{5,7},{7,5},{9,11},{11,9},{13,15},{15,13},{17,19},{19,... | collective-permute-start | bytes 1032200 | tf_op jit(solution)/shard_map/ppermute | solution.py:20
  28.9 9.0 %collective-permute-start.4 = (bf16[128,1152]{1,0:T(8,128)(2,1)S(1)}, bf16[128,1152]{1,0:T(8,128)(2,1)S(1)}, u32[]{:S(2)}, u32[]{:S(2)}) collective-permute-start(bf16[128,1152]{1,0:T(8,128)(2,1)S(1)} %get-tuple-element.55), channel_id=1, source_target_pairs={{3,0},{1,2},{7,4},{5,6},{11,8},{9,10},{15,12},{13,14},{19,16},{17,... | collective-permute-start | bytes 884744 | tf_op jit(solution)/shard_map/ppermute | solution.py:25
  38.8 19.8 %collective-permute-start.7 = (bf16[64,2944]{1,0:T(8,128)(2,1)S(1)}, bf16[64,2944]{1,0:T(8,128)(2,1)S(1)}, u32[]{:S(2)}, u32[]{:S(2)}) collective-permute-start(bf16[64,2944]{1,0:T(8,128)(2,1)S(1)} %shard_map.60.refs_1_), channel_id=1, source_target_pairs={{1,5},{3,7},{5,1},{7,3},{9,13},{11,15},{13,9},{15,11},{17,21},{19,... | collective-permute-start | bytes 1130504 | tf_op jit(solution)/shard_map/ppermute | solution.py:20
  59.6 11.4 %collective-permute-start.11 = (bf16[64,2176]{1,0:T(8,128)(2,1)S(1)}, bf16[64,2176]{1,0:T(8,128)(2,1)S(1)}, u32[]{:S(2)}, u32[]{:S(2)}) collective-permute-start(bf16[64,2176]{1,0:T(8,128)(2,1)S(1)} %get-tuple-element.67.refs_1_), channel_id=1, source_target_pairs={{1,13},{3,15},{5,9},{7,11},{9,5},{11,7},{13,1},{15,3},{17,29},{19,... | collective-permute-start | bytes 835592 | tf_op jit(solution)/shard_map/ppermute | solution.py:20
  65.1 9.8 %collective-permute-start.6 = (bf16[192,896]{1,0:T(8,128)(2,1)S(1)}, bf16[192,896]{1,0:T(8,128)(2,1)S(1)}, u32[]{:S(2)}, u32[]{:S(2)}) collective-permute-start(bf16[192,896]{1,0:T(8,128)(2,1)S(1)} %get-tuple-element.61.refs_1_), channel_id=1, source_target_pairs={{0,4},{2,6},{4,0},{6,2},{8,12},{10,14},{12,8},{14,10},{16,20},{18,... | collective-permute-start | bytes 1032200 | tf_op jit(solution)/shard_map/ppermute | solution.py:20
  65.8 9.1 %collective-permute-start.8 = (bf16[128,1024]{1,0:T(8,128)(2,1)S(1)}, bf16[128,1024]{1,0:T(8,128)(2,1)S(1)}, u32[]{:S(2)}, u32[]{:S(2)}) collective-permute-start(bf16[128,1024]{1,0:T(8,128)(2,1)S(1)} %get-tuple-element.64), channel_id=1, source_target_pairs={{1,0},{3,2},{5,4},{7,6},{9,8},{11,10},{13,12},{15,14},{17,16},{19,... | collective-permute-start | bytes 786440 | tf_op jit(solution)/shard_map/ppermute | solution.py:25
  67.1 7.8 %collective-permute-start.9 = (bf16[128,1024]{1,0:T(8,128)(2,1)S(1)}, bf16[128,1024]{1,0:T(8,128)(2,1)S(1)}, u32[]{:S(2)}, u32[]{:S(2)}) collective-permute-start(bf16[128,1024]{1,0:T(8,128)(2,1)S(1)} %get-tuple-element.64), channel_id=1, source_target_pairs={{3,0},{1,2},{7,4},{5,6},{11,8},{9,10},{15,12},{13,14},{19,16},{17,... | collective-permute-start | bytes 786440 | tf_op jit(solution)/shard_map/ppermute | solution.py:25
  71.8 11.0 %collective-permute-start.15 = (bf16[64,1536]{1,0:T(8,128)(2,1)S(1)}, bf16[64,1536]{1,0:T(8,128)(2,1)S(1)}, u32[]{:S(2)}, u32[]{:S(2)}) collective-permute-start(bf16[64,1536]{1,0:T(8,128)(2,1)S(1)} %get-tuple-element.71.refs_1_), channel_id=1, source_target_pairs={{1,17},{3,19},{5,21},{7,23},{9,25},{11,27},{13,29},{15,31},{17,1},... | collective-permute-start | bytes 589832 | tf_op jit(solution)/shard_map/ppermute | solution.py:20
  75.6 12.3 %collective-permute-start.10 = (bf16[192,768]{1,0:T(8,128)(2,1)S(1)}, bf16[192,768]{1,0:T(8,128)(2,1)S(1)}, u32[]{:S(2)}, u32[]{:S(2)}) collective-permute-start(bf16[192,768]{1,0:T(8,128)(2,1)S(1)} %get-tuple-element.66.refs_1_), channel_id=1, source_target_pairs={{0,12},{2,14},{4,8},{6,10},{8,4},{10,6},{12,0},{14,2},{16,28},{18,... | collective-permute-start | bytes 884744 | tf_op jit(solution)/shard_map/ppermute | solution.py:20
  76.2 11.6 %collective-permute-start.12 = (bf16[128,896]{1,0:T(8,128)(2,1)S(1)}, bf16[128,896]{1,0:T(8,128)(2,1)S(1)}, u32[]{:S(2)}, u32[]{:S(2)}) collective-permute-start(bf16[128,896]{1,0:T(8,128)(2,1)S(1)} %get-tuple-element.68), channel_id=1, source_target_pairs={{1,0},{3,2},{5,4},{7,6},{9,8},{11,10},{13,12},{15,14},{17,16},{19,... | collective-permute-start | bytes 688136 | tf_op jit(solution)/shard_map/ppermute | solution.py:25
  81.2 6.7 %collective-permute-start.13 = (bf16[128,896]{1,0:T(8,128)(2,1)S(1)}, bf16[128,896]{1,0:T(8,128)(2,1)S(1)}, u32[]{:S(2)}, u32[]{:S(2)}) collective-permute-start(bf16[128,896]{1,0:T(8,128)(2,1)S(1)} %get-tuple-element.68), channel_id=1, source_target_pairs={{3,0},{1,2},{7,4},{5,6},{11,8},{9,10},{15,12},{13,14},{19,16},{17,... | collective-permute-start | bytes 688136 | tf_op jit(solution)/shard_map/ppermute | solution.py:25
  83.8 8.0 %collective-permute-start.19 = (bf16[64,1024]{1,0:T(8,128)(2,1)S(1)}, bf16[64,1024]{1,0:T(8,128)(2,1)S(1)}, u32[]{:S(2)}, u32[]{:S(2)}) collective-permute-start(bf16[64,1024]{1,0:T(8,128)(2,1)S(1)} %get-tuple-element.75.refs_1_), channel_id=1, source_target_pairs={{1,33},{3,35},{5,37},{7,39},{9,41},{11,43},{13,45},{15,47},{17,49}... | collective-permute-start | bytes 393224 | tf_op jit(solution)/shard_map/ppermute | solution.py:20
  88.4 22.0 %collective-permute-start.14 = (bf16[192,640]{1,0:T(8,128)(2,1)S(1)}, bf16[192,640]{1,0:T(8,128)(2,1)S(1)}, u32[]{:S(2)}, u32[]{:S(2)}) collective-permute-start(bf16[192,640]{1,0:T(8,128)(2,1)S(1)} %get-tuple-element.70.refs_1_), channel_id=1, source_target_pairs={{0,16},{2,18},{4,20},{6,22},{8,24},{10,26},{12,28},{14,30},{16,0},... | collective-permute-start | bytes 737288 | tf_op jit(solution)/shard_map/ppermute | solution.py:20
  92.8 7.4 %collective-permute-start.23 = (bf16[64,640]{1,0:T(8,128)(2,1)S(1)}, bf16[64,640]{1,0:T(8,128)(2,1)S(1)}, u32[]{:S(2)}, u32[]{:S(2)}) collective-permute-start(bf16[64,640]{1,0:T(8,128)(2,1)S(1)} %get-tuple-element.79.refs_1_), channel_id=1, source_target_pairs={{1,97},{3,99},{5,101},{7,103},{9,105},{11,107},{13,109},{15,111},{... | collective-permute-start | bytes 245768 | tf_op jit(solution)/shard_map/ppermute | solution.py:20
  97.5 10.3 %collective-permute-start.16 = (bf16[128,768]{1,0:T(8,128)(2,1)S(1)}, bf16[128,768]{1,0:T(8,128)(2,1)S(1)}, u32[]{:S(2)}, u32[]{:S(2)}) collective-permute-start(bf16[128,768]{1,0:T(8,128)(2,1)S(1)} %get-tuple-element.72), channel_id=1, source_target_pairs={{1,0},{3,2},{5,4},{7,6},{9,8},{11,10},{13,12},{15,14},{17,16},{19,... | collective-permute-start | bytes 589832 | tf_op jit(solution)/shard_map/ppermute | solution.py:25
  98.8 10.3 %collective-permute-start.17 = (bf16[128,768]{1,0:T(8,128)(2,1)S(1)}, bf16[128,768]{1,0:T(8,128)(2,1)S(1)}, u32[]{:S(2)}, u32[]{:S(2)}) collective-permute-start(bf16[128,768]{1,0:T(8,128)(2,1)S(1)} %get-tuple-element.72), channel_id=1, source_target_pairs={{3,0},{1,2},{7,4},{5,6},{11,8},{9,10},{15,12},{13,14},{19,16},{17,... | collective-permute-start | bytes 589832 | tf_op jit(solution)/shard_map/ppermute | solution.py:25
  104.1 7.6 %collective-permute-start.20 = (bf16[128,640]{1,0:T(8,128)(2,1)S(1)}, bf16[128,640]{1,0:T(8,128)(2,1)S(1)}, u32[]{:S(2)}, u32[]{:S(2)}) collective-permute-start(bf16[128,640]{1,0:T(8,128)(2,1)S(1)} %get-tuple-element.76), channel_id=1, source_target_pairs={{1,0},{3,2},{5,4},{7,6},{9,8},{11,10},{13,12},{15,14},{17,16},{19,... | collective-permute-start | bytes 491528 | tf_op jit(solution)/shard_map/ppermute | solution.py:25
  105.8 8.6 %collective-permute-start.21 = (bf16[128,640]{1,0:T(8,128)(2,1)S(1)}, bf16[128,640]{1,0:T(8,128)(2,1)S(1)}, u32[]{:S(2)}, u32[]{:S(2)}) collective-permute-start(bf16[128,640]{1,0:T(8,128)(2,1)S(1)} %get-tuple-element.76), channel_id=1, source_target_pairs={{3,0},{1,2},{7,4},{5,6},{11,8},{9,10},{15,12},{13,14},{19,16},{17,... | collective-permute-start | bytes 491528 | tf_op jit(solution)/shard_map/ppermute | solution.py:25
  107.8 9.2 %collective-permute-start.24 = (bf16[128,512]{1,0:T(8,128)(2,1)S(1)}, bf16[128,512]{1,0:T(8,128)(2,1)S(1)}, u32[]{:S(2)}, u32[]{:S(2)}) collective-permute-start(bf16[128,512]{1,0:T(8,128)(2,1)S(1)} %get-tuple-element.80), channel_id=1, source_target_pairs={{1,0},{3,2},{5,4},{7,6},{9,8},{11,10},{13,12},{15,14},{17,16},{19,... | collective-permute-start | bytes 393224 | tf_op jit(solution)/shard_map/ppermute | solution.py:25
  109.2 7.9 %collective-permute-start.25 = (bf16[128,512]{1,0:T(8,128)(2,1)S(1)}, bf16[128,512]{1,0:T(8,128)(2,1)S(1)}, u32[]{:S(2)}, u32[]{:S(2)}) collective-permute-start(bf16[128,512]{1,0:T(8,128)(2,1)S(1)} %get-tuple-element.80), channel_id=1, source_target_pairs={{3,0},{1,2},{7,4},{5,6},{11,8},{9,10},{15,12},{13,14},{19,16},{17,... | collective-permute-start | bytes 393224 | tf_op jit(solution)/shard_map/ppermute | solution.py:25
  111.7 26.5 %collective-permute-start.31 = (bf16[128,384]{1,0:T(8,128)(2,1)S(1)}, bf16[128,384]{1,0:T(8,128)(2,1)S(1)}, u32[]{:S(2)}, u32[]{:S(2)}) collective-permute-start(bf16[128,384]{1,0:T(8,128)(2,1)S(1)} %get-tuple-element.85), channel_id=1, source_target_pairs={{1,0},{3,2},{5,4},{7,6},{9,8},{11,10},{13,12},{15,14},{17,16},{19,... | collective-permute-start | bytes 294920 | tf_op jit(solution)/shard_map/ppermute | solution.py:25
  114.4 25.1 %collective-permute-start.32 = (bf16[128,384]{1,0:T(8,128)(2,1)S(1)}, bf16[128,384]{1,0:T(8,128)(2,1)S(1)}, u32[]{:S(2)}, u32[]{:S(2)}) collective-permute-start(bf16[128,384]{1,0:T(8,128)(2,1)S(1)} %get-tuple-element.85), channel_id=1, source_target_pairs={{3,0},{1,2},{7,4},{5,6},{11,8},{9,10},{15,12},{13,14},{19,16},{17,... | collective-permute-start | bytes 294920 | tf_op jit(solution)/shard_map/ppermute | solution.py:25
  117.6 32.0 %collective-permute-start.26 = (bf16[6,192,128]{2,1,0:T(8,128)(2,1)S(1)}, bf16[6,192,128]{2,1,0:T(8,128)(2,1)S(1)}, u32[]{:S(2)}, u32[]{:S(2)}) collective-permute-start(bf16[6,192,128]{2,1,0:T(8,128)(2,1)S(1)} %get-tuple-element.91), channel_id=1, source_target_pairs={{0,2},{2,0},{4,6},{6,4},{8,10},{10,8},{12,14},{14,12},{16,18},{18,... | collective-permute-start | bytes 884744 | tf_op jit(solution)/shard_map/ppermute | solution.py:20
  118.3 22.5 %collective-permute-start.29 = (bf16[192,256]{1,0:T(8,128)(2,1)S(1)}, bf16[192,256]{1,0:T(8,128)(2,1)S(1)}, u32[]{:S(2)}, u32[]{:S(2)}) collective-permute-start(bf16[192,256]{1,0:T(8,128)(2,1)S(1)} %get-tuple-element.83.refs_1_), channel_id=1, source_target_pairs={{0,128},{2,130},{4,132},{6,134},{8,136},{10,138},{12,140},{14,142}... | collective-permute-start | bytes 294920 | tf_op jit(solution)/shard_map/ppermute | solution.py:20
  125.5 20.2 %collective-permute-start.35 = (bf16[128,256]{1,0:T(8,128)(2,1)S(1)}, bf16[128,256]{1,0:T(8,128)(2,1)S(1)}, u32[]{:S(2)}, u32[]{:S(2)}) collective-permute-start(bf16[128,256]{1,0:T(8,128)(2,1)S(1)} %shard_map.74), channel_id=1, source_target_pairs={{1,0},{3,2},{5,4},{7,6},{9,8},{11,10},{13,12},{15,14},{17,16},{19,... | collective-permute-start | bytes 196616 | tf_op jit(solution)/shard_map/ppermute | solution.py:25
  138.2 12.7 %collective-permute-start.27 = (bf16[6,192,128]{2,1,0:T(8,128)(2,1)S(1)}, bf16[6,192,128]{2,1,0:T(8,128)(2,1)S(1)}, u32[]{:S(2)}, u32[]{:S(2)}) collective-permute-start(bf16[6,192,128]{2,1,0:T(8,128)(2,1)S(1)} %get-tuple-element.92.refs_8_), channel_id=1, source_target_pairs={{0,1},{2,3},{4,5},{6,7},{8,9},{10,11},{12,13},{14,15},{16,17},{18,... | collective-permute-start | bytes 884744 | tf_op jit(solution)/shard_map/ppermute | solution.py:25
  139.5 11.4 %collective-permute-start.28 = (bf16[6,192,128]{2,1,0:T(8,128)(2,1)S(1)}, bf16[6,192,128]{2,1,0:T(8,128)(2,1)S(1)}, u32[]{:S(2)}, u32[]{:S(2)}) collective-permute-start(bf16[6,192,128]{2,1,0:T(8,128)(2,1)S(1)} %get-tuple-element.91), channel_id=1, source_target_pairs={{2,1},{0,3},{6,5},{4,7},{10,9},{8,11},{14,13},{12,15},{18,17},{16,... | collective-permute-start | bytes 884744 | tf_op jit(solution)/shard_map/ppermute | solution.py:25
  140.9 6.2 %collective-permute-start.36 = (bf16[128,256]{1,0:T(8,128)(2,1)S(1)}, bf16[128,256]{1,0:T(8,128)(2,1)S(1)}, u32[]{:S(2)}, u32[]{:S(2)}) collective-permute-start(bf16[128,256]{1,0:T(8,128)(2,1)S(1)} %shard_map.74), channel_id=1, source_target_pairs={{3,0},{1,2},{7,4},{5,6},{11,8},{9,10},{15,12},{13,14},{19,16},{17,... | collective-permute-start | bytes 196616 | tf_op jit(solution)/shard_map/ppermute | solution.py:25
  148.4 9.5 %collective-permute-start.38 = (bf16[2,192,128]{2,1,0:T(8,128)(2,1)S(1)}, bf16[2,192,128]{2,1,0:T(8,128)(2,1)S(1)}, u32[]{:S(2)}, u32[]{:S(2)}) collective-permute-start(bf16[2,192,128]{2,1,0:T(8,128)(2,1)S(1)} %pad_maximum_fusion.refs_4_), channel_id=1, source_target_pairs={{0,1},{2,3},{4,5},{6,7},{8,9},{10,11},{12,13},{14,15},{16,17},{18,... | collective-permute-start | bytes 294920 | tf_op jit(solution)/shard_map/ppermute | solution.py:25
  149.7 12.1 %collective-permute-start.39 = (bf16[2,192,128]{2,1,0:T(8,128)(2,1)S(1)}, bf16[2,192,128]{2,1,0:T(8,128)(2,1)S(1)}, u32[]{:S(2)}, u32[]{:S(2)}) collective-permute-start(bf16[2,192,128]{2,1,0:T(8,128)(2,1)S(1)} %pad_maximum_fusion.refs_4_), channel_id=1, source_target_pairs={{2,1},{0,3},{6,5},{4,7},{10,9},{8,11},{14,13},{12,15},{18,17},{16,... | collective-permute-start | bytes 294920 | tf_op jit(solution)/shard_map/ppermute | solution.py:25
  (14 other events, 87.5 us)

commit v4 on v3

--- a/solution.py
+++ b/solution.py
@@ -34,13 +34,11 @@
 TN = ((0,), (0,))
 
 
-SMEM = pl.BlockSpec(memory_space=pltpu.SMEM)
 VMEM = pl.BlockSpec(memory_space=pltpu.VMEM)
-HBM = pl.BlockSpec(memory_space=pltpu.HBM)
 ANY = pl.BlockSpec(memory_space=pl.ANY)
 
 
-def call(body, outs, args, specs, scratch=(), grid=(1,), out_specs=None, limit=40):
+def call(body, outs, args, specs, scratch=(), grid=(1,), out_specs=None):
     return pl.pallas_call(
         body,
         out_shape=outs,
@@ -48,7 +46,7 @@
         in_specs=specs,
         out_specs=out_specs or [VMEM] * len(outs),
         scratch_shapes=list(scratch),
-        compiler_params=pltpu.CompilerParams(vmem_limit_bytes=limit * 2**20),
+        compiler_params=pltpu.CompilerParams(vmem_limit_bytes=40 * 2**20),
         cost_estimate=pl.CostEstimate(
             flops=0, bytes_accessed=sum(a.size * a.dtype.itemsize for a in args), transcendentals=0
         ),
@@ -63,43 +61,29 @@
     return pltpu.VMEM(array.shape, array.dtype)
 
 
+def bit(level):
+    return lax.axis_index(AXIS) >> level & 1
+
+
 def rows_of(part, count):
     return pl.ds(pl.multiple_of(part * count, count), count)
 
 
-def front_body(
-    inverse_hbm, right_hbm, project_hbm, spread_hbm, static_ref, state_ref, sums_ref,
-    inverse, right, project, spread, project_sems, spread_sems, inverse_sem, right_sem,
-):
-    levels = project.shape[0]
-    copies = {}
-    for level in range(1, levels):
-        if level < levels - 1:
-            copies["s", level] = pltpu.make_async_copy(spread_hbm.at[level], spread.at[level], spread_sems.at[level])
-            copies["s", level].start()
-        if level > 1:
-            copies["p", level] = pltpu.make_async_copy(project_hbm.at[level], project.at[level], project_sems.at[level])
-            copies["p", level].start()
-    late = [
-        pltpu.make_async_copy(inverse_hbm.at[0], inverse, inverse_sem),
-        pltpu.make_async_copy(right_hbm, right, right_sem),
-        pltpu.make_async_copy(project_hbm.at[0], project.at[0], project_sems.at[0]),
-    ]
-    for copy in late:
-        copy.start()
-    for copy in copies.values():
-        copy.wait()
+def blocks_body(project_ref, spread_ref, static_ref):
+    levels = project_ref.shape[0]
     at = 0
     for low in range(1, levels - 1):
-        block = [dot(spread[low], project[high], TN) for high in range(low + 1, levels)]
-        for part in block:
-            static_ref[:, at : at + part.shape[1]] = part.astype(BF)
-            at += part.shape[1]
-    for copy in late:
-        copy.wait()
-    state = dot(inverse[...], right[...], NN)
+        spread = spread_ref[low]
+        for high in range(low + 1, levels):
+            block = dot(spread, project_ref[high], TN)
+            static_ref[:, at : at + block.shape[1]] = block.astype(BF)
+            at += block.shape[1]
+
+
+def leaf_body(inverse_ref, right_ref, project_ref, state_ref, sums_ref):
+    state = dot(inverse_ref[0], right_ref[...], NN)
     state_ref[...] = state
-    sums_ref[...] = dot(project[0], state.astype(BF), TN).astype(BF)
+    sums_ref[...] = dot(project_ref[0], state.astype(BF), TN).astype(BF)
 
 
 def first_body(state_ref, stacked_ref, capacity_ref, spread_ref, project_ref, first_ref, sums_ref):
@@ -120,22 +104,22 @@
         copy.wait()
 
 
-def merge_body(bits_ref, own_any, other_any, keep_ref, send_ref, own, other, sems):
-    @pl.when(bits_ref[0] == 0)
+def merge_body(own_any, other_any, keep_ref, send_ref, own, other, sems):
+    @pl.when(bit(0) == 0)
     def _():
         fetch([(own_any, own), (other_any, other)], sems)
-        side = bits_ref[1]
+        side = bit(1)
         count = keep_ref.shape[0]
         for part, out_ref in ((side, keep_ref), (1 - side, send_ref)):
             rows = rows_of(part, count)
             out_ref[...] = (own[rows, :].astype(F32) + other[rows, :].astype(F32)).astype(BF)
 
 
-def cut_body(bits_ref, own_any, other_any, capacity_ref, first_ref, keep_ref, send_ref, own, other, sems):
-    @pl.when(bits_ref[0] == 1)
+def cut_body(own_any, other_any, capacity_ref, first_ref, keep_ref, send_ref, own, other, sems):
+    @pl.when(bit(0) == 1)
     def _():
         fetch([(own_any, own), (other_any, other)], sems)
-        side = bits_ref[1]
+        side = bit(1)
         width = first_ref.shape[1] - capacity_ref.shape[2]
         first_ref[:, :width] = (own[:, :width].astype(F32) + other[:, :width].astype(F32)).astype(BF)
         first_ref[:, width:] = capacity_ref[0]
@@ -146,10 +130,10 @@
             out_ref[...] = total.astype(BF)
 
 
-def static_body(bits_ref, own_any, other_any, capacity_ref, *refs, cut, width, outs):
+def static_body(own_any, other_any, capacity_ref, *refs, cut, width, outs):
     out_refs, (own, other, sems) = refs[:outs], refs[outs:]
 
-    @pl.when(bits_ref[0] == 1)
+    @pl.when(bit(0) == 1)
     def _():
         fetch([(own_any, own), (other_any, other)], sems)
         count = own.shape[0]
@@ -163,19 +147,19 @@
         if width:
             total = own[:, cut : cut + width].astype(F32) + other[:, cut : cut + width].astype(F32)
             message_ref[:, :width] = total.astype(BF)
-        message_ref[:, width : width + inner] = capacity_ref[0, rows_of(bits_ref[1], count), :]
+        message_ref[:, width : width + inner] = capacity_ref[0, rows_of(bit(1), count), :]
         if own.shape[1] > cut + width:
             rest = own[:, cut + width :].astype(F32) + other[:, cut + width :].astype(F32)
             message_ref[:, width + inner :] = rest.astype(BF)
 
 
-def step_body(bits_ref, own_ref, other_ref, near_ref, far_ref, *out_refs, level):
+def step_body(own_ref, other_ref, near_ref, far_ref, *out_refs, level):
     rank = near_ref.shape[0]
     width = own_ref.shape[1] - rank
 
-    @pl.when(bits_ref[0] == 0)
+    @pl.when(bit(0) == 0)
     def _():
-        lower = bits_ref[level] == 0
+        lower = bit(level) == 0
         own, other = own_ref[:, :rank], other_ref[:, :rank]
         stacked = jnp.concatenate([jnp.where(lower, own, other), jnp.where(lower, other, own)], 1)
         capacity = jnp.concatenate([near_ref[:, width:], far_ref[:, width:]], 0)
@@ -183,7 +167,7 @@
         if level == 1:
             out_refs[0][...] = both
         else:
-            first = bits_ref[1] == 0
+            first = bit(1) == 0
             part = rank // 2
             near, far = both[:, :part], both[:, rank : rank + part]
             out_refs[0][...] = jnp.concatenate([jnp.where(first, near, far), jnp.where(first, far, near)], 1)
@@ -193,11 +177,11 @@
             out_refs[1][...] = (total - dot(both, static, NN)).astype(BF)
 
 
-def spread_body(bits_ref, state_ref, *refs, count, zero):
+def spread_body(state_ref, *refs, count, zero):
     spreads, (near0_ref, far0_ref, near1_ref, far1_ref), rest = refs[:count], refs[count : count + 4], refs[count + 4 :]
     out_ref = rest[-1]
-    zero_core = bits_ref[0] == 0
-    first = bits_ref[1] == 0
+    zero_core = bit(0) == 0
+    first = bit(1) == 0
     total = state_ref[...]
     if zero:
         total = total - dot(rest[0][0], rest[1][...], NN)
@@ -217,26 +201,23 @@
     columns = right_side.shape[1]
     inner = capacity.shape[2]
     size = lax.axis_size(AXIS)
-    device = lax.axis_index(AXIS)
-    bits = (device >> jnp.arange(levels, dtype=jnp.int32) & 1).astype(jnp.int32)
     dma = pltpu.SemaphoreType.DMA
 
     def level_block(array, level):
         return pl.BlockSpec((1,) + array.shape[1:], lambda i: (level, 0, 0))
 
     pairs = (levels - 1) * (levels - 2) // 2
-    static, state, sums = call(
-        front_body,
-        [sds((rank, pairs * rank), BF), sds((samples, columns), F32), sds((rank, columns), BF)],
-        [leaf_inverse, right_side, project_rows, spread_rows],
-        [HBM] * 4,
-        [
-            pltpu.VMEM(leaf_inverse.shape[1:], BF), like(right_side), like(project_rows), like(spread_rows),
-            dma((levels,)), dma((levels,)), dma, dma,
-        ],
-        limit=60,
+    (static,) = call(
+        blocks_body, [sds((rank, pairs * rank), BF)], [project_rows, spread_rows], [VMEM, VMEM]
     )
     static_other = to_core(static, 1)
+    state, sums = call(
+        leaf_body,
+        [sds((samples, columns), F32), sds((rank, columns), BF)],
+        [leaf_inverse, right_side, project_rows],
+        [VMEM, VMEM, level_block(project_rows, 0)],
+    )
+    static_other, sums = lax.optimization_barrier((static_other, sums))
     stacked = lax.all_gather(
         sums, AXIS, axis_index_groups=[[d, d + 1] for d in range(0, size, 2)], tiled=True
     )
@@ -249,8 +230,8 @@
             sds((part, pairs * rank - width), BF),
             sds((part, pairs * rank - width), BF),
         ],
-        [bits, static, static_other, capacity],
-        [SMEM, ANY, ANY, level_block(capacity, 1)],
+        [static, static_other, capacity],
+        [ANY, ANY, level_block(capacity, 1)],
         [like(static), like(static), dma((2,))],
     )
     near, far = to_core(first, 0), to_core(first, 0, 3)
@@ -267,8 +248,8 @@
     own, send = call(
         merge_body,
         [sds((half, (levels - 1) * rank), BF)] * 2,
-        [bits, sums, to_core(sums, 0)],
-        [SMEM, ANY, ANY],
+        [sums, to_core(sums, 0)],
+        [ANY, ANY],
         [like(sums), like(sums), dma((2,))],
     )
 
@@ -285,8 +266,8 @@
             return pl.BlockSpec((1, tile, rank), lambda i: (level, i, 0))
 
         whole = pl.BlockSpec((tile, columns), lambda i: (i, 0))
-        args = [bits, state] + [spread_rows] * count + [near0, far0, near1, far1]
-        specs = [SMEM, whole] + [spread_block(base + i) for i in range(count)] + [VMEM] * 4
+        args = [state] + [spread_rows] * count + [near0, far0, near1, far1]
+        specs = [whole] + [spread_block(base + i) for i in range(count)] + [VMEM] * 4
         if zero is not None:
             args += [spread_rows, zero]
             specs += [spread_block(0), VMEM]
@@ -314,8 +295,8 @@
         results = call(
             lambda *refs, c=cut, w=width, n=len(outs): static_body(*refs, cut=c, width=w, outs=n),
             outs,
-            [bits, message, static_got, capacity],
-            [SMEM, ANY, ANY, level_block(capacity, min(level + 1, levels - 1))],
+            [message, static_got, capacity],
+            [ANY, ANY, level_block(capacity, min(level + 1, levels - 1))],
             [like(message), like(message), dma((2,))],
         )
         if level < levels - 1:
@@ -332,12 +313,13 @@
         results = call(
             lambda *refs, l=level: step_body(*refs, level=l),
             outs,
-            [bits, own, other, near, far],
-            [SMEM, VMEM, VMEM, VMEM, VMEM],
+            [own, other, near, far],
+            [VMEM, VMEM, VMEM, VMEM],
         )
         gathered.append(results[0])
         if width:
-            own = send = results[1]
+            own, static_got = lax.optimization_barrier((results[1], static_got))
+            send = own
         if level == early:
             state = spread_out(state, gathered, 1, zero)
     return spread_out(state, gathered[early:], early + 1, None)

time: 165 us -> 161 us (0.976)
  waiting for transfers between devices: 42.1 us -> 61.3 us
  Pallas kernels: 21.9 us -> 8.4 us
  blocking collectives: 9.17 us -> 1.93 us
  starting transfers between devices: 87.1 us -> 84.5 us
    pallas_call x22 -> x23, Pallas kernels: 21.9 us -> 8.4 us  [call(): pl.pallas_call(body, out_shape=outs, grid=grid, in_specs=specs, out_specs...]
    ppermute x22, waiting for transfers between devices: 18 us -> 29.7 us  [to_core(): return lax.ppermute(value, AXIS, pairs)]
    ppermute x18, waiting for transfers between devices: 24.1 us -> 31.6 us  [swap(): return lax.ppermute(value, AXIS, pairs)]
    all_gather x1, blocking collectives: 9.17 us -> 1.93 us  [on_device(): lax.all_gather(sums, AXIS, axis_index_groups=[[d, d + 1] for d in range(0...]
    ppermute x22, starting transfers between devices: 51.2 us -> 48.8 us  [to_core(): return lax.ppermute(value, AXIS, pairs)]
  transfers between devices with their start and end apart: 40 -> 40, of which waited for: 10 -> 13; matrix products, arithmetic and copies ran while one was open for 0% -> 0% of each run, Pallas kernels for 7% -> 2%
where the time goes in v4:
time: 161 us; the launch traced here: 160 us
  starting transfers between devices  84.5 us (52%)
  waiting for transfers between devices  61.3 us (38%)
  Pallas kernels  8.4 us (5%)
  local copies, waits for them, and re-layouts  3.26 us (2%)
  blocking collectives  1.93 us (1%)
    ppermute x22, starting transfers between devices, to_core(): return lax.ppermute(value, AXIS, pairs)  48.8 us
    ppermute x18, starting transfers between devices, swap(): return lax.ppermute(value, AXIS, pairs)  35.7 us
    ppermute x18, waiting for transfers between devices, swap(): return lax.ppermute(value, AXIS, pairs)  31.6 us
    ppermute x22, waiting for transfers between devices, to_core(): return lax.ppermute(value, AXIS, pairs)  29.7 us
    pallas_call x23, Pallas kernels, call(): pl.pallas_call(body, out_shape=outs, grid=grid, in_specs=specs, out_specs...  8.4 us
    unnamed x19, local copies, waits for them, and re-layouts  3.24 us
  transfers between devices with their start and end apart: 40, of which 13 were waited for; matrix products, arithmetic and copies ran while one was open for 0% of the time, Pallas kernels for 2%

profile of v4, /device:TPU:1, one launch (start us, length us, event | category | flops | bytes accessed | tf_op | source)
XLA Modules:
  0.0 160.2 jit_solution(13459470471735601819)
XLA Ops:
  3.7 1.4 collective-permute-start
  5.8 8.2 %collective-permute-done.other_any = bf16[128,3584]{1,0:T(8,128)(2,1)S(1)} collective-permute-done((bf16[128,3584]{1,0:T(8,128)(2,1)S(1)}, bf16[128,3584]{1,0:T(8,128)(2,1)S(1)}, u32[]{:S(2)}, u32[]{:S(2)}) %collective-permute-start) | collective-permute-done | bytes 917536 | tf_op jit(solution)/shard_map/ppermute | solution.py:25
  14.0 1.9 %all_gather.3.stacked_ref = bf16[256,384]{1,0:T(8,128)(2,1)S(1)} all-gather(bf16[128,384]{1,0:T(8,128)(2,1)S(1)} %get-tuple-element.64), channel_id=1, replica_groups={{0,1},{2,3},{4,5},{6,7},{8,9},{10,11},{12,13},{14,15},{16,17},{18,19},{..., dimensions={0}, use_global_device_ids=true | all-gather | bytes 294912 | tf_op jit(solution)/shard_map/all_gather | solution.py:221
  18.5 2.1 %collective-permute-start.1 = (bf16[384,1024]{1,0:T(8,128)(2,1)S(1)}, bf16[384,1024]{1,0:T(8,128)(2,1)S(1)}, u32[]{:S(2)}, u32[]{:S(2)}) collective-permute-start(bf16[384,1024]{1,0:T(8,128)(2,1)S(1)} %get-tuple-element.68.own_any), channel_id=1, source_target_pairs={{1,0},{3,2},{5,4},{7,6},{9,8},{11,10},{13,12},{15,14},{17,16},{19,... | collective-permute-start | bytes 2359304 | tf_op jit(solution)/shard_map/ppermute | solution.py:25
  20.7 1.8 %collective-permute-done.1.other_any = bf16[384,1024]{1,0:T(8,128)(2,1)S(1)} collective-permute-done((bf16[384,1024]{1,0:T(8,128)(2,1)S(1)}, bf16[384,1024]{1,0:T(8,128)(2,1)S(1)}, u32[]{:S(2)}, u32[]{:S(2)}) %collective-permute-start.1) | collective-permute-done | bytes 786464 | tf_op jit(solution)/shard_map/ppermute | solution.py:25
  23.2 1.9 %collective-permute-start.2 = (bf16[64,2688]{1,0:T(8,128)(2,1)S(1)}, bf16[64,2688]{1,0:T(8,128)(2,1)S(1)}, u32[]{:S(2)}, u32[]{:S(2)}) collective-permute-start(bf16[64,2688]{1,0:T(8,128)(2,1)S(1)} %get-tuple-element.70), channel_id=1, source_target_pairs={{1,3},{3,1},{5,7},{7,5},{9,11},{11,9},{13,15},{15,13},{17,19},{19,... | collective-permute-start | bytes 1032200 | tf_op jit(solution)/shard_map/ppermute | solution.py:20
  25.2 2.6 %collective-permute-start.3 = (bf16[128,1152]{1,0:T(8,128)(2,1)S(1)}, bf16[128,1152]{1,0:T(8,128)(2,1)S(1)}, u32[]{:S(2)}, u32[]{:S(2)}) collective-permute-start(bf16[128,1152]{1,0:T(8,128)(2,1)S(1)} %get-tuple-element.71), channel_id=1, source_target_pairs={{1,0},{3,2},{5,4},{7,6},{9,8},{11,10},{13,12},{15,14},{17,16},{19,... | collective-permute-start | bytes 884744 | tf_op jit(solution)/shard_map/ppermute | solution.py:25
  27.7 2.9 %collective-permute-start.4 = (bf16[128,1152]{1,0:T(8,128)(2,1)S(1)}, bf16[128,1152]{1,0:T(8,128)(2,1)S(1)}, u32[]{:S(2)}, u32[]{:S(2)}) collective-permute-start(bf16[128,1152]{1,0:T(8,128)(2,1)S(1)} %get-tuple-element.71), channel_id=1, source_target_pairs={{3,0},{1,2},{7,4},{5,6},{11,8},{9,10},{15,12},{13,14},{19,16},{17,... | collective-permute-start | bytes 884744 | tf_op jit(solution)/shard_map/ppermute | solution.py:25
  30.7 6.0 %collective-permute-done.4.refs_3_ = bf16[128,1152]{1,0:T(8,128)(2,1)S(1)} collective-permute-done((bf16[128,1152]{1,0:T(8,128)(2,1)S(1)}, bf16[128,1152]{1,0:T(8,128)(2,1)S(1)}, u32[]{:S(2)}, u32[]{:S(2)}) %collective-permute-start.4) | collective-permute-done | bytes 294944 | tf_op jit(solution)/shard_map/ppermute | solution.py:25
  37.1 3.0 %collective-permute-start.6 = (bf16[64,2944]{1,0:T(8,128)(2,1)S(1)}, bf16[64,2944]{1,0:T(8,128)(2,1)S(1)}, u32[]{:S(2)}, u32[]{:S(2)}) collective-permute-start(bf16[64,2944]{1,0:T(8,128)(2,1)S(1)} %shard_map.61.refs_0_), channel_id=1, source_target_pairs={{1,5},{3,7},{5,1},{7,3},{9,13},{11,15},{13,9},{15,11},{17,21},{19,... | collective-permute-start | bytes 1130504 | tf_op jit(solution)/shard_map/ppermute | solution.py:20
  40.1 17.0 %collective-permute-done.6.refs_1_ = bf16[64,2944]{1,0:T(8,128)(2,1)S(1)} collective-permute-done((bf16[64,2944]{1,0:T(8,128)(2,1)S(1)}, bf16[64,2944]{1,0:T(8,128)(2,1)S(1)}, u32[]{:S(2)}, u32[]{:S(2)}) %collective-permute-start.6) | collective-permute-done | bytes 376864 | tf_op jit(solution)/shard_map/ppermute | solution.py:20
  58.1 5.1 %collective-permute-start.10 = (bf16[64,2176]{1,0:T(8,128)(2,1)S(1)}, bf16[64,2176]{1,0:T(8,128)(2,1)S(1)}, u32[]{:S(2)}, u32[]{:S(2)}) collective-permute-start(bf16[64,2176]{1,0:T(8,128)(2,1)S(1)} %get-tuple-element.85.refs_0_), channel_id=1, source_target_pairs={{1,13},{3,15},{5,9},{7,11},{9,5},{11,7},{13,1},{15,3},{17,29},{19,... | collective-permute-start | bytes 835592 | tf_op jit(solution)/shard_map/ppermute | solution.py:20
  65.8 6.2 %collective-permute-done.9.refs_3_ = bf16[128,1024]{1,0:T(8,128)(2,1)S(1)} collective-permute-done((bf16[128,1024]{1,0:T(8,128)(2,1)S(1)}, bf16[128,1024]{1,0:T(8,128)(2,1)S(1)}, u32[]{:S(2)}, u32[]{:S(2)}) %collective-permute-start.9) | collective-permute-done | bytes 262176 | tf_op jit(solution)/shard_map/ppermute | solution.py:25
  72.9 5.2 %collective-permute-start.12 = (bf16[128,896]{1,0:T(8,128)(2,1)S(1)}, bf16[128,896]{1,0:T(8,128)(2,1)S(1)}, u32[]{:S(2)}, u32[]{:S(2)}) collective-permute-start(bf16[128,896]{1,0:T(8,128)(2,1)S(1)} %get-tuple-element.88), channel_id=1, source_target_pairs={{1,0},{3,2},{5,4},{7,6},{9,8},{11,10},{13,12},{15,14},{17,16},{19,... | collective-permute-start | bytes 688136 | tf_op jit(solution)/shard_map/ppermute | solution.py:25
  78.0 2.1 %collective-permute-start.13 = (bf16[128,896]{1,0:T(8,128)(2,1)S(1)}, bf16[128,896]{1,0:T(8,128)(2,1)S(1)}, u32[]{:S(2)}, u32[]{:S(2)}) collective-permute-start(bf16[128,896]{1,0:T(8,128)(2,1)S(1)} %get-tuple-element.88), channel_id=1, source_target_pairs={{3,0},{1,2},{7,4},{5,6},{11,8},{9,10},{15,12},{13,14},{19,16},{17,... | collective-permute-start | bytes 688136 | tf_op jit(solution)/shard_map/ppermute | solution.py:25
  80.1 3.2 %collective-permute-start.14 = (bf16[64,1536]{1,0:T(8,128)(2,1)S(1)}, bf16[64,1536]{1,0:T(8,128)(2,1)S(1)}, u32[]{:S(2)}, u32[]{:S(2)}) collective-permute-start(bf16[64,1536]{1,0:T(8,128)(2,1)S(1)} %get-tuple-element.91.refs_0_), channel_id=1, source_target_pairs={{1,17},{3,19},{5,21},{7,23},{9,25},{11,27},{13,29},{15,31},{17,1},... | collective-permute-start | bytes 589832 | tf_op jit(solution)/shard_map/ppermute | solution.py:20
  83.4 3.1 %collective-permute-done.14.refs_1_ = bf16[64,1536]{1,0:T(8,128)(2,1)S(1)} collective-permute-done((bf16[64,1536]{1,0:T(8,128)(2,1)S(1)}, bf16[64,1536]{1,0:T(8,128)(2,1)S(1)}, u32[]{:S(2)}, u32[]{:S(2)}) %collective-permute-start.14) | collective-permute-done | bytes 196640 | tf_op jit(solution)/shard_map/ppermute | solution.py:20
  87.8 2.8 %collective-permute-start.16 = (bf16[128,768]{1,0:T(8,128)(2,1)S(1)}, bf16[128,768]{1,0:T(8,128)(2,1)S(1)}, u32[]{:S(2)}, u32[]{:S(2)}) collective-permute-start(bf16[128,768]{1,0:T(8,128)(2,1)S(1)} %get-tuple-element.94), channel_id=1, source_target_pairs={{1,0},{3,2},{5,4},{7,6},{9,8},{11,10},{13,12},{15,14},{17,16},{19,... | collective-permute-start | bytes 589832 | tf_op jit(solution)/shard_map/ppermute | solution.py:25
  90.7 5.2 %collective-permute-start.17 = (bf16[128,768]{1,0:T(8,128)(2,1)S(1)}, bf16[128,768]{1,0:T(8,128)(2,1)S(1)}, u32[]{:S(2)}, u32[]{:S(2)}) collective-permute-start(bf16[128,768]{1,0:T(8,128)(2,1)S(1)} %get-tuple-element.94), channel_id=1, source_target_pairs={{3,0},{1,2},{7,4},{5,6},{11,8},{9,10},{15,12},{13,14},{19,16},{17,... | collective-permute-start | bytes 589832 | tf_op jit(solution)/shard_map/ppermute | solution.py:25
  95.9 4.2 %collective-permute-start.18 = (bf16[64,1024]{1,0:T(8,128)(2,1)S(1)}, bf16[64,1024]{1,0:T(8,128)(2,1)S(1)}, u32[]{:S(2)}, u32[]{:S(2)}) collective-permute-start(bf16[64,1024]{1,0:T(8,128)(2,1)S(1)} %get-tuple-element.97.refs_0_), channel_id=1, source_target_pairs={{1,33},{3,35},{5,37},{7,39},{9,41},{11,43},{13,45},{15,47},{17,49}... | collective-permute-start | bytes 393224 | tf_op jit(solution)/shard_map/ppermute | solution.py:20
  100.2 3.6 %collective-permute-done.18.refs_1_ = bf16[64,1024]{1,0:T(8,128)(2,1)S(1)} collective-permute-done((bf16[64,1024]{1,0:T(8,128)(2,1)S(1)}, bf16[64,1024]{1,0:T(8,128)(2,1)S(1)}, u32[]{:S(2)}, u32[]{:S(2)}) %collective-permute-start.18) | collective-permute-done | bytes 131104 | tf_op jit(solution)/shard_map/ppermute | solution.py:20
  107.4 4.1 %collective-permute-start.22 = (bf16[64,640]{1,0:T(8,128)(2,1)S(1)}, bf16[64,640]{1,0:T(8,128)(2,1)S(1)}, u32[]{:S(2)}, u32[]{:S(2)}) collective-permute-start(bf16[64,640]{1,0:T(8,128)(2,1)S(1)} %get-tuple-element.103.refs_0_), channel_id=1, source_target_pairs={{1,97},{3,99},{5,101},{7,103},{9,105},{11,107},{13,109},{15,111},{... | collective-permute-start | bytes 245768 | tf_op jit(solution)/shard_map/ppermute | solution.py:20
  111.7 4.6 %collective-permute-done.22.refs_1_ = bf16[64,640]{1,0:T(8,128)(2,1)S(1)} collective-permute-done((bf16[64,640]{1,0:T(8,128)(2,1)S(1)}, bf16[64,640]{1,0:T(8,128)(2,1)S(1)}, u32[]{:S(2)}, u32[]{:S(2)}) %collective-permute-start.22) | collective-permute-done | bytes 81952 | tf_op jit(solution)/shard_map/ppermute | solution.py:20
  119.7 3.1 %collective-permute-start.29 = (bf16[64,384]{1,0:T(8,128)(2,1)S(1)}, bf16[64,384]{1,0:T(8,128)(2,1)S(1)}, u32[]{:S(2)}, u32[]{:S(2)}) collective-permute-start(bf16[64,384]{1,0:T(8,128)(2,1)S(1)} %get-tuple-element.110.refs_0_), channel_id=1, source_target_pairs={{1,129},{3,131},{5,133},{7,135},{9,137},{11,139},{13,141},{15,143}... | collective-permute-start | bytes 147464 | tf_op jit(solution)/shard_map/ppermute | solution.py:20
  122.9 1.9 %collective-permute-done.29.refs_1_ = bf16[64,384]{1,0:T(8,128)(2,1)S(1)} collective-permute-done((bf16[64,384]{1,0:T(8,128)(2,1)S(1)}, bf16[64,384]{1,0:T(8,128)(2,1)S(1)}, u32[]{:S(2)}, u32[]{:S(2)}) %collective-permute-start.29) | collective-permute-done | bytes 49184 | tf_op jit(solution)/shard_map/ppermute | solution.py:20
  125.0 2.9 %collective-permute-start.31 = (bf16[128,384]{1,0:T(8,128)(2,1)S(1)}, bf16[128,384]{1,0:T(8,128)(2,1)S(1)}, u32[]{:S(2)}, u32[]{:S(2)}) collective-permute-start(bf16[128,384]{1,0:T(8,128)(2,1)S(1)} %get-tuple-element.113), channel_id=1, source_target_pairs={{1,0},{3,2},{5,4},{7,6},{9,8},{11,10},{13,12},{15,14},{17,16},{19,... | collective-permute-start | bytes 294920 | tf_op jit(solution)/shard_map/ppermute | solution.py:25
  127.9 2.5 %collective-permute-start.32 = (bf16[128,384]{1,0:T(8,128)(2,1)S(1)}, bf16[128,384]{1,0:T(8,128)(2,1)S(1)}, u32[]{:S(2)}, u32[]{:S(2)}) collective-permute-start(bf16[128,384]{1,0:T(8,128)(2,1)S(1)} %get-tuple-element.113), channel_id=1, source_target_pairs={{3,0},{1,2},{7,4},{5,6},{11,8},{9,10},{15,12},{13,14},{19,16},{17,... | collective-permute-start | bytes 294920 | tf_op jit(solution)/shard_map/ppermute | solution.py:25
  131.8 4.4 %collective-permute-start.33 = (bf16[64,256]{1,0:T(8,128)(2,1)S(1)}, bf16[64,256]{1,0:T(8,128)(2,1)S(1)}, u32[]{:S(2)}, u32[]{:S(2)}) collective-permute-start(bf16[64,256]{1,0:T(8,128)(2,1)S(1)} %get-tuple-element.116.refs_0_), channel_id=1, source_target_pairs={{1,385},{3,387},{5,389},{7,391},{9,393},{11,395},{13,397},{15,399}... | collective-permute-start | bytes 98312 | tf_op jit(solution)/shard_map/ppermute | solution.py:20
  141.0 4.2 %collective-permute-start.35 = (bf16[128,256]{1,0:T(8,128)(2,1)S(1)}, bf16[128,256]{1,0:T(8,128)(2,1)S(1)}, u32[]{:S(2)}, u32[]{:S(2)}) collective-permute-start(bf16[128,256]{1,0:T(8,128)(2,1)S(1)} %shard_map.75), channel_id=1, source_target_pairs={{1,0},{3,2},{5,4},{7,6},{9,8},{11,10},{13,12},{15,14},{17,16},{19,... | collective-permute-start | bytes 196616 | tf_op jit(solution)/shard_map/ppermute | solution.py:25
  145.2 2.0 %collective-permute-start.36 = (bf16[128,256]{1,0:T(8,128)(2,1)S(1)}, bf16[128,256]{1,0:T(8,128)(2,1)S(1)}, u32[]{:S(2)}, u32[]{:S(2)}) collective-permute-start(bf16[128,256]{1,0:T(8,128)(2,1)S(1)} %shard_map.75), channel_id=1, source_target_pairs={{3,0},{1,2},{7,4},{5,6},{11,8},{9,10},{15,12},{13,14},{19,16},{17,... | collective-permute-start | bytes 196616 | tf_op jit(solution)/shard_map/ppermute | solution.py:25
  152.7 2.8 %collective-permute-done.38.refs_5_ = bf16[2,192,128]{2,1,0:T(8,128)(2,1)S(1)} collective-permute-done((bf16[2,192,128]{2,1,0:T(8,128)(2,1)S(1)}, bf16[2,192,128]{2,1,0:T(8,128)(2,1)S(1)}, u32[]{:S(2)}, u32[]{:S(2)}) %collective-permute-start.38) | collective-permute-done | bytes 98336 | tf_op jit(solution)/shard_map/ppermute | solution.py:25
  155.6 3.3 %collective-permute-done.39.refs_6_ = bf16[2,192,128]{2,1,0:T(8,128)(2,1)S(1)} collective-permute-done((bf16[2,192,128]{2,1,0:T(8,128)(2,1)S(1)}, bf16[2,192,128]{2,1,0:T(8,128)(2,1)S(1)}, u32[]{:S(2)}, u32[]{:S(2)}) %collective-permute-start.39) | collective-permute-done | bytes 98336 | tf_op jit(solution)/shard_map/ppermute | solution.py:25
  (93 shorter events, 34.1 us)
Async XLA Ops:
  3.7 10.3 %collective-permute-start = (bf16[128,3584]{1,0:T(8,128)(2,1)S(1)}, bf16[128,3584]{1,0:T(8,128)(2,1)S(1)}, u32[]{:S(2)}, u32[]{:S(2)}) collective-permute-start(bf16[128,3584]{1,0:T(8,128)(2,1)S(1)} %shard_map.56.own_any), channel_id=1, source_target_pairs={{0,1},{2,3},{4,5},{6,7},{8,9},{10,11},{12,13},{14,15},{16,17},{18,... | collective-permute-start | bytes 2752520 | tf_op jit(solution)/shard_map/ppermute | solution.py:25
  22.5 14.2 %collective-permute-start.5 = (bf16[192,1024]{1,0:T(8,128)(2,1)S(1)}, bf16[192,1024]{1,0:T(8,128)(2,1)S(1)}, u32[]{:S(2)}, u32[]{:S(2)}) collective-permute-start(bf16[192,1024]{1,0:T(8,128)(2,1)S(1)} %get-tuple-element.72), channel_id=1, source_target_pairs={{0,2},{2,0},{4,6},{6,4},{8,10},{10,8},{12,14},{14,12},{16,18},{18,... | collective-permute-start | bytes 1179656 | tf_op jit(solution)/shard_map/ppermute | solution.py:20
  23.2 13.5 %collective-permute-start.2 = (bf16[64,2688]{1,0:T(8,128)(2,1)S(1)}, bf16[64,2688]{1,0:T(8,128)(2,1)S(1)}, u32[]{:S(2)}, u32[]{:S(2)}) collective-permute-start(bf16[64,2688]{1,0:T(8,128)(2,1)S(1)} %get-tuple-element.70), channel_id=1, source_target_pairs={{1,3},{3,1},{5,7},{7,5},{9,11},{11,9},{13,15},{15,13},{17,19},{19,... | collective-permute-start | bytes 1032200 | tf_op jit(solution)/shard_map/ppermute | solution.py:20
  25.2 5.5 %collective-permute-start.3 = (bf16[128,1152]{1,0:T(8,128)(2,1)S(1)}, bf16[128,1152]{1,0:T(8,128)(2,1)S(1)}, u32[]{:S(2)}, u32[]{:S(2)}) collective-permute-start(bf16[128,1152]{1,0:T(8,128)(2,1)S(1)} %get-tuple-element.71), channel_id=1, source_target_pairs={{1,0},{3,2},{5,4},{7,6},{9,8},{11,10},{13,12},{15,14},{17,16},{19,... | collective-permute-start | bytes 884744 | tf_op jit(solution)/shard_map/ppermute | solution.py:25
  27.7 9.0 %collective-permute-start.4 = (bf16[128,1152]{1,0:T(8,128)(2,1)S(1)}, bf16[128,1152]{1,0:T(8,128)(2,1)S(1)}, u32[]{:S(2)}, u32[]{:S(2)}) collective-permute-start(bf16[128,1152]{1,0:T(8,128)(2,1)S(1)} %get-tuple-element.71), channel_id=1, source_target_pairs={{3,0},{1,2},{7,4},{5,6},{11,8},{9,10},{15,12},{13,14},{19,16},{17,... | collective-permute-start | bytes 884744 | tf_op jit(solution)/shard_map/ppermute | solution.py:25
  37.1 20.0 %collective-permute-start.6 = (bf16[64,2944]{1,0:T(8,128)(2,1)S(1)}, bf16[64,2944]{1,0:T(8,128)(2,1)S(1)}, u32[]{:S(2)}, u32[]{:S(2)}) collective-permute-start(bf16[64,2944]{1,0:T(8,128)(2,1)S(1)} %shard_map.61.refs_0_), channel_id=1, source_target_pairs={{1,5},{3,7},{5,1},{7,3},{9,13},{11,15},{13,9},{15,11},{17,21},{19,... | collective-permute-start | bytes 1130504 | tf_op jit(solution)/shard_map/ppermute | solution.py:20
  57.0 15.0 %collective-permute-start.7 = (bf16[192,896]{1,0:T(8,128)(2,1)S(1)}, bf16[192,896]{1,0:T(8,128)(2,1)S(1)}, u32[]{:S(2)}, u32[]{:S(2)}) collective-permute-start(bf16[192,896]{1,0:T(8,128)(2,1)S(1)} %get-tuple-element.80.refs_0_), channel_id=1, source_target_pairs={{0,4},{2,6},{4,0},{6,2},{8,12},{10,14},{12,8},{14,10},{16,20},{18,... | collective-permute-start | bytes 1032200 | tf_op jit(solution)/shard_map/ppermute | solution.py:20
  58.1 13.9 %collective-permute-start.10 = (bf16[64,2176]{1,0:T(8,128)(2,1)S(1)}, bf16[64,2176]{1,0:T(8,128)(2,1)S(1)}, u32[]{:S(2)}, u32[]{:S(2)}) collective-permute-start(bf16[64,2176]{1,0:T(8,128)(2,1)S(1)} %get-tuple-element.85.refs_0_), channel_id=1, source_target_pairs={{1,13},{3,15},{5,9},{7,11},{9,5},{11,7},{13,1},{15,3},{17,29},{19,... | collective-permute-start | bytes 835592 | tf_op jit(solution)/shard_map/ppermute | solution.py:20
  64.5 7.5 %collective-permute-start.9 = (bf16[128,1024]{1,0:T(8,128)(2,1)S(1)}, bf16[128,1024]{1,0:T(8,128)(2,1)S(1)}, u32[]{:S(2)}, u32[]{:S(2)}) collective-permute-start(bf16[128,1024]{1,0:T(8,128)(2,1)S(1)} %get-tuple-element.82), channel_id=1, source_target_pairs={{3,0},{1,2},{7,4},{5,6},{11,8},{9,10},{15,12},{13,14},{19,16},{17,... | collective-permute-start | bytes 786440 | tf_op jit(solution)/shard_map/ppermute | solution.py:25
  72.0 11.4 %collective-permute-start.11 = (bf16[192,768]{1,0:T(8,128)(2,1)S(1)}, bf16[192,768]{1,0:T(8,128)(2,1)S(1)}, u32[]{:S(2)}, u32[]{:S(2)}) collective-permute-start(bf16[192,768]{1,0:T(8,128)(2,1)S(1)} %get-tuple-element.86.refs_0_), channel_id=1, source_target_pairs={{0,12},{2,14},{4,8},{6,10},{8,4},{10,6},{12,0},{14,2},{16,28},{18,... | collective-permute-start | bytes 884744 | tf_op jit(solution)/shard_map/ppermute | solution.py:20
  72.9 10.5 %collective-permute-start.12 = (bf16[128,896]{1,0:T(8,128)(2,1)S(1)}, bf16[128,896]{1,0:T(8,128)(2,1)S(1)}, u32[]{:S(2)}, u32[]{:S(2)}) collective-permute-start(bf16[128,896]{1,0:T(8,128)(2,1)S(1)} %get-tuple-element.88), channel_id=1, source_target_pairs={{1,0},{3,2},{5,4},{7,6},{9,8},{11,10},{13,12},{15,14},{17,16},{19,... | collective-permute-start | bytes 688136 | tf_op jit(solution)/shard_map/ppermute | solution.py:25
  78.0 5.3 %collective-permute-start.13 = (bf16[128,896]{1,0:T(8,128)(2,1)S(1)}, bf16[128,896]{1,0:T(8,128)(2,1)S(1)}, u32[]{:S(2)}, u32[]{:S(2)}) collective-permute-start(bf16[128,896]{1,0:T(8,128)(2,1)S(1)} %get-tuple-element.88), channel_id=1, source_target_pairs={{3,0},{1,2},{7,4},{5,6},{11,8},{9,10},{15,12},{13,14},{19,16},{17,... | collective-permute-start | bytes 688136 | tf_op jit(solution)/shard_map/ppermute | solution.py:25
  80.1 6.4 %collective-permute-start.14 = (bf16[64,1536]{1,0:T(8,128)(2,1)S(1)}, bf16[64,1536]{1,0:T(8,128)(2,1)S(1)}, u32[]{:S(2)}, u32[]{:S(2)}) collective-permute-start(bf16[64,1536]{1,0:T(8,128)(2,1)S(1)} %get-tuple-element.91.refs_0_), channel_id=1, source_target_pairs={{1,17},{3,19},{5,21},{7,23},{9,25},{11,27},{13,29},{15,31},{17,1},... | collective-permute-start | bytes 589832 | tf_op jit(solution)/shard_map/ppermute | solution.py:20
  86.5 13.6 %collective-permute-start.15 = (bf16[192,640]{1,0:T(8,128)(2,1)S(1)}, bf16[192,640]{1,0:T(8,128)(2,1)S(1)}, u32[]{:S(2)}, u32[]{:S(2)}) collective-permute-start(bf16[192,640]{1,0:T(8,128)(2,1)S(1)} %get-tuple-element.92.refs_0_), channel_id=1, source_target_pairs={{0,16},{2,18},{4,20},{6,22},{8,24},{10,26},{12,28},{14,30},{16,0},... | collective-permute-start | bytes 737288 | tf_op jit(solution)/shard_map/ppermute | solution.py:20
  87.8 12.3 %collective-permute-start.16 = (bf16[128,768]{1,0:T(8,128)(2,1)S(1)}, bf16[128,768]{1,0:T(8,128)(2,1)S(1)}, u32[]{:S(2)}, u32[]{:S(2)}) collective-permute-start(bf16[128,768]{1,0:T(8,128)(2,1)S(1)} %get-tuple-element.94), channel_id=1, source_target_pairs={{1,0},{3,2},{5,4},{7,6},{9,8},{11,10},{13,12},{15,14},{17,16},{19,... | collective-permute-start | bytes 589832 | tf_op jit(solution)/shard_map/ppermute | solution.py:25
  90.7 9.5 %collective-permute-start.17 = (bf16[128,768]{1,0:T(8,128)(2,1)S(1)}, bf16[128,768]{1,0:T(8,128)(2,1)S(1)}, u32[]{:S(2)}, u32[]{:S(2)}) collective-permute-start(bf16[128,768]{1,0:T(8,128)(2,1)S(1)} %get-tuple-element.94), channel_id=1, source_target_pairs={{3,0},{1,2},{7,4},{5,6},{11,8},{9,10},{15,12},{13,14},{19,16},{17,... | collective-permute-start | bytes 589832 | tf_op jit(solution)/shard_map/ppermute | solution.py:25
  95.9 7.9 %collective-permute-start.18 = (bf16[64,1024]{1,0:T(8,128)(2,1)S(1)}, bf16[64,1024]{1,0:T(8,128)(2,1)S(1)}, u32[]{:S(2)}, u32[]{:S(2)}) collective-permute-start(bf16[64,1024]{1,0:T(8,128)(2,1)S(1)} %get-tuple-element.97.refs_0_), channel_id=1, source_target_pairs={{1,33},{3,35},{5,37},{7,39},{9,41},{11,43},{13,45},{15,47},{17,49}... | collective-permute-start | bytes 393224 | tf_op jit(solution)/shard_map/ppermute | solution.py:20
  104.1 7.5 %collective-permute-start.20 = (bf16[128,640]{1,0:T(8,128)(2,1)S(1)}, bf16[128,640]{1,0:T(8,128)(2,1)S(1)}, u32[]{:S(2)}, u32[]{:S(2)}) collective-permute-start(bf16[128,640]{1,0:T(8,128)(2,1)S(1)} %get-tuple-element.100), channel_id=1, source_target_pairs={{1,0},{3,2},{5,4},{7,6},{9,8},{11,10},{13,12},{15,14},{17,16},{19,... | collective-permute-start | bytes 491528 | tf_op jit(solution)/shard_map/ppermute | solution.py:25
  105.5 6.2 %collective-permute-start.21 = (bf16[128,640]{1,0:T(8,128)(2,1)S(1)}, bf16[128,640]{1,0:T(8,128)(2,1)S(1)}, u32[]{:S(2)}, u32[]{:S(2)}) collective-permute-start(bf16[128,640]{1,0:T(8,128)(2,1)S(1)} %get-tuple-element.100), channel_id=1, source_target_pairs={{3,0},{1,2},{7,4},{5,6},{11,8},{9,10},{15,12},{13,14},{19,16},{17,... | collective-permute-start | bytes 491528 | tf_op jit(solution)/shard_map/ppermute | solution.py:25
  107.4 8.8 %collective-permute-start.22 = (bf16[64,640]{1,0:T(8,128)(2,1)S(1)}, bf16[64,640]{1,0:T(8,128)(2,1)S(1)}, u32[]{:S(2)}, u32[]{:S(2)}) collective-permute-start(bf16[64,640]{1,0:T(8,128)(2,1)S(1)} %get-tuple-element.103.refs_0_), channel_id=1, source_target_pairs={{1,97},{3,99},{5,101},{7,103},{9,105},{11,107},{13,109},{15,111},{... | collective-permute-start | bytes 245768 | tf_op jit(solution)/shard_map/ppermute | solution.py:20
  116.5 6.4 %collective-permute-start.24 = (bf16[128,512]{1,0:T(8,128)(2,1)S(1)}, bf16[128,512]{1,0:T(8,128)(2,1)S(1)}, u32[]{:S(2)}, u32[]{:S(2)}) collective-permute-start(bf16[128,512]{1,0:T(8,128)(2,1)S(1)} %get-tuple-element.106), channel_id=1, source_target_pairs={{1,0},{3,2},{5,4},{7,6},{9,8},{11,10},{13,12},{15,14},{17,16},{19,... | collective-permute-start | bytes 393224 | tf_op jit(solution)/shard_map/ppermute | solution.py:25
  125.0 11.2 %collective-permute-start.31 = (bf16[128,384]{1,0:T(8,128)(2,1)S(1)}, bf16[128,384]{1,0:T(8,128)(2,1)S(1)}, u32[]{:S(2)}, u32[]{:S(2)}) collective-permute-start(bf16[128,384]{1,0:T(8,128)(2,1)S(1)} %get-tuple-element.113), channel_id=1, source_target_pairs={{1,0},{3,2},{5,4},{7,6},{9,8},{11,10},{13,12},{15,14},{17,16},{19,... | collective-permute-start | bytes 294920 | tf_op jit(solution)/shard_map/ppermute | solution.py:25
  127.9 8.3 %collective-permute-start.32 = (bf16[128,384]{1,0:T(8,128)(2,1)S(1)}, bf16[128,384]{1,0:T(8,128)(2,1)S(1)}, u32[]{:S(2)}, u32[]{:S(2)}) collective-permute-start(bf16[128,384]{1,0:T(8,128)(2,1)S(1)} %get-tuple-element.113), channel_id=1, source_target_pairs={{3,0},{1,2},{7,4},{5,6},{11,8},{9,10},{15,12},{13,14},{19,16},{17,... | collective-permute-start | bytes 294920 | tf_op jit(solution)/shard_map/ppermute | solution.py:25
  130.4 5.8 %collective-permute-start.30 = (bf16[192,256]{1,0:T(8,128)(2,1)S(1)}, bf16[192,256]{1,0:T(8,128)(2,1)S(1)}, u32[]{:S(2)}, u32[]{:S(2)}) collective-permute-start(bf16[192,256]{1,0:T(8,128)(2,1)S(1)} %get-tuple-element.111.refs_0_), channel_id=1, source_target_pairs={{0,128},{2,130},{4,132},{6,134},{8,136},{10,138},{12,140},{14,142}... | collective-permute-start | bytes 294920 | tf_op jit(solution)/shard_map/ppermute | solution.py:20
  131.1 19.4 %collective-permute-start.26 = (bf16[6,192,128]{2,1,0:T(8,128)(2,1)S(1)}, bf16[6,192,128]{2,1,0:T(8,128)(2,1)S(1)}, u32[]{:S(2)}, u32[]{:S(2)}) collective-permute-start(bf16[6,192,128]{2,1,0:T(8,128)(2,1)S(1)} %get-tuple-element.121), channel_id=1, source_target_pairs={{0,2},{2,0},{4,6},{6,4},{8,10},{10,8},{12,14},{14,12},{16,18},{18,... | collective-permute-start | bytes 884744 | tf_op jit(solution)/shard_map/ppermute | solution.py:20
  131.8 5.9 %collective-permute-start.33 = (bf16[64,256]{1,0:T(8,128)(2,1)S(1)}, bf16[64,256]{1,0:T(8,128)(2,1)S(1)}, u32[]{:S(2)}, u32[]{:S(2)}) collective-permute-start(bf16[64,256]{1,0:T(8,128)(2,1)S(1)} %get-tuple-element.116.refs_0_), channel_id=1, source_target_pairs={{1,385},{3,387},{5,389},{7,391},{9,393},{11,395},{13,397},{15,399}... | collective-permute-start | bytes 98312 | tf_op jit(solution)/shard_map/ppermute | solution.py:20
  137.7 7.5 %collective-permute-start.34 = (bf16[192,128]{1,0:T(8,128)(2,1)S(1)}, bf16[192,128]{1,0:T(8,128)(2,1)S(1)}, u32[]{:S(2)}, u32[]{:S(2)}) collective-permute-start(bf16[192,128]{1,0:T(8,128)(2,1)S(1)} %get-tuple-element.117.refs_0_), channel_id=1, source_target_pairs={{0,384},{2,386},{4,388},{6,390},{8,392},{10,394},{12,396},{14,398}... | collective-permute-start | bytes 147464 | tf_op jit(solution)/shard_map/ppermute | solution.py:20
  138.3 13.5 %collective-permute-start.27 = (bf16[6,192,128]{2,1,0:T(8,128)(2,1)S(1)}, bf16[6,192,128]{2,1,0:T(8,128)(2,1)S(1)}, u32[]{:S(2)}, u32[]{:S(2)}) collective-permute-start(bf16[6,192,128]{2,1,0:T(8,128)(2,1)S(1)} %get-tuple-element.122.refs_7_), channel_id=1, source_target_pairs={{0,1},{2,3},{4,5},{6,7},{8,9},{10,11},{12,13},{14,15},{16,17},{18,... | collective-permute-start | bytes 884744 | tf_op jit(solution)/shard_map/ppermute | solution.py:25
  139.6 12.2 %collective-permute-start.28 = (bf16[6,192,128]{2,1,0:T(8,128)(2,1)S(1)}, bf16[6,192,128]{2,1,0:T(8,128)(2,1)S(1)}, u32[]{:S(2)}, u32[]{:S(2)}) collective-permute-start(bf16[6,192,128]{2,1,0:T(8,128)(2,1)S(1)} %get-tuple-element.121), channel_id=1, source_target_pairs={{2,1},{0,3},{6,5},{4,7},{10,9},{8,11},{14,13},{12,15},{18,17},{16,... | collective-permute-start | bytes 884744 | tf_op jit(solution)/shard_map/ppermute | solution.py:25
  141.0 6.2 %collective-permute-start.35 = (bf16[128,256]{1,0:T(8,128)(2,1)S(1)}, bf16[128,256]{1,0:T(8,128)(2,1)S(1)}, u32[]{:S(2)}, u32[]{:S(2)}) collective-permute-start(bf16[128,256]{1,0:T(8,128)(2,1)S(1)} %shard_map.75), channel_id=1, source_target_pairs={{1,0},{3,2},{5,4},{7,6},{9,8},{11,10},{13,12},{15,14},{17,16},{19,... | collective-permute-start | bytes 196616 | tf_op jit(solution)/shard_map/ppermute | solution.py:25
  149.2 6.4 %collective-permute-start.38 = (bf16[2,192,128]{2,1,0:T(8,128)(2,1)S(1)}, bf16[2,192,128]{2,1,0:T(8,128)(2,1)S(1)}, u32[]{:S(2)}, u32[]{:S(2)}) collective-permute-start(bf16[2,192,128]{2,1,0:T(8,128)(2,1)S(1)} %pad_maximum_fusion.refs_3_), channel_id=1, source_target_pairs={{0,1},{2,3},{4,5},{6,7},{8,9},{10,11},{12,13},{14,15},{16,17},{18,... | collective-permute-start | bytes 294920 | tf_op jit(solution)/shard_map/ppermute | solution.py:25
  150.5 8.4 %collective-permute-start.39 = (bf16[2,192,128]{2,1,0:T(8,128)(2,1)S(1)}, bf16[2,192,128]{2,1,0:T(8,128)(2,1)S(1)}, u32[]{:S(2)}, u32[]{:S(2)}) collective-permute-start(bf16[2,192,128]{2,1,0:T(8,128)(2,1)S(1)} %pad_maximum_fusion.refs_3_), channel_id=1, source_target_pairs={{2,1},{0,3},{6,5},{4,7},{10,9},{8,11},{14,13},{12,15},{18,17},{16,... | collective-permute-start | bytes 294920 | tf_op jit(solution)/shard_map/ppermute | solution.py:25
  (15 other events, 57.0 us)

commit v5 on v4

--- a/solution.py
+++ b/solution.py
@@ -115,22 +115,27 @@
             out_ref[...] = (own[rows, :].astype(F32) + other[rows, :].astype(F32)).astype(BF)
 
 
-def cut_body(own_any, other_any, capacity_ref, first_ref, keep_ref, send_ref, own, other, sems):
+def cut_body(own_any, other_any, capacity_ref, message_ref, keep_ref, own, other, sems, *, first, last):
     @pl.when(bit(0) == 1)
     def _():
         fetch([(own_any, own), (other_any, other)], sems)
-        side = bit(1)
-        width = first_ref.shape[1] - capacity_ref.shape[2]
-        first_ref[:, :width] = (own[:, :width].astype(F32) + other[:, :width].astype(F32)).astype(BF)
-        first_ref[:, width:] = capacity_ref[0]
-        count = keep_ref.shape[0]
-        for part, out_ref in ((side, keep_ref), (1 - side, send_ref)):
-            rows = rows_of(part, count)
-            total = own[rows, width:].astype(F32) + other[rows, width:].astype(F32)
-            out_ref[...] = total.astype(BF)
-
-
-def static_body(own_any, other_any, capacity_ref, *refs, cut, width, outs):
+        inner = capacity_ref.shape[2]
+        count = own.shape[0] // 2
+        part = (own.shape[1] - last) // 2
+
+        def total(rows, low, high):
+            return (own[rows, low:high].astype(F32) + other[rows, low:high].astype(F32)).astype(BF)
+
+        message_ref[:, :first] = total(slice(None), 0, first)
+        message_ref[:, first : first + inner] = capacity_ref[0]
+        message_ref[:, first + inner : last + inner] = total(slice(None), first, last)
+        for place, out_ref, at in ((bit(1), keep_ref, 0), (1 - bit(1), message_ref, last + inner)):
+            rows = rows_of(place, count)
+            out_ref[:count, at:] = total(rows, last, last + part)
+            out_ref[count:, at:] = total(rows, last + part, last + 2 * part)
+
+
+def static_body(own_any, other_any, keep_ref, capacity_ref, *refs, cut, width, outs, kept, plain):
     out_refs, (own, other, sems) = refs[:outs], refs[outs:]
 
     @pl.when(bit(0) == 1)
@@ -138,23 +143,50 @@
         fetch([(own_any, own), (other_any, other)], sems)
         count = own.shape[0]
         inner = capacity_ref.shape[2]
-        if cut:
-            out_refs[0][:count, :] = own[:, :cut]
-            out_refs[0][count:, :] = other[:, :cut]
-        if outs == 1 and cut:
+        out_refs[0][:count, :] = own[:, :cut]
+        out_refs[0][count:, :] = other[:, :cut]
+        if outs == 1:
             return
-        message_ref = out_refs[-1]
+        message_ref = out_refs[1]
+
+        def total(low, high):
+            return (own[:, low:high].astype(F32) + other[:, low:high].astype(F32)).astype(BF)
+
+        if plain:
+            message_ref[...] = total(cut, own.shape[1])
+            return
         if width:
-            total = own[:, cut : cut + width].astype(F32) + other[:, cut : cut + width].astype(F32)
-            message_ref[:, :width] = total.astype(BF)
-        message_ref[:, width : width + inner] = capacity_ref[0, rows_of(bit(1), count), :]
-        if own.shape[1] > cut + width:
-            rest = own[:, cut + width :].astype(F32) + other[:, cut + width :].astype(F32)
-            message_ref[:, width + inner :] = rest.astype(BF)
-
-
-def step_body(own_ref, other_ref, near_ref, far_ref, *out_refs, level):
-    rank = near_ref.shape[0]
+            message_ref[:, :width] = total(cut, cut + width)
+        message_ref[:, width : width + inner] = capacity_ref[0]
+        end = own.shape[1] - kept
+        if end > cut + width:
+            message_ref[:, width + inner : end - cut + inner] = total(cut + width, end)
+        if kept:
+            rest = keep_ref[...].astype(F32) + other[:, end:].astype(F32)
+            message_ref[:, end - cut + inner :] = rest.astype(BF)
+
+
+def join_body(own_ref, other_ref, capacity_ref, message_ref, *, width):
+    @pl.when(bit(0) == 1)
+    def _():
+        inner = capacity_ref.shape[2]
+        part = own_ref.shape[1]
+        count = own_ref.shape[0] // 2
+        message_ref[:, width : width + inner] = capacity_ref[0]
+        for place, ref in ((bit(1), own_ref), (1 - bit(1), other_ref)):
+            rows = rows_of(place, count)
+            for half in range(2):
+                low, high = half * part, (half + 1) * part
+                middle = min(max(low, width), high)
+                block = ref[half * count : (half + 1) * count, :]
+                if middle > low:
+                    message_ref[rows, low:middle] = block[:, : middle - low]
+                if high > middle:
+                    message_ref[rows, middle + inner : high + inner] = block[:, middle - low :]
+
+
+def step_body(own_ref, other_ref, static_ref, *out_refs, level):
+    rank = static_ref.shape[0] // 2
     width = own_ref.shape[1] - rank
 
     @pl.when(bit(0) == 0)
@@ -162,19 +194,11 @@
         lower = bit(level) == 0
         own, other = own_ref[:, :rank], other_ref[:, :rank]
         stacked = jnp.concatenate([jnp.where(lower, own, other), jnp.where(lower, other, own)], 1)
-        capacity = jnp.concatenate([near_ref[:, width:], far_ref[:, width:]], 0)
-        both = dot(stacked, capacity, NT).astype(BF)
-        if level == 1:
-            out_refs[0][...] = both
-        else:
-            first = bit(1) == 0
-            part = rank // 2
-            near, far = both[:, :part], both[:, rank : rank + part]
-            out_refs[0][...] = jnp.concatenate([jnp.where(first, near, far), jnp.where(first, far, near)], 1)
+        both = dot(stacked, static_ref[:, width:], NT).astype(BF)
+        out_refs[0][...] = both[:, : out_refs[0].shape[1]]
         if width:
             total = own_ref[:, rank:].astype(F32) + other_ref[:, rank:].astype(F32)
-            static = jnp.concatenate([near_ref[:, :width], far_ref[:, :width]], 0)
-            out_refs[1][...] = (total - dot(both, static, NN)).astype(BF)
+            out_refs[1][...] = (total - dot(both, static_ref[:, :width], NN)).astype(BF)
 
 
 def spread_body(state_ref, *refs, count, zero):
@@ -221,23 +245,20 @@
     stacked = lax.all_gather(
         sums, AXIS, axis_index_groups=[[d, d + 1] for d in range(0, size, 2)], tiled=True
     )
-    width = (levels - 2) * rank
-    part = rank // 2
-    first, keep, send = call(
-        cut_body,
-        [
-            sds((rank, width + inner), BF),
-            sds((part, pairs * rank - width), BF),
-            sds((part, pairs * rank - width), BF),
-        ],
+    def blocks(low, high):
+        return sum(levels - 1 - level for level in range(low, min(high, levels - 1))) * rank
+
+    split = 4
+    rest = blocks(split, levels) // 2
+    message, keep = call(
+        lambda *refs: cut_body(*refs, first=blocks(1, 2), last=blocks(1, split)),
+        [sds((rank, blocks(1, split) + inner + rest), BF), sds((rank, rest), BF)],
         [static, static_other, capacity],
         [ANY, ANY, level_block(capacity, 1)],
         [like(static), like(static), dma((2,))],
     )
-    near, far = to_core(first, 0), to_core(first, 0, 3)
-
-    stacked, send = lax.optimization_barrier((stacked, send))
-    static_got = swap(send, 2, 1)
+    stacked, message = lax.optimization_barrier((stacked, message))
+    static_got = swap(message, mask_of(1), 1)
     zero, sums = call(
         first_body,
         [sds((rank, columns), BF), sds((columns, (levels - 1) * rank), BF)],
@@ -282,29 +303,37 @@
 
     gathered = []
     early = levels - 3
-    message, cut = keep, 0
     for level in range(1, levels):
         other = swap(send, mask_of(level), 0)
-        if level == 1:
-            static_got, near, far, other = lax.optimization_barrier((static_got, near, far, other))
-        width = max(levels - 2 - level, 0) * rank
-        total = message.shape[1] - cut + inner
-        outs = [sds((rank, cut), BF)] if cut else []
-        if level < levels - 1:
-            outs.append(sds((part, total), BF))
+        plain = level == split - 1 and rest > 0
+        outs = [sds((2 * rank, blocks(level, level + 1) + inner), BF)]
+        if plain:
+            outs.append(sds((rank, rest), BF))
+        elif level < levels - 1:
+            late = rest if level < split else blocks(level + 2, levels)
+            outs.append(sds((rank, blocks(level + 1, max(split, level + 2) if level < split else level + 2) + inner + late), BF))
         results = call(
-            lambda *refs, c=cut, w=width, n=len(outs): static_body(*refs, cut=c, width=w, outs=n),
+            lambda *refs, l=level, n=len(outs), p=plain: static_body(
+                *refs, cut=blocks(l, l + 1) + inner, width=blocks(l + 1, l + 2), outs=n, kept=rest if l == 1 else 0, plain=p
+            ),
             outs,
-            [message, static_got, capacity],
-            [ANY, ANY, level_block(capacity, min(level + 1, levels - 1))],
+            [message, static_got, keep, capacity],
+            [ANY, ANY, VMEM, level_block(capacity, min(level + 1, levels - 1))],
             [like(message), like(message), dma((2,))],
         )
+        both = results[0]
+        static_block = to_core(both, 0)
+        if plain:
+            (message,) = call(
+                lambda *refs: join_body(*refs, width=blocks(split, split + 1)),
+                [sds((rank, 2 * rest + inner), BF)],
+                [results[1], swap(results[1], 2, 1), capacity],
+                [VMEM, VMEM, level_block(capacity, split)],
+            )
+        elif level < levels - 1:
+            message = results[1]
         if level < levels - 1:
-            message = results[-1]
             static_got = swap(message, mask_of(level + 1), 1)
-        if level > 1:
-            near, far = to_core(results[0], 0), to_core(results[0], 0, 3)
-        cut = width + inner
 
         width = (levels - 1 - level) * rank
         outs = [sds((half, 2 * rank if level == 1 else rank), BF)]
@@ -313,12 +342,12 @@
         results = call(
             lambda *refs, l=level: step_body(*refs, level=l),
             outs,
-            [own, other, near, far],
-            [VMEM, VMEM, VMEM, VMEM],
+            [own, other, static_block],
+            [VMEM, VMEM, VMEM],
         )
         gathered.append(results[0])
         if width:
-            own, static_got = lax.optimization_barrier((results[1], static_got))
+            own = results[1]
             send = own
         if level == early:
             state = spread_out(state, gathered, 1, zero)

time: 161 us -> 150 us (0.932)
  starting transfers between devices: 84.5 us -> 51.9 us
  waiting for transfers between devices: 61.3 us -> 83.3 us
    ppermute x22 -> x14, starting transfers between devices: 48.8 us -> 18.4 us  [to_core(): return lax.ppermute(value, AXIS, pairs)]
    ppermute x18 -> x19, waiting for transfers between devices: 31.6 us -> 61.3 us  [swap(): return lax.ppermute(value, AXIS, pairs)]
    ppermute x22 -> x14, waiting for transfers between devices: 29.7 us -> 22 us  [to_core(): return lax.ppermute(value, AXIS, pairs)]
    ppermute x18 -> x19, starting transfers between devices: 35.7 us -> 33.5 us  [swap(): return lax.ppermute(value, AXIS, pairs)]
    pallas_call x23 -> x24, Pallas kernels: 8.4 us -> 8.8 us  [call(): pl.pallas_call(body, out_shape=outs, grid=grid, in_specs=specs, out_specs...]
  transfers between devices with their start and end apart: 40 -> 33, of which waited for: 13 -> 13; matrix products, arithmetic and copies ran while one was open for 0% -> 0% of each run, Pallas kernels for 2% -> 4%
where the time goes in v5:
time: 150 us; the launch traced here: 149 us
  waiting for transfers between devices  83.3 us (56%)
  starting transfers between devices  51.9 us (35%)
  Pallas kernels  8.8 us (6%)
  local copies, waits for them, and re-layouts  2.67 us (2%)
  blocking collectives  1.93 us (1%)
    ppermute x19, waiting for transfers between devices, swap(): return lax.ppermute(value, AXIS, pairs)  61.3 us
    ppermute x19, starting transfers between devices, swap(): return lax.ppermute(value, AXIS, pairs)  33.5 us
    ppermute x14, waiting for transfers between devices, to_core(): return lax.ppermute(value, AXIS, pairs)  22 us
    ppermute x14, starting transfers between devices, to_core(): return lax.ppermute(value, AXIS, pairs)  18.4 us
    pallas_call x24, Pallas kernels, call(): pl.pallas_call(body, out_shape=outs, grid=grid, in_specs=specs, out_specs...  8.8 us
  transfers between devices with their start and end apart: 33, of which 13 were waited for; matrix products, arithmetic and copies ran while one was open for 0% of the time, Pallas kernels for 4%

profile of v5, /device:TPU:1, one launch (start us, length us, event | category | flops | bytes accessed | tf_op | source)
XLA Modules:
  0.0 149.3 jit_solution(7957216717230877020)
XLA Ops:
  3.7 1.4 collective-permute-start
  5.8 8.2 %collective-permute-done.refs_1_ = bf16[128,3584]{1,0:T(8,128)(2,1)S(1)} collective-permute-done((bf16[128,3584]{1,0:T(8,128)(2,1)S(1)}, bf16[128,3584]{1,0:T(8,128)(2,1)S(1)}, u32[]{:S(2)}, u32[]{:S(2)}) %collective-permute-start) | collective-permute-done | bytes 917536 | tf_op jit(solution)/shard_map/ppermute | solution.py:25
  14.0 1.9 %all_gather.3.stacked_ref = bf16[256,384]{1,0:T(8,128)(2,1)S(1)} all-gather(bf16[128,384]{1,0:T(8,128)(2,1)S(1)} %get-tuple-element.47), channel_id=1, replica_groups={{0,1},{2,3},{4,5},{6,7},{8,9},{10,11},{12,13},{14,15},{16,17},{18,19},{..., dimensions={0}, use_global_device_ids=true | all-gather | bytes 294912 | tf_op jit(solution)/shard_map/all_gather | solution.py:245
  16.6 1.9 %collective-permute-start.3 = (bf16[128,3200]{1,0:T(8,128)(2,1)S(1)}, bf16[128,3200]{1,0:T(8,128)(2,1)S(1)}, u32[]{:S(2)}, u32[]{:S(2)}) collective-permute-start(bf16[128,3200]{1,0:T(8,128)(2,1)S(1)} %get-tuple-element.54.refs_0_), channel_id=1, source_target_pairs={{1,3},{3,1},{5,7},{7,5},{9,11},{11,9},{13,15},{15,13},{17,19},{19,... | collective-permute-start | bytes 2457608 | tf_op jit(solution)/shard_map/ppermute | solution.py:20
  18.5 1.4 shard_map.58
  19.9 1.3 collective-permute-start.1
  21.2 9.8 %collective-permute-done.3.refs_1_ = bf16[128,3200]{1,0:T(8,128)(2,1)S(1)} collective-permute-done((bf16[128,3200]{1,0:T(8,128)(2,1)S(1)}, bf16[128,3200]{1,0:T(8,128)(2,1)S(1)}, u32[]{:S(2)}, u32[]{:S(2)}) %collective-permute-start.3) | collective-permute-done | bytes 819232 | tf_op jit(solution)/shard_map/ppermute | solution.py:20
  31.4 1.9 %collective-permute-start.6 = (bf16[128,2304]{1,0:T(8,128)(2,1)S(1)}, bf16[128,2304]{1,0:T(8,128)(2,1)S(1)}, u32[]{:S(2)}, u32[]{:S(2)}) collective-permute-start(bf16[128,2304]{1,0:T(8,128)(2,1)S(1)} %get-tuple-element.59.refs_0_), channel_id=1, source_target_pairs={{1,5},{3,7},{5,1},{7,3},{9,13},{11,15},{13,9},{15,11},{17,21},{19,... | collective-permute-start | bytes 1769480 | tf_op jit(solution)/shard_map/ppermute | solution.py:20
  33.4 1.3 collective-permute-start.4
  34.7 20.9 %collective-permute-done.6.refs_1_ = bf16[128,2304]{1,0:T(8,128)(2,1)S(1)} collective-permute-done((bf16[128,2304]{1,0:T(8,128)(2,1)S(1)}, bf16[128,2304]{1,0:T(8,128)(2,1)S(1)}, u32[]{:S(2)}, u32[]{:S(2)}) %collective-permute-start.6) | collective-permute-done | bytes 589856 | tf_op jit(solution)/shard_map/ppermute | solution.py:20
  56.0 2.9 %collective-permute-start.9 = (bf16[128,1536]{1,0:T(8,128)(2,1)S(1)}, bf16[128,1536]{1,0:T(8,128)(2,1)S(1)}, u32[]{:S(2)}, u32[]{:S(2)}) collective-permute-start(bf16[128,1536]{1,0:T(8,128)(2,1)S(1)} %get-tuple-element.63.refs_0_), channel_id=1, source_target_pairs={{1,13},{3,15},{5,9},{7,11},{9,5},{11,7},{13,1},{15,3},{17,29},{19,... | collective-permute-start | bytes 1179656 | tf_op jit(solution)/shard_map/ppermute | solution.py:20
  59.7 1.3 collective-permute-start.7
  61.0 6.8 %collective-permute-done.9.refs_1_ = bf16[128,1536]{1,0:T(8,128)(2,1)S(1)} collective-permute-done((bf16[128,1536]{1,0:T(8,128)(2,1)S(1)}, bf16[128,1536]{1,0:T(8,128)(2,1)S(1)}, u32[]{:S(2)}, u32[]{:S(2)}) %collective-permute-start.9) | collective-permute-done | bytes 393248 | tf_op jit(solution)/shard_map/ppermute | solution.py:20
  68.3 10.0 %collective-permute-start.12 = (bf16[128,640]{1,0:T(8,128)(2,1)S(1)}, bf16[128,640]{1,0:T(8,128)(2,1)S(1)}, u32[]{:S(2)}, u32[]{:S(2)}) collective-permute-start(bf16[128,640]{1,0:T(8,128)(2,1)S(1)} %get-tuple-element.67.refs_0_), channel_id=1, source_target_pairs={{1,3},{3,1},{5,7},{7,5},{9,11},{11,9},{13,15},{15,13},{17,19},{19,... | collective-permute-start | bytes 491528 | tf_op jit(solution)/shard_map/ppermute | solution.py:20
  79.1 2.0 %collective-permute-done.12.refs_1_ = bf16[128,640]{1,0:T(8,128)(2,1)S(1)} collective-permute-done((bf16[128,640]{1,0:T(8,128)(2,1)S(1)}, bf16[128,640]{1,0:T(8,128)(2,1)S(1)}, u32[]{:S(2)}, u32[]{:S(2)}) %collective-permute-start.12) | collective-permute-done | bytes 163872 | tf_op jit(solution)/shard_map/ppermute | solution.py:20
  81.1 1.9 %collective-permute-start.13 = (bf16[128,1536]{1,0:T(8,128)(2,1)S(1)}, bf16[128,1536]{1,0:T(8,128)(2,1)S(1)}, u32[]{:S(2)}, u32[]{:S(2)}) collective-permute-start(bf16[128,1536]{1,0:T(8,128)(2,1)S(1)} %shard_map.66.refs_0_), channel_id=1, source_target_pairs={{1,17},{3,19},{5,21},{7,23},{9,25},{11,27},{13,29},{15,31},{17,1},... | collective-permute-start | bytes 1179656 | tf_op jit(solution)/shard_map/ppermute | solution.py:20
  83.0 1.3 collective-permute-start.10
  85.1 4.5 %collective-permute-done.13.refs_1_ = bf16[128,1536]{1,0:T(8,128)(2,1)S(1)} collective-permute-done((bf16[128,1536]{1,0:T(8,128)(2,1)S(1)}, bf16[128,1536]{1,0:T(8,128)(2,1)S(1)}, u32[]{:S(2)}, u32[]{:S(2)}) %collective-permute-start.13) | collective-permute-done | bytes 393248 | tf_op jit(solution)/shard_map/ppermute | solution.py:20
  90.1 1.9 %collective-permute-start.16 = (bf16[128,1024]{1,0:T(8,128)(2,1)S(1)}, bf16[128,1024]{1,0:T(8,128)(2,1)S(1)}, u32[]{:S(2)}, u32[]{:S(2)}) collective-permute-start(bf16[128,1024]{1,0:T(8,128)(2,1)S(1)} %get-tuple-element.71.refs_0_), channel_id=1, source_target_pairs={{1,33},{3,35},{5,37},{7,39},{9,41},{11,43},{13,45},{15,47},{17,49}... | collective-permute-start | bytes 786440 | tf_op jit(solution)/shard_map/ppermute | solution.py:20
  92.8 1.3 collective-permute-start.14
  94.1 6.5 %collective-permute-done.16.refs_1_ = bf16[128,1024]{1,0:T(8,128)(2,1)S(1)} collective-permute-done((bf16[128,1024]{1,0:T(8,128)(2,1)S(1)}, bf16[128,1024]{1,0:T(8,128)(2,1)S(1)}, u32[]{:S(2)}, u32[]{:S(2)}) %collective-permute-start.16) | collective-permute-done | bytes 262176 | tf_op jit(solution)/shard_map/ppermute | solution.py:20
  100.8 1.3 collective-permute-start.17
  102.1 1.9 %collective-permute-start.19 = (bf16[128,640]{1,0:T(8,128)(2,1)S(1)}, bf16[128,640]{1,0:T(8,128)(2,1)S(1)}, u32[]{:S(2)}, u32[]{:S(2)}) collective-permute-start(bf16[128,640]{1,0:T(8,128)(2,1)S(1)} %get-tuple-element.75.refs_0_), channel_id=1, source_target_pairs={{1,97},{3,99},{5,101},{7,103},{9,105},{11,107},{13,109},{15,111},{... | collective-permute-start | bytes 491528 | tf_op jit(solution)/shard_map/ppermute | solution.py:20
  104.8 5.5 %collective-permute-done.19.refs_1_ = bf16[128,640]{1,0:T(8,128)(2,1)S(1)} collective-permute-done((bf16[128,640]{1,0:T(8,128)(2,1)S(1)}, bf16[128,640]{1,0:T(8,128)(2,1)S(1)}, u32[]{:S(2)}, u32[]{:S(2)}) %collective-permute-start.19) | collective-permute-done | bytes 163872 | tf_op jit(solution)/shard_map/ppermute | solution.py:20
  110.7 1.3 collective-permute-start.20
  112.0 1.9 %collective-permute-start.25 = (bf16[128,384]{1,0:T(8,128)(2,1)S(1)}, bf16[128,384]{1,0:T(8,128)(2,1)S(1)}, u32[]{:S(2)}, u32[]{:S(2)}) collective-permute-start(bf16[128,384]{1,0:T(8,128)(2,1)S(1)} %get-tuple-element.80.refs_0_), channel_id=1, source_target_pairs={{1,129},{3,131},{5,133},{7,135},{9,137},{11,139},{13,141},{15,143}... | collective-permute-start | bytes 294920 | tf_op jit(solution)/shard_map/ppermute | solution.py:20
  114.0 3.4 %collective-permute-done.25.refs_1_ = bf16[128,384]{1,0:T(8,128)(2,1)S(1)} collective-permute-done((bf16[128,384]{1,0:T(8,128)(2,1)S(1)}, bf16[128,384]{1,0:T(8,128)(2,1)S(1)}, u32[]{:S(2)}, u32[]{:S(2)}) %collective-permute-start.25) | collective-permute-done | bytes 98336 | tf_op jit(solution)/shard_map/ppermute | solution.py:20
  119.0 2.2 %collective-permute-start.28 = (bf16[128,256]{1,0:T(8,128)(2,1)S(1)}, bf16[128,256]{1,0:T(8,128)(2,1)S(1)}, u32[]{:S(2)}, u32[]{:S(2)}) collective-permute-start(bf16[128,256]{1,0:T(8,128)(2,1)S(1)} %get-tuple-element.84.refs_0_), channel_id=1, source_target_pairs={{1,385},{3,387},{5,389},{7,391},{9,393},{11,395},{13,397},{15,399}... | collective-permute-start | bytes 196616 | tf_op jit(solution)/shard_map/ppermute | solution.py:20
  123.4 1.8 %collective-permute-done.28.refs_1_ = bf16[128,256]{1,0:T(8,128)(2,1)S(1)} collective-permute-done((bf16[128,256]{1,0:T(8,128)(2,1)S(1)}, bf16[128,256]{1,0:T(8,128)(2,1)S(1)}, u32[]{:S(2)}, u32[]{:S(2)}) %collective-permute-start.28) | collective-permute-done | bytes 65568 | tf_op jit(solution)/shard_map/ppermute | solution.py:20
  133.3 2.8 %collective-permute-done.23.refs_10_ = bf16[6,192,128]{2,1,0:T(8,128)(2,1)S(1)} collective-permute-done((bf16[6,192,128]{2,1,0:T(8,128)(2,1)S(1)}, bf16[6,192,128]{2,1,0:T(8,128)(2,1)S(1)}, u32[]{:S(2)}, u32[]{:S(2)}) %collective-permute-start.23) | collective-permute-done | bytes 294944 | tf_op jit(solution)/shard_map/ppermute | solution.py:25
  137.0 6.9 %collective-permute-done.31.refs_5_ = bf16[2,192,128]{2,1,0:T(8,128)(2,1)S(1)} collective-permute-done((bf16[2,192,128]{2,1,0:T(8,128)(2,1)S(1)}, bf16[2,192,128]{2,1,0:T(8,128)(2,1)S(1)}, u32[]{:S(2)}, u32[]{:S(2)}) %collective-permute-start.31) | collective-permute-done | bytes 98336 | tf_op jit(solution)/shard_map/ppermute | solution.py:25
  143.9 4.0 %collective-permute-done.32.refs_6_ = bf16[2,192,128]{2,1,0:T(8,128)(2,1)S(1)} collective-permute-done((bf16[2,192,128]{2,1,0:T(8,128)(2,1)S(1)}, bf16[2,192,128]{2,1,0:T(8,128)(2,1)S(1)}, u32[]{:S(2)}, u32[]{:S(2)}) %collective-permute-start.32) | collective-permute-done | bytes 98336 | tf_op jit(solution)/shard_map/ppermute | solution.py:25
  (80 shorter events, 24.7 us)
Async XLA Ops:
  3.7 10.3 %collective-permute-start = (bf16[128,3584]{1,0:T(8,128)(2,1)S(1)}, bf16[128,3584]{1,0:T(8,128)(2,1)S(1)}, u32[]{:S(2)}, u32[]{:S(2)}) collective-permute-start(bf16[128,3584]{1,0:T(8,128)(2,1)S(1)} %shard_map.56.refs_0_), channel_id=1, source_target_pairs={{0,1},{2,3},{4,5},{6,7},{8,9},{10,11},{12,13},{14,15},{16,17},{18,... | collective-permute-start | bytes 2752520 | tf_op jit(solution)/shard_map/ppermute | solution.py:25
  16.6 14.4 %collective-permute-start.3 = (bf16[128,3200]{1,0:T(8,128)(2,1)S(1)}, bf16[128,3200]{1,0:T(8,128)(2,1)S(1)}, u32[]{:S(2)}, u32[]{:S(2)}) collective-permute-start(bf16[128,3200]{1,0:T(8,128)(2,1)S(1)} %get-tuple-element.54.refs_0_), channel_id=1, source_target_pairs={{1,3},{3,1},{5,7},{7,5},{9,11},{11,9},{13,15},{15,13},{17,19},{19,... | collective-permute-start | bytes 2457608 | tf_op jit(solution)/shard_map/ppermute | solution.py:20
  19.9 39.1 %collective-permute-start.1 = (bf16[384,1024]{1,0:T(8,128)(2,1)S(1)}, bf16[384,1024]{1,0:T(8,128)(2,1)S(1)}, u32[]{:S(2)}, u32[]{:S(2)}) collective-permute-start(bf16[384,1024]{1,0:T(8,128)(2,1)S(1)} %get-tuple-element.51.own_any), channel_id=1, source_target_pairs={{1,0},{3,2},{5,4},{7,6},{9,8},{11,10},{13,12},{15,14},{17,16},{19,... | collective-permute-start | bytes 2359304 | tf_op jit(solution)/shard_map/ppermute | solution.py:25
  31.4 24.2 %collective-permute-start.6 = (bf16[128,2304]{1,0:T(8,128)(2,1)S(1)}, bf16[128,2304]{1,0:T(8,128)(2,1)S(1)}, u32[]{:S(2)}, u32[]{:S(2)}) collective-permute-start(bf16[128,2304]{1,0:T(8,128)(2,1)S(1)} %get-tuple-element.59.refs_0_), channel_id=1, source_target_pairs={{1,5},{3,7},{5,1},{7,3},{9,13},{11,15},{13,9},{15,11},{17,21},{19,... | collective-permute-start | bytes 1769480 | tf_op jit(solution)/shard_map/ppermute | solution.py:20
  33.4 45.0 %collective-permute-start.4 = (bf16[256,1152]{1,0:T(8,128)(2,1)S(1)}, bf16[256,1152]{1,0:T(8,128)(2,1)S(1)}, u32[]{:S(2)}, u32[]{:S(2)}) collective-permute-start(bf16[256,1152]{1,0:T(8,128)(2,1)S(1)} %get-tuple-element.56), channel_id=1, source_target_pairs={{1,0},{3,2},{5,4},{7,6},{9,8},{11,10},{13,12},{15,14},{17,16},{19,... | collective-permute-start | bytes 1769480 | tf_op jit(solution)/shard_map/ppermute | solution.py:25
  56.0 11.9 %collective-permute-start.9 = (bf16[128,1536]{1,0:T(8,128)(2,1)S(1)}, bf16[128,1536]{1,0:T(8,128)(2,1)S(1)}, u32[]{:S(2)}, u32[]{:S(2)}) collective-permute-start(bf16[128,1536]{1,0:T(8,128)(2,1)S(1)} %get-tuple-element.63.refs_0_), channel_id=1, source_target_pairs={{1,13},{3,15},{5,9},{7,11},{9,5},{11,7},{13,1},{15,3},{17,29},{19,... | collective-permute-start | bytes 1179656 | tf_op jit(solution)/shard_map/ppermute | solution.py:20
  59.0 19.4 %collective-permute-start.2 = (bf16[192,1024]{1,0:T(8,128)(2,1)S(1)}, bf16[192,1024]{1,0:T(8,128)(2,1)S(1)}, u32[]{:S(2)}, u32[]{:S(2)}) collective-permute-start(bf16[192,1024]{1,0:T(8,128)(2,1)S(1)} %get-tuple-element.53), channel_id=1, source_target_pairs={{0,2},{2,0},{4,6},{6,4},{8,10},{10,8},{12,14},{14,12},{16,18},{18,... | collective-permute-start | bytes 1179656 | tf_op jit(solution)/shard_map/ppermute | solution.py:20
  59.7 24.7 %collective-permute-start.7 = (bf16[256,1024]{1,0:T(8,128)(2,1)S(1)}, bf16[256,1024]{1,0:T(8,128)(2,1)S(1)}, u32[]{:S(2)}, u32[]{:S(2)}) collective-permute-start(bf16[256,1024]{1,0:T(8,128)(2,1)S(1)} %get-tuple-element.60), channel_id=1, source_target_pairs={{1,0},{3,2},{5,4},{7,6},{9,8},{11,10},{13,12},{15,14},{17,16},{19,... | collective-permute-start | bytes 1572872 | tf_op jit(solution)/shard_map/ppermute | solution.py:25
  68.3 12.7 %collective-permute-start.12 = (bf16[128,640]{1,0:T(8,128)(2,1)S(1)}, bf16[128,640]{1,0:T(8,128)(2,1)S(1)}, u32[]{:S(2)}, u32[]{:S(2)}) collective-permute-start(bf16[128,640]{1,0:T(8,128)(2,1)S(1)} %get-tuple-element.67.refs_0_), channel_id=1, source_target_pairs={{1,3},{3,1},{5,7},{7,5},{9,11},{11,9},{13,15},{15,13},{17,19},{19,... | collective-permute-start | bytes 491528 | tf_op jit(solution)/shard_map/ppermute | solution.py:20
  78.4 5.9 %collective-permute-start.5 = (bf16[192,896]{1,0:T(8,128)(2,1)S(1)}, bf16[192,896]{1,0:T(8,128)(2,1)S(1)}, u32[]{:S(2)}, u32[]{:S(2)}) collective-permute-start(bf16[192,896]{1,0:T(8,128)(2,1)S(1)} %get-tuple-element.58.refs_0_), channel_id=1, source_target_pairs={{0,4},{2,6},{4,0},{6,2},{8,12},{10,14},{12,8},{14,10},{16,20},{18,... | collective-permute-start | bytes 1032200 | tf_op jit(solution)/shard_map/ppermute | solution.py:20
  81.1 8.5 %collective-permute-start.13 = (bf16[128,1536]{1,0:T(8,128)(2,1)S(1)}, bf16[128,1536]{1,0:T(8,128)(2,1)S(1)}, u32[]{:S(2)}, u32[]{:S(2)}) collective-permute-start(bf16[128,1536]{1,0:T(8,128)(2,1)S(1)} %shard_map.66.refs_0_), channel_id=1, source_target_pairs={{1,17},{3,19},{5,21},{7,23},{9,25},{11,27},{13,29},{15,31},{17,1},... | collective-permute-start | bytes 1179656 | tf_op jit(solution)/shard_map/ppermute | solution.py:20
  83.0 9.0 %collective-permute-start.10 = (bf16[256,896]{1,0:T(8,128)(2,1)S(1)}, bf16[256,896]{1,0:T(8,128)(2,1)S(1)}, u32[]{:S(2)}, u32[]{:S(2)}) collective-permute-start(bf16[256,896]{1,0:T(8,128)(2,1)S(1)} %get-tuple-element.64), channel_id=1, source_target_pairs={{1,0},{3,2},{5,4},{7,6},{9,8},{11,10},{13,12},{15,14},{17,16},{19,... | collective-permute-start | bytes 1376264 | tf_op jit(solution)/shard_map/ppermute | solution.py:25
  84.4 7.6 %collective-permute-start.8 = (bf16[192,768]{1,0:T(8,128)(2,1)S(1)}, bf16[192,768]{1,0:T(8,128)(2,1)S(1)}, u32[]{:S(2)}, u32[]{:S(2)}) collective-permute-start(bf16[192,768]{1,0:T(8,128)(2,1)S(1)} %get-tuple-element.62.refs_0_), channel_id=1, source_target_pairs={{0,12},{2,14},{4,8},{6,10},{8,4},{10,6},{12,0},{14,2},{16,28},{18,... | collective-permute-start | bytes 884744 | tf_op jit(solution)/shard_map/ppermute | solution.py:20
  90.1 10.6 %collective-permute-start.16 = (bf16[128,1024]{1,0:T(8,128)(2,1)S(1)}, bf16[128,1024]{1,0:T(8,128)(2,1)S(1)}, u32[]{:S(2)}, u32[]{:S(2)}) collective-permute-start(bf16[128,1024]{1,0:T(8,128)(2,1)S(1)} %get-tuple-element.71.refs_0_), channel_id=1, source_target_pairs={{1,33},{3,35},{5,37},{7,39},{9,41},{11,43},{13,45},{15,47},{17,49}... | collective-permute-start | bytes 786440 | tf_op jit(solution)/shard_map/ppermute | solution.py:20
  92.1 12.0 %collective-permute-start.11 = (bf16[192,640]{1,0:T(8,128)(2,1)S(1)}, bf16[192,640]{1,0:T(8,128)(2,1)S(1)}, u32[]{:S(2)}, u32[]{:S(2)}) collective-permute-start(bf16[192,640]{1,0:T(8,128)(2,1)S(1)} %get-tuple-element.66.refs_0_), channel_id=1, source_target_pairs={{0,16},{2,18},{4,20},{6,22},{8,24},{10,26},{12,28},{14,30},{16,0},... | collective-permute-start | bytes 737288 | tf_op jit(solution)/shard_map/ppermute | solution.py:20
  92.8 11.3 %collective-permute-start.14 = (bf16[256,768]{1,0:T(8,128)(2,1)S(1)}, bf16[256,768]{1,0:T(8,128)(2,1)S(1)}, u32[]{:S(2)}, u32[]{:S(2)}) collective-permute-start(bf16[256,768]{1,0:T(8,128)(2,1)S(1)} %get-tuple-element.68), channel_id=1, source_target_pairs={{1,0},{3,2},{5,4},{7,6},{9,8},{11,10},{13,12},{15,14},{17,16},{19,... | collective-permute-start | bytes 1179656 | tf_op jit(solution)/shard_map/ppermute | solution.py:25
  100.8 20.5 %collective-permute-start.17 = (bf16[256,640]{1,0:T(8,128)(2,1)S(1)}, bf16[256,640]{1,0:T(8,128)(2,1)S(1)}, u32[]{:S(2)}, u32[]{:S(2)}) collective-permute-start(bf16[256,640]{1,0:T(8,128)(2,1)S(1)} %get-tuple-element.72), channel_id=1, source_target_pairs={{1,0},{3,2},{5,4},{7,6},{9,8},{11,10},{13,12},{15,14},{17,16},{19,... | collective-permute-start | bytes 983048 | tf_op jit(solution)/shard_map/ppermute | solution.py:25
  102.1 8.2 %collective-permute-start.19 = (bf16[128,640]{1,0:T(8,128)(2,1)S(1)}, bf16[128,640]{1,0:T(8,128)(2,1)S(1)}, u32[]{:S(2)}, u32[]{:S(2)}) collective-permute-start(bf16[128,640]{1,0:T(8,128)(2,1)S(1)} %get-tuple-element.75.refs_0_), channel_id=1, source_target_pairs={{1,97},{3,99},{5,101},{7,103},{9,105},{11,107},{13,109},{15,111},{... | collective-permute-start | bytes 491528 | tf_op jit(solution)/shard_map/ppermute | solution.py:20
  104.1 17.1 %collective-permute-start.15 = (bf16[192,512]{1,0:T(8,128)(2,1)S(1)}, bf16[192,512]{1,0:T(8,128)(2,1)S(1)}, u32[]{:S(2)}, u32[]{:S(2)}) collective-permute-start(bf16[192,512]{1,0:T(8,128)(2,1)S(1)} %get-tuple-element.70.refs_0_), channel_id=1, source_target_pairs={{0,32},{2,34},{4,36},{6,38},{8,40},{10,42},{12,44},{14,46},{16,48}... | collective-permute-start | bytes 589832 | tf_op jit(solution)/shard_map/ppermute | solution.py:20
  110.7 11.3 %collective-permute-start.20 = (bf16[256,512]{1,0:T(8,128)(2,1)S(1)}, bf16[256,512]{1,0:T(8,128)(2,1)S(1)}, u32[]{:S(2)}, u32[]{:S(2)}) collective-permute-start(bf16[256,512]{1,0:T(8,128)(2,1)S(1)} %get-tuple-element.76), channel_id=1, source_target_pairs={{1,0},{3,2},{5,4},{7,6},{9,8},{11,10},{13,12},{15,14},{17,16},{19,... | collective-permute-start | bytes 786440 | tf_op jit(solution)/shard_map/ppermute | solution.py:25
  112.0 5.4 %collective-permute-start.25 = (bf16[128,384]{1,0:T(8,128)(2,1)S(1)}, bf16[128,384]{1,0:T(8,128)(2,1)S(1)}, u32[]{:S(2)}, u32[]{:S(2)}) collective-permute-start(bf16[128,384]{1,0:T(8,128)(2,1)S(1)} %get-tuple-element.80.refs_0_), channel_id=1, source_target_pairs={{1,129},{3,131},{5,133},{7,135},{9,137},{11,139},{13,141},{15,143}... | collective-permute-start | bytes 294920 | tf_op jit(solution)/shard_map/ppermute | solution.py:20
  117.6 10.3 %collective-permute-start.26 = (bf16[256,384]{1,0:T(8,128)(2,1)S(1)}, bf16[256,384]{1,0:T(8,128)(2,1)S(1)}, u32[]{:S(2)}, u32[]{:S(2)}) collective-permute-start(bf16[256,384]{1,0:T(8,128)(2,1)S(1)} %get-tuple-element.81), channel_id=1, source_target_pairs={{1,0},{3,2},{5,4},{7,6},{9,8},{11,10},{13,12},{15,14},{17,16},{19,... | collective-permute-start | bytes 589832 | tf_op jit(solution)/shard_map/ppermute | solution.py:25
  119.0 6.2 %collective-permute-start.28 = (bf16[128,256]{1,0:T(8,128)(2,1)S(1)}, bf16[128,256]{1,0:T(8,128)(2,1)S(1)}, u32[]{:S(2)}, u32[]{:S(2)}) collective-permute-start(bf16[128,256]{1,0:T(8,128)(2,1)S(1)} %get-tuple-element.84.refs_0_), channel_id=1, source_target_pairs={{1,385},{3,387},{5,389},{7,391},{9,393},{11,395},{13,397},{15,399}... | collective-permute-start | bytes 196616 | tf_op jit(solution)/shard_map/ppermute | solution.py:20
  121.3 0.7 collective-permute-start.18
  122.0 10.0 %collective-permute-start.21 = (bf16[6,192,128]{2,1,0:T(8,128)(2,1)S(1)}, bf16[6,192,128]{2,1,0:T(8,128)(2,1)S(1)}, u32[]{:S(2)}, u32[]{:S(2)}) collective-permute-start(bf16[6,192,128]{2,1,0:T(8,128)(2,1)S(1)} %get-tuple-element.87), channel_id=1, source_target_pairs={{0,2},{2,0},{4,6},{6,4},{8,10},{10,8},{12,14},{14,12},{16,18},{18,... | collective-permute-start | bytes 884744 | tf_op jit(solution)/shard_map/ppermute | solution.py:20
  122.7 6.6 %collective-permute-start.24 = (bf16[192,256]{1,0:T(8,128)(2,1)S(1)}, bf16[192,256]{1,0:T(8,128)(2,1)S(1)}, u32[]{:S(2)}, u32[]{:S(2)}) collective-permute-start(bf16[192,256]{1,0:T(8,128)(2,1)S(1)} %get-tuple-element.79.refs_0_), channel_id=1, source_target_pairs={{0,128},{2,130},{4,132},{6,134},{8,136},{10,138},{12,140},{14,142}... | collective-permute-start | bytes 294920 | tf_op jit(solution)/shard_map/ppermute | solution.py:20
  125.4 4.6 %collective-permute-start.29 = (bf16[256,256]{1,0:T(8,128)(2,1)S(1)}, bf16[256,256]{1,0:T(8,128)(2,1)S(1)}, u32[]{:S(2)}, u32[]{:S(2)}) collective-permute-start(bf16[256,256]{1,0:T(8,128)(2,1)S(1)} %shard_map.76), channel_id=1, source_target_pairs={{1,0},{3,2},{5,4},{7,6},{9,8},{11,10},{13,12},{15,14},{17,16},{19,... | collective-permute-start | bytes 393224 | tf_op jit(solution)/shard_map/ppermute | solution.py:25
  126.7 6.7 %collective-permute-start.22 = (bf16[6,192,128]{2,1,0:T(8,128)(2,1)S(1)}, bf16[6,192,128]{2,1,0:T(8,128)(2,1)S(1)}, u32[]{:S(2)}, u32[]{:S(2)}) collective-permute-start(bf16[6,192,128]{2,1,0:T(8,128)(2,1)S(1)} %get-tuple-element.88.refs_7_), channel_id=1, source_target_pairs={{0,1},{2,3},{4,5},{6,7},{8,9},{10,11},{12,13},{14,15},{16,17},{18,... | collective-permute-start | bytes 884744 | tf_op jit(solution)/shard_map/ppermute | solution.py:25
  128.0 8.2 %collective-permute-start.23 = (bf16[6,192,128]{2,1,0:T(8,128)(2,1)S(1)}, bf16[6,192,128]{2,1,0:T(8,128)(2,1)S(1)}, u32[]{:S(2)}, u32[]{:S(2)}) collective-permute-start(bf16[6,192,128]{2,1,0:T(8,128)(2,1)S(1)} %get-tuple-element.87), channel_id=1, source_target_pairs={{2,1},{0,3},{6,5},{4,7},{10,9},{8,11},{14,13},{12,15},{18,17},{16,... | collective-permute-start | bytes 884744 | tf_op jit(solution)/shard_map/ppermute | solution.py:25
  130.0 7.0 %collective-permute-start.30 = (bf16[2,192,128]{2,1,0:T(8,128)(2,1)S(1)}, bf16[2,192,128]{2,1,0:T(8,128)(2,1)S(1)}, u32[]{:S(2)}, u32[]{:S(2)}) collective-permute-start(bf16[2,192,128]{2,1,0:T(8,128)(2,1)S(1)} %pad_maximum_fusion.refs_3_), channel_id=1, source_target_pairs={{0,2},{2,0},{4,6},{6,4},{8,10},{10,8},{12,14},{14,12},{16,18},{18,... | collective-permute-start | bytes 294920 | tf_op jit(solution)/shard_map/ppermute | solution.py:20
  130.7 13.2 %collective-permute-start.31 = (bf16[2,192,128]{2,1,0:T(8,128)(2,1)S(1)}, bf16[2,192,128]{2,1,0:T(8,128)(2,1)S(1)}, u32[]{:S(2)}, u32[]{:S(2)}) collective-permute-start(bf16[2,192,128]{2,1,0:T(8,128)(2,1)S(1)} %pad_maximum_fusion.refs_3_), channel_id=1, source_target_pairs={{0,1},{2,3},{4,5},{6,7},{8,9},{10,11},{12,13},{14,15},{16,17},{18,... | collective-permute-start | bytes 294920 | tf_op jit(solution)/shard_map/ppermute | solution.py:25
  132.0 16.0 %collective-permute-start.32 = (bf16[2,192,128]{2,1,0:T(8,128)(2,1)S(1)}, bf16[2,192,128]{2,1,0:T(8,128)(2,1)S(1)}, u32[]{:S(2)}, u32[]{:S(2)}) collective-permute-start(bf16[2,192,128]{2,1,0:T(8,128)(2,1)S(1)} %pad_maximum_fusion.refs_3_), channel_id=1, source_target_pairs={{2,1},{0,3},{6,5},{4,7},{10,9},{8,11},{14,13},{12,15},{18,17},{16,... | collective-permute-start | bytes 294920 | tf_op jit(solution)/shard_map/ppermute | solution.py:25
  (8 other events, 25.9 us)

commit v6 on v5

--- a/solution.py
+++ b/solution.py
@@ -135,7 +135,7 @@
             out_ref[count:, at:] = total(rows, last + part, last + 2 * part)
 
 
-def static_body(own_any, other_any, keep_ref, capacity_ref, *refs, cut, width, outs, kept, plain):
+def static_body(own_any, other_any, keep_ref, capacity_ref, *refs, cut, width, outs, kept):
     out_refs, (own, other, sems) = refs[:outs], refs[outs:]
 
     @pl.when(bit(0) == 1)
@@ -152,9 +152,6 @@
         def total(low, high):
             return (own[:, low:high].astype(F32) + other[:, low:high].astype(F32)).astype(BF)
 
-        if plain:
-            message_ref[...] = total(cut, own.shape[1])
-            return
         if width:
             message_ref[:, :width] = total(cut, cut + width)
         message_ref[:, width : width + inner] = capacity_ref[0]
@@ -164,6 +161,13 @@
         if kept:
             rest = keep_ref[...].astype(F32) + other[:, end:].astype(F32)
             message_ref[:, end - cut + inner :] = rest.astype(BF)
+
+
+def tail_body(own_any, other_any, out_ref, own, other, sems, *, cut):
+    @pl.when(bit(0) == 1)
+    def _():
+        fetch([(own_any, own), (other_any, other)], sems)
+        out_ref[...] = (own[:, cut:].astype(F32) + other[:, cut:].astype(F32)).astype(BF)
 
 
 def join_body(own_ref, other_ref, capacity_ref, message_ref, *, width):
@@ -274,13 +278,13 @@
         [like(sums), like(sums), dma((2,))],
     )
 
-    def spread_out(state, mine, base, zero):
-        near0 = jnp.stack([c[:, :rank] for c in mine])
-        theirs = jnp.stack([c[:, -rank:] for c in mine])
-        far0 = swap(theirs, 2, 0)
+    def stacks(mine):
+        return jnp.stack([c[:, :rank] for c in mine]), jnp.stack([c[:, -rank:] for c in mine])
+
+    def spread_out(state, near0, theirs, far0, base, zero):
         near1 = to_core(near0, 1)
         far1 = to_core(theirs, 1, 3)
-        count = len(mine)
+        count = near0.shape[0]
         tile = samples // 2
 
         def spread_block(level):
@@ -304,30 +308,36 @@
     gathered = []
     early = levels - 3
     for level in range(1, levels):
-        other = swap(send, mask_of(level), 0)
+        if level == split - 1:
+            other = swap(send, mask_of(level), 0)
         plain = level == split - 1 and rest > 0
         outs = [sds((2 * rank, blocks(level, level + 1) + inner), BF)]
-        if plain:
-            outs.append(sds((rank, rest), BF))
-        elif level < levels - 1:
+        if level < levels - 1 and not plain:
             late = rest if level < split else blocks(level + 2, levels)
             outs.append(sds((rank, blocks(level + 1, max(split, level + 2) if level < split else level + 2) + inner + late), BF))
         results = call(
-            lambda *refs, l=level, n=len(outs), p=plain: static_body(
-                *refs, cut=blocks(l, l + 1) + inner, width=blocks(l + 1, l + 2), outs=n, kept=rest if l == 1 else 0, plain=p
+            lambda *refs, l=level, n=len(outs): static_body(
+                *refs, cut=blocks(l, l + 1) + inner, width=blocks(l + 1, l + 2), outs=n, kept=rest if l == 1 else 0
             ),
             outs,
             [message, static_got, keep, capacity],
             [ANY, ANY, VMEM, level_block(capacity, min(level + 1, levels - 1))],
             [like(message), like(message), dma((2,))],
         )
-        both = results[0]
-        static_block = to_core(both, 0)
+        static_block = to_core(results[0], 0)
         if plain:
+            static_got, other, static_block = lax.optimization_barrier((static_got, other, static_block))
+            (tail,) = call(
+                lambda *refs, c=blocks(level, level + 1) + inner: tail_body(*refs, cut=c),
+                [sds((rank, rest), BF)],
+                [message, static_got],
+                [ANY, ANY],
+                [like(message), like(message), dma((2,))],
+            )
             (message,) = call(
                 lambda *refs: join_body(*refs, width=blocks(split, split + 1)),
                 [sds((rank, 2 * rest + inner), BF)],
-                [results[1], swap(results[1], 2, 1), capacity],
+                [tail, swap(tail, 2, 1), capacity],
                 [VMEM, VMEM, level_block(capacity, split)],
             )
         elif level < levels - 1:
@@ -335,6 +345,8 @@
         if level < levels - 1:
             static_got = swap(message, mask_of(level + 1), 1)
 
+        if level != split - 1:
+            other = swap(send, mask_of(level), 0)
         width = (levels - 1 - level) * rank
         outs = [sds((half, 2 * rank if level == 1 else rank), BF)]
         if width:
@@ -348,10 +360,17 @@
         gathered.append(results[0])
         if width:
             own = results[1]
+            if level < split - 1:
+                own, static_got = lax.optimization_barrier((own, static_got))
             send = own
         if level == early:
-            state = spread_out(state, gathered, 1, zero)
-    return spread_out(state, gathered[early:], early + 1, None)
+            near0, theirs = stacks(gathered)
+            far0 = swap(theirs, 2, 0)
+        if level == early + 1:
+            near0, theirs, _ = lax.optimization_barrier((near0, theirs, gathered[-1]))
+            state = spread_out(state, near0, theirs, far0, 1, zero)
+    near0, theirs = stacks(gathered[early:])
+    return spread_out(state, near0, theirs, swap(theirs, 2, 0), early + 1, None)
 
 
 def solution(mesh):

time: 150 us -> 156 us (1.040)
  waiting for transfers between devices: 83.3 us -> 87.2 us
    ppermute x19, waiting for transfers between devices: 61.3 us -> 66 us  [swap(): return lax.ppermute(value, AXIS, pairs)]
    ppermute x14, starting transfers between devices: 18.4 us -> 20.1 us  [to_core(): return lax.ppermute(value, AXIS, pairs)]
    pallas_call x24 -> x25, Pallas kernels: 8.8 us -> 9.17 us  [call(): pl.pallas_call(body, out_shape=outs, grid=grid, in_specs=specs, out_specs...]
  transfers between devices with their start and end apart: 33 -> 33, of which waited for: 13 -> 14; matrix products, arithmetic and copies ran while one was open for 0% -> 0% of each run, Pallas kernels for 4% -> 3%
where the time goes in v6:
time: 156 us; the launch traced here: 155 us
  waiting for transfers between devices  87.2 us (56%)
  starting transfers between devices  53.3 us (34%)
  Pallas kernels  9.17 us (6%)
  local copies, waits for them, and re-layouts  2.67 us (2%)
  blocking collectives  1.93 us (1%)
    ppermute x19, waiting for transfers between devices, swap(): return lax.ppermute(value, AXIS, pairs)  66 us
    ppermute x19, starting transfers between devices, swap(): return lax.ppermute(value, AXIS, pairs)  33.2 us
    ppermute x14, waiting for transfers between devices, to_core(): return lax.ppermute(value, AXIS, pairs)  21.2 us
    ppermute x14, starting transfers between devices, to_core(): return lax.ppermute(value, AXIS, pairs)  20.1 us
    pallas_call x25, Pallas kernels, call(): pl.pallas_call(body, out_shape=outs, grid=grid, in_specs=specs, out_specs...  9.17 us
  transfers between devices with their start and end apart: 33, of which 14 were waited for; matrix products, arithmetic and copies ran while one was open for 0% of the time, Pallas kernels for 3%

profile of v6, /device:TPU:1, one launch (start us, length us, event | category | flops | bytes accessed | tf_op | source)
XLA Modules:
  0.0 154.9 jit_solution(16041769083067035923)
XLA Ops:
  3.7 1.4 collective-permute-start
  5.8 8.2 %collective-permute-done.refs_1_ = bf16[128,3584]{1,0:T(8,128)(2,1)S(1)} collective-permute-done((bf16[128,3584]{1,0:T(8,128)(2,1)S(1)}, bf16[128,3584]{1,0:T(8,128)(2,1)S(1)}, u32[]{:S(2)}, u32[]{:S(2)}) %collective-permute-start) | collective-permute-done | bytes 917536 | tf_op jit(solution)/shard_map/ppermute | solution.py:25
  14.0 1.9 %all_gather.3.stacked_ref = bf16[256,384]{1,0:T(8,128)(2,1)S(1)} all-gather(bf16[128,384]{1,0:T(8,128)(2,1)S(1)} %get-tuple-element.54), channel_id=1, replica_groups={{0,1},{2,3},{4,5},{6,7},{8,9},{10,11},{12,13},{14,15},{16,17},{18,19},{..., dimensions={0}, use_global_device_ids=true | all-gather | bytes 294912 | tf_op jit(solution)/shard_map/all_gather | solution.py:249
  16.6 1.9 %collective-permute-start.3 = (bf16[128,3200]{1,0:T(8,128)(2,1)S(1)}, bf16[128,3200]{1,0:T(8,128)(2,1)S(1)}, u32[]{:S(2)}, u32[]{:S(2)}) collective-permute-start(bf16[128,3200]{1,0:T(8,128)(2,1)S(1)} %get-tuple-element.61.refs_0_), channel_id=1, source_target_pairs={{1,3},{3,1},{5,7},{7,5},{9,11},{11,9},{13,15},{15,13},{17,19},{19,... | collective-permute-start | bytes 2457608 | tf_op jit(solution)/shard_map/ppermute | solution.py:20
  18.5 1.4 shard_map.58
  19.9 1.3 collective-permute-start.1
  21.2 9.8 %collective-permute-done.3.refs_1_ = bf16[128,3200]{1,0:T(8,128)(2,1)S(1)} collective-permute-done((bf16[128,3200]{1,0:T(8,128)(2,1)S(1)}, bf16[128,3200]{1,0:T(8,128)(2,1)S(1)}, u32[]{:S(2)}, u32[]{:S(2)}) %collective-permute-start.3) | collective-permute-done | bytes 819232 | tf_op jit(solution)/shard_map/ppermute | solution.py:20
  31.4 1.3 collective-permute-start.4
  32.8 1.9 %collective-permute-start.5 = (bf16[128,2304]{1,0:T(8,128)(2,1)S(1)}, bf16[128,2304]{1,0:T(8,128)(2,1)S(1)}, u32[]{:S(2)}, u32[]{:S(2)}) collective-permute-start(bf16[128,2304]{1,0:T(8,128)(2,1)S(1)} %get-tuple-element.66.refs_0_), channel_id=1, source_target_pairs={{1,5},{3,7},{5,1},{7,3},{9,13},{11,15},{13,9},{15,11},{17,21},{19,... | collective-permute-start | bytes 1769480 | tf_op jit(solution)/shard_map/ppermute | solution.py:20
  35.5 21.5 %collective-permute-done.5.refs_1_ = bf16[128,2304]{1,0:T(8,128)(2,1)S(1)} collective-permute-done((bf16[128,2304]{1,0:T(8,128)(2,1)S(1)}, bf16[128,2304]{1,0:T(8,128)(2,1)S(1)}, u32[]{:S(2)}, u32[]{:S(2)}) %collective-permute-start.5) | collective-permute-done | bytes 589856 | tf_op jit(solution)/shard_map/ppermute | solution.py:20
  57.3 1.3 collective-permute-start.7
  58.7 2.9 %collective-permute-start.8 = (bf16[128,1536]{1,0:T(8,128)(2,1)S(1)}, bf16[128,1536]{1,0:T(8,128)(2,1)S(1)}, u32[]{:S(2)}, u32[]{:S(2)}) collective-permute-start(bf16[128,1536]{1,0:T(8,128)(2,1)S(1)} %get-tuple-element.72.refs_0_), channel_id=1, source_target_pairs={{1,13},{3,15},{5,9},{7,11},{9,5},{11,7},{13,1},{15,3},{17,29},{19,... | collective-permute-start | bytes 1179656 | tf_op jit(solution)/shard_map/ppermute | solution.py:20
  62.4 11.8 %collective-permute-done.8.refs_1_ = bf16[128,1536]{1,0:T(8,128)(2,1)S(1)} collective-permute-done((bf16[128,1536]{1,0:T(8,128)(2,1)S(1)}, bf16[128,1536]{1,0:T(8,128)(2,1)S(1)}, u32[]{:S(2)}, u32[]{:S(2)}) %collective-permute-start.8) | collective-permute-done | bytes 393248 | tf_op jit(solution)/shard_map/ppermute | solution.py:20
  74.6 1.3 collective-permute-start.10
  77.7 8.8 %collective-permute-start.12 = (bf16[128,640]{1,0:T(8,128)(2,1)S(1)}, bf16[128,640]{1,0:T(8,128)(2,1)S(1)}, u32[]{:S(2)}, u32[]{:S(2)}) collective-permute-start(bf16[128,640]{1,0:T(8,128)(2,1)S(1)} %shard_map.66.refs_0_), channel_id=1, source_target_pairs={{1,3},{3,1},{5,7},{7,5},{9,11},{11,9},{13,15},{15,13},{17,19},{19,... | collective-permute-start | bytes 491528 | tf_op jit(solution)/shard_map/ppermute | solution.py:20
  86.5 2.7 %collective-permute-done.12.refs_1_ = bf16[128,640]{1,0:T(8,128)(2,1)S(1)} collective-permute-done((bf16[128,640]{1,0:T(8,128)(2,1)S(1)}, bf16[128,640]{1,0:T(8,128)(2,1)S(1)}, u32[]{:S(2)}, u32[]{:S(2)}) %collective-permute-start.12) | collective-permute-done | bytes 163872 | tf_op jit(solution)/shard_map/ppermute | solution.py:20
  89.3 1.9 %collective-permute-start.13 = (bf16[128,1536]{1,0:T(8,128)(2,1)S(1)}, bf16[128,1536]{1,0:T(8,128)(2,1)S(1)}, u32[]{:S(2)}, u32[]{:S(2)}) collective-permute-start(bf16[128,1536]{1,0:T(8,128)(2,1)S(1)} %shard_map.67.refs_0_), channel_id=1, source_target_pairs={{1,17},{3,19},{5,21},{7,23},{9,25},{11,27},{13,29},{15,31},{17,1},... | collective-permute-start | bytes 1179656 | tf_op jit(solution)/shard_map/ppermute | solution.py:20
  91.2 6.6 %collective-permute-done.13.refs_1_ = bf16[128,1536]{1,0:T(8,128)(2,1)S(1)} collective-permute-done((bf16[128,1536]{1,0:T(8,128)(2,1)S(1)}, bf16[128,1536]{1,0:T(8,128)(2,1)S(1)}, u32[]{:S(2)}, u32[]{:S(2)}) %collective-permute-start.13) | collective-permute-done | bytes 393248 | tf_op jit(solution)/shard_map/ppermute | solution.py:20
  98.3 2.0 %collective-permute-start.16 = (bf16[128,1024]{1,0:T(8,128)(2,1)S(1)}, bf16[128,1024]{1,0:T(8,128)(2,1)S(1)}, u32[]{:S(2)}, u32[]{:S(2)}) collective-permute-start(bf16[128,1024]{1,0:T(8,128)(2,1)S(1)} %get-tuple-element.83.refs_0_), channel_id=1, source_target_pairs={{1,33},{3,35},{5,37},{7,39},{9,41},{11,43},{13,45},{15,47},{17,49}... | collective-permute-start | bytes 786440 | tf_op jit(solution)/shard_map/ppermute | solution.py:20
  101.0 1.3 collective-permute-start.14
  102.4 6.4 %collective-permute-done.16.refs_1_ = bf16[128,1024]{1,0:T(8,128)(2,1)S(1)} collective-permute-done((bf16[128,1024]{1,0:T(8,128)(2,1)S(1)}, bf16[128,1024]{1,0:T(8,128)(2,1)S(1)}, u32[]{:S(2)}, u32[]{:S(2)}) %collective-permute-start.16) | collective-permute-done | bytes 262176 | tf_op jit(solution)/shard_map/ppermute | solution.py:20
  108.9 3.0 %collective-permute-start.19 = (bf16[128,640]{1,0:T(8,128)(2,1)S(1)}, bf16[128,640]{1,0:T(8,128)(2,1)S(1)}, u32[]{:S(2)}, u32[]{:S(2)}) collective-permute-start(bf16[128,640]{1,0:T(8,128)(2,1)S(1)} %get-tuple-element.87.refs_0_), channel_id=1, source_target_pairs={{1,97},{3,99},{5,101},{7,103},{9,105},{11,107},{13,109},{15,111},{... | collective-permute-start | bytes 491528 | tf_op jit(solution)/shard_map/ppermute | solution.py:20
  112.0 1.3 collective-permute-start.17
  114.0 4.3 %collective-permute-done.19.refs_1_ = bf16[128,640]{1,0:T(8,128)(2,1)S(1)} collective-permute-done((bf16[128,640]{1,0:T(8,128)(2,1)S(1)}, bf16[128,640]{1,0:T(8,128)(2,1)S(1)}, u32[]{:S(2)}, u32[]{:S(2)}) %collective-permute-start.19) | collective-permute-done | bytes 163872 | tf_op jit(solution)/shard_map/ppermute | solution.py:20
  118.8 1.9 %collective-permute-start.22 = (bf16[128,384]{1,0:T(8,128)(2,1)S(1)}, bf16[128,384]{1,0:T(8,128)(2,1)S(1)}, u32[]{:S(2)}, u32[]{:S(2)}) collective-permute-start(bf16[128,384]{1,0:T(8,128)(2,1)S(1)} %get-tuple-element.91.refs_0_), channel_id=1, source_target_pairs={{1,129},{3,131},{5,133},{7,135},{9,137},{11,139},{13,141},{15,143}... | collective-permute-start | bytes 294920 | tf_op jit(solution)/shard_map/ppermute | solution.py:20
  120.7 1.3 collective-permute-start.20
  122.0 2.1 %collective-permute-done.22.refs_1_ = bf16[128,384]{1,0:T(8,128)(2,1)S(1)} collective-permute-done((bf16[128,384]{1,0:T(8,128)(2,1)S(1)}, bf16[128,384]{1,0:T(8,128)(2,1)S(1)}, u32[]{:S(2)}, u32[]{:S(2)}) %collective-permute-start.22) | collective-permute-done | bytes 98336 | tf_op jit(solution)/shard_map/ppermute | solution.py:20
  124.4 2.0 %collective-permute-start.28 = (bf16[128,256]{1,0:T(8,128)(2,1)S(1)}, bf16[128,256]{1,0:T(8,128)(2,1)S(1)}, u32[]{:S(2)}, u32[]{:S(2)}) collective-permute-start(bf16[128,256]{1,0:T(8,128)(2,1)S(1)} %get-tuple-element.98.refs_0_), channel_id=1, source_target_pairs={{1,385},{3,387},{5,389},{7,391},{9,393},{11,395},{13,397},{15,399}... | collective-permute-start | bytes 196616 | tf_op jit(solution)/shard_map/ppermute | solution.py:20
  130.8 2.9 %collective-permute-start.29 = (bf16[256,256]{1,0:T(8,128)(2,1)S(1)}, bf16[256,256]{1,0:T(8,128)(2,1)S(1)}, u32[]{:S(2)}, u32[]{:S(2)}) collective-permute-start(bf16[256,256]{1,0:T(8,128)(2,1)S(1)} %shard_map.77), channel_id=1, source_target_pairs={{1,0},{3,2},{5,4},{7,6},{9,8},{11,10},{13,12},{15,14},{17,16},{19,... | collective-permute-start | bytes 393224 | tf_op jit(solution)/shard_map/ppermute | solution.py:25
  140.5 2.7 %collective-permute-done.26.refs_10_ = bf16[6,192,128]{2,1,0:T(8,128)(2,1)S(1)} collective-permute-done((bf16[6,192,128]{2,1,0:T(8,128)(2,1)S(1)}, bf16[6,192,128]{2,1,0:T(8,128)(2,1)S(1)}, u32[]{:S(2)}, u32[]{:S(2)}) %collective-permute-start.26) | collective-permute-done | bytes 294944 | tf_op jit(solution)/shard_map/ppermute | solution.py:25
  144.0 6.6 %collective-permute-done.31.refs_5_ = bf16[2,192,128]{2,1,0:T(8,128)(2,1)S(1)} collective-permute-done((bf16[2,192,128]{2,1,0:T(8,128)(2,1)S(1)}, bf16[2,192,128]{2,1,0:T(8,128)(2,1)S(1)}, u32[]{:S(2)}, u32[]{:S(2)}) %collective-permute-start.31) | collective-permute-done | bytes 98336 | tf_op jit(solution)/shard_map/ppermute | solution.py:25
  150.6 3.0 %collective-permute-done.32.refs_6_ = bf16[2,192,128]{2,1,0:T(8,128)(2,1)S(1)} collective-permute-done((bf16[2,192,128]{2,1,0:T(8,128)(2,1)S(1)}, bf16[2,192,128]{2,1,0:T(8,128)(2,1)S(1)}, u32[]{:S(2)}, u32[]{:S(2)}) %collective-permute-start.32) | collective-permute-done | bytes 98336 | tf_op jit(solution)/shard_map/ppermute | solution.py:25
  (81 shorter events, 25.2 us)
Async XLA Ops:
  3.7 10.3 %collective-permute-start = (bf16[128,3584]{1,0:T(8,128)(2,1)S(1)}, bf16[128,3584]{1,0:T(8,128)(2,1)S(1)}, u32[]{:S(2)}, u32[]{:S(2)}) collective-permute-start(bf16[128,3584]{1,0:T(8,128)(2,1)S(1)} %shard_map.56.refs_0_), channel_id=1, source_target_pairs={{0,1},{2,3},{4,5},{6,7},{8,9},{10,11},{12,13},{14,15},{16,17},{18,... | collective-permute-start | bytes 2752520 | tf_op jit(solution)/shard_map/ppermute | solution.py:25
  16.6 14.4 %collective-permute-start.3 = (bf16[128,3200]{1,0:T(8,128)(2,1)S(1)}, bf16[128,3200]{1,0:T(8,128)(2,1)S(1)}, u32[]{:S(2)}, u32[]{:S(2)}) collective-permute-start(bf16[128,3200]{1,0:T(8,128)(2,1)S(1)} %get-tuple-element.61.refs_0_), channel_id=1, source_target_pairs={{1,3},{3,1},{5,7},{7,5},{9,11},{11,9},{13,15},{15,13},{17,19},{19,... | collective-permute-start | bytes 2457608 | tf_op jit(solution)/shard_map/ppermute | solution.py:20
  19.9 14.8 %collective-permute-start.1 = (bf16[384,1024]{1,0:T(8,128)(2,1)S(1)}, bf16[384,1024]{1,0:T(8,128)(2,1)S(1)}, u32[]{:S(2)}, u32[]{:S(2)}) collective-permute-start(bf16[384,1024]{1,0:T(8,128)(2,1)S(1)} %get-tuple-element.58.own_any), channel_id=1, source_target_pairs={{1,0},{3,2},{5,4},{7,6},{9,8},{11,10},{13,12},{15,14},{17,16},{19,... | collective-permute-start | bytes 2359304 | tf_op jit(solution)/shard_map/ppermute | solution.py:25
  31.4 4.0 %collective-permute-start.4 = (bf16[256,1152]{1,0:T(8,128)(2,1)S(1)}, bf16[256,1152]{1,0:T(8,128)(2,1)S(1)}, u32[]{:S(2)}, u32[]{:S(2)}) collective-permute-start(bf16[256,1152]{1,0:T(8,128)(2,1)S(1)} %get-tuple-element.63), channel_id=1, source_target_pairs={{1,0},{3,2},{5,4},{7,6},{9,8},{11,10},{13,12},{15,14},{17,16},{19,... | collective-permute-start | bytes 1769480 | tf_op jit(solution)/shard_map/ppermute | solution.py:25
  32.8 24.2 %collective-permute-start.5 = (bf16[128,2304]{1,0:T(8,128)(2,1)S(1)}, bf16[128,2304]{1,0:T(8,128)(2,1)S(1)}, u32[]{:S(2)}, u32[]{:S(2)}) collective-permute-start(bf16[128,2304]{1,0:T(8,128)(2,1)S(1)} %get-tuple-element.66.refs_0_), channel_id=1, source_target_pairs={{1,5},{3,7},{5,1},{7,3},{9,13},{11,15},{13,9},{15,11},{17,21},{19,... | collective-permute-start | bytes 1769480 | tf_op jit(solution)/shard_map/ppermute | solution.py:20
  34.7 0.7 collective-permute-start.2
  57.3 5.0 %collective-permute-start.7 = (bf16[256,1024]{1,0:T(8,128)(2,1)S(1)}, bf16[256,1024]{1,0:T(8,128)(2,1)S(1)}, u32[]{:S(2)}, u32[]{:S(2)}) collective-permute-start(bf16[256,1024]{1,0:T(8,128)(2,1)S(1)} %get-tuple-element.69), channel_id=1, source_target_pairs={{1,0},{3,2},{5,4},{7,6},{9,8},{11,10},{13,12},{15,14},{17,16},{19,... | collective-permute-start | bytes 1572872 | tf_op jit(solution)/shard_map/ppermute | solution.py:25
  58.7 15.5 %collective-permute-start.8 = (bf16[128,1536]{1,0:T(8,128)(2,1)S(1)}, bf16[128,1536]{1,0:T(8,128)(2,1)S(1)}, u32[]{:S(2)}, u32[]{:S(2)}) collective-permute-start(bf16[128,1536]{1,0:T(8,128)(2,1)S(1)} %get-tuple-element.72.refs_0_), channel_id=1, source_target_pairs={{1,13},{3,15},{5,9},{7,11},{9,5},{11,7},{13,1},{15,3},{17,29},{19,... | collective-permute-start | bytes 1179656 | tf_op jit(solution)/shard_map/ppermute | solution.py:20
  61.6 0.7 collective-permute-start.6
  74.6 2.7 %collective-permute-start.10 = (bf16[256,896]{1,0:T(8,128)(2,1)S(1)}, bf16[256,896]{1,0:T(8,128)(2,1)S(1)}, u32[]{:S(2)}, u32[]{:S(2)}) collective-permute-start(bf16[256,896]{1,0:T(8,128)(2,1)S(1)} %shard_map.64), channel_id=1, source_target_pairs={{1,0},{3,2},{5,4},{7,6},{9,8},{11,10},{13,12},{15,14},{17,16},{19,... | collective-permute-start | bytes 1376264 | tf_op jit(solution)/shard_map/ppermute | solution.py:25
  75.9 0.7 collective-permute-start.9
  77.7 11.5 %collective-permute-start.12 = (bf16[128,640]{1,0:T(8,128)(2,1)S(1)}, bf16[128,640]{1,0:T(8,128)(2,1)S(1)}, u32[]{:S(2)}, u32[]{:S(2)}) collective-permute-start(bf16[128,640]{1,0:T(8,128)(2,1)S(1)} %shard_map.66.refs_0_), channel_id=1, source_target_pairs={{1,3},{3,1},{5,7},{7,5},{9,11},{11,9},{13,15},{15,13},{17,19},{19,... | collective-permute-start | bytes 491528 | tf_op jit(solution)/shard_map/ppermute | solution.py:20
  89.3 8.5 %collective-permute-start.13 = (bf16[128,1536]{1,0:T(8,128)(2,1)S(1)}, bf16[128,1536]{1,0:T(8,128)(2,1)S(1)}, u32[]{:S(2)}, u32[]{:S(2)}) collective-permute-start(bf16[128,1536]{1,0:T(8,128)(2,1)S(1)} %shard_map.67.refs_0_), channel_id=1, source_target_pairs={{1,17},{3,19},{5,21},{7,23},{9,25},{11,27},{13,29},{15,31},{17,1},... | collective-permute-start | bytes 1179656 | tf_op jit(solution)/shard_map/ppermute | solution.py:20
  98.3 10.6 %collective-permute-start.16 = (bf16[128,1024]{1,0:T(8,128)(2,1)S(1)}, bf16[128,1024]{1,0:T(8,128)(2,1)S(1)}, u32[]{:S(2)}, u32[]{:S(2)}) collective-permute-start(bf16[128,1024]{1,0:T(8,128)(2,1)S(1)} %get-tuple-element.83.refs_0_), channel_id=1, source_target_pairs={{1,33},{3,35},{5,37},{7,39},{9,41},{11,43},{13,45},{15,47},{17,49}... | collective-permute-start | bytes 786440 | tf_op jit(solution)/shard_map/ppermute | solution.py:20
  100.3 13.0 %collective-permute-start.11 = (bf16[192,640]{1,0:T(8,128)(2,1)S(1)}, bf16[192,640]{1,0:T(8,128)(2,1)S(1)}, u32[]{:S(2)}, u32[]{:S(2)}) collective-permute-start(bf16[192,640]{1,0:T(8,128)(2,1)S(1)} %get-tuple-element.78.refs_0_), channel_id=1, source_target_pairs={{0,16},{2,18},{4,20},{6,22},{8,24},{10,26},{12,28},{14,30},{16,0},... | collective-permute-start | bytes 737288 | tf_op jit(solution)/shard_map/ppermute | solution.py:20
  101.0 12.3 %collective-permute-start.14 = (bf16[256,768]{1,0:T(8,128)(2,1)S(1)}, bf16[256,768]{1,0:T(8,128)(2,1)S(1)}, u32[]{:S(2)}, u32[]{:S(2)}) collective-permute-start(bf16[256,768]{1,0:T(8,128)(2,1)S(1)} %get-tuple-element.80), channel_id=1, source_target_pairs={{1,0},{3,2},{5,4},{7,6},{9,8},{11,10},{13,12},{15,14},{17,16},{19,... | collective-permute-start | bytes 1179656 | tf_op jit(solution)/shard_map/ppermute | solution.py:25
  108.9 9.4 %collective-permute-start.19 = (bf16[128,640]{1,0:T(8,128)(2,1)S(1)}, bf16[128,640]{1,0:T(8,128)(2,1)S(1)}, u32[]{:S(2)}, u32[]{:S(2)}) collective-permute-start(bf16[128,640]{1,0:T(8,128)(2,1)S(1)} %get-tuple-element.87.refs_0_), channel_id=1, source_target_pairs={{1,97},{3,99},{5,101},{7,103},{9,105},{11,107},{13,109},{15,111},{... | collective-permute-start | bytes 491528 | tf_op jit(solution)/shard_map/ppermute | solution.py:20
  112.0 15.8 %collective-permute-start.17 = (bf16[256,640]{1,0:T(8,128)(2,1)S(1)}, bf16[256,640]{1,0:T(8,128)(2,1)S(1)}, u32[]{:S(2)}, u32[]{:S(2)}) collective-permute-start(bf16[256,640]{1,0:T(8,128)(2,1)S(1)} %get-tuple-element.84), channel_id=1, source_target_pairs={{1,0},{3,2},{5,4},{7,6},{9,8},{11,10},{13,12},{15,14},{17,16},{19,... | collective-permute-start | bytes 983048 | tf_op jit(solution)/shard_map/ppermute | solution.py:25
  113.4 14.4 %collective-permute-start.15 = (bf16[192,512]{1,0:T(8,128)(2,1)S(1)}, bf16[192,512]{1,0:T(8,128)(2,1)S(1)}, u32[]{:S(2)}, u32[]{:S(2)}) collective-permute-start(bf16[192,512]{1,0:T(8,128)(2,1)S(1)} %get-tuple-element.82.refs_0_), channel_id=1, source_target_pairs={{0,32},{2,34},{4,36},{6,38},{8,40},{10,42},{12,44},{14,46},{16,48}... | collective-permute-start | bytes 589832 | tf_op jit(solution)/shard_map/ppermute | solution.py:20
  118.8 5.4 %collective-permute-start.22 = (bf16[128,384]{1,0:T(8,128)(2,1)S(1)}, bf16[128,384]{1,0:T(8,128)(2,1)S(1)}, u32[]{:S(2)}, u32[]{:S(2)}) collective-permute-start(bf16[128,384]{1,0:T(8,128)(2,1)S(1)} %get-tuple-element.91.refs_0_), channel_id=1, source_target_pairs={{1,129},{3,131},{5,133},{7,135},{9,137},{11,139},{13,141},{15,143}... | collective-permute-start | bytes 294920 | tf_op jit(solution)/shard_map/ppermute | solution.py:20
  120.7 7.8 %collective-permute-start.20 = (bf16[256,512]{1,0:T(8,128)(2,1)S(1)}, bf16[256,512]{1,0:T(8,128)(2,1)S(1)}, u32[]{:S(2)}, u32[]{:S(2)}) collective-permute-start(bf16[256,512]{1,0:T(8,128)(2,1)S(1)} %get-tuple-element.88), channel_id=1, source_target_pairs={{1,0},{3,2},{5,4},{7,6},{9,8},{11,10},{13,12},{15,14},{17,16},{19,... | collective-permute-start | bytes 786440 | tf_op jit(solution)/shard_map/ppermute | solution.py:25
  124.4 6.2 %collective-permute-start.28 = (bf16[128,256]{1,0:T(8,128)(2,1)S(1)}, bf16[128,256]{1,0:T(8,128)(2,1)S(1)}, u32[]{:S(2)}, u32[]{:S(2)}) collective-permute-start(bf16[128,256]{1,0:T(8,128)(2,1)S(1)} %get-tuple-element.98.refs_0_), channel_id=1, source_target_pairs={{1,385},{3,387},{5,389},{7,391},{9,393},{11,395},{13,397},{15,399}... | collective-permute-start | bytes 196616 | tf_op jit(solution)/shard_map/ppermute | solution.py:20
  126.4 7.3 %collective-permute-start.23 = (bf16[256,384]{1,0:T(8,128)(2,1)S(1)}, bf16[256,384]{1,0:T(8,128)(2,1)S(1)}, u32[]{:S(2)}, u32[]{:S(2)}) collective-permute-start(bf16[256,384]{1,0:T(8,128)(2,1)S(1)} %get-tuple-element.92), channel_id=1, source_target_pairs={{1,0},{3,2},{5,4},{7,6},{9,8},{11,10},{13,12},{15,14},{17,16},{19,... | collective-permute-start | bytes 589832 | tf_op jit(solution)/shard_map/ppermute | solution.py:25
  127.8 0.7 collective-permute-start.18
  128.5 5.3 %collective-permute-start.21 = (bf16[192,256]{1,0:T(8,128)(2,1)S(1)}, bf16[192,256]{1,0:T(8,128)(2,1)S(1)}, u32[]{:S(2)}, u32[]{:S(2)}) collective-permute-start(bf16[192,256]{1,0:T(8,128)(2,1)S(1)} %get-tuple-element.90.refs_0_), channel_id=1, source_target_pairs={{0,128},{2,130},{4,132},{6,134},{8,136},{10,138},{12,140},{14,142}... | collective-permute-start | bytes 294920 | tf_op jit(solution)/shard_map/ppermute | solution.py:20
  129.2 9.9 %collective-permute-start.24 = (bf16[6,192,128]{2,1,0:T(8,128)(2,1)S(1)}, bf16[6,192,128]{2,1,0:T(8,128)(2,1)S(1)}, u32[]{:S(2)}, u32[]{:S(2)}) collective-permute-start(bf16[6,192,128]{2,1,0:T(8,128)(2,1)S(1)} %get-tuple-element.95), channel_id=1, source_target_pairs={{0,2},{2,0},{4,6},{6,4},{8,10},{10,8},{12,14},{14,12},{16,18},{18,... | collective-permute-start | bytes 884744 | tf_op jit(solution)/shard_map/ppermute | solution.py:20
  130.8 6.3 %collective-permute-start.29 = (bf16[256,256]{1,0:T(8,128)(2,1)S(1)}, bf16[256,256]{1,0:T(8,128)(2,1)S(1)}, u32[]{:S(2)}, u32[]{:S(2)}) collective-permute-start(bf16[256,256]{1,0:T(8,128)(2,1)S(1)} %shard_map.77), channel_id=1, source_target_pairs={{1,0},{3,2},{5,4},{7,6},{9,8},{11,10},{13,12},{15,14},{17,16},{19,... | collective-permute-start | bytes 393224 | tf_op jit(solution)/shard_map/ppermute | solution.py:25
  133.8 6.6 %collective-permute-start.25 = (bf16[6,192,128]{2,1,0:T(8,128)(2,1)S(1)}, bf16[6,192,128]{2,1,0:T(8,128)(2,1)S(1)}, u32[]{:S(2)}, u32[]{:S(2)}) collective-permute-start(bf16[6,192,128]{2,1,0:T(8,128)(2,1)S(1)} %get-tuple-element.94.refs_7_), channel_id=1, source_target_pairs={{0,1},{2,3},{4,5},{6,7},{8,9},{10,11},{12,13},{14,15},{16,17},{18,... | collective-permute-start | bytes 884744 | tf_op jit(solution)/shard_map/ppermute | solution.py:25
  135.1 8.0 %collective-permute-start.26 = (bf16[6,192,128]{2,1,0:T(8,128)(2,1)S(1)}, bf16[6,192,128]{2,1,0:T(8,128)(2,1)S(1)}, u32[]{:S(2)}, u32[]{:S(2)}) collective-permute-start(bf16[6,192,128]{2,1,0:T(8,128)(2,1)S(1)} %get-tuple-element.95), channel_id=1, source_target_pairs={{2,1},{0,3},{6,5},{4,7},{10,9},{8,11},{14,13},{12,15},{18,17},{16,... | collective-permute-start | bytes 884744 | tf_op jit(solution)/shard_map/ppermute | solution.py:25
  137.2 6.9 %collective-permute-start.30 = (bf16[2,192,128]{2,1,0:T(8,128)(2,1)S(1)}, bf16[2,192,128]{2,1,0:T(8,128)(2,1)S(1)}, u32[]{:S(2)}, u32[]{:S(2)}) collective-permute-start(bf16[2,192,128]{2,1,0:T(8,128)(2,1)S(1)} %pad_maximum_fusion.refs_3_), channel_id=1, source_target_pairs={{0,2},{2,0},{4,6},{6,4},{8,10},{10,8},{12,14},{14,12},{16,18},{18,... | collective-permute-start | bytes 294920 | tf_op jit(solution)/shard_map/ppermute | solution.py:20
  137.8 12.8 %collective-permute-start.31 = (bf16[2,192,128]{2,1,0:T(8,128)(2,1)S(1)}, bf16[2,192,128]{2,1,0:T(8,128)(2,1)S(1)}, u32[]{:S(2)}, u32[]{:S(2)}) collective-permute-start(bf16[2,192,128]{2,1,0:T(8,128)(2,1)S(1)} %pad_maximum_fusion.refs_3_), channel_id=1, source_target_pairs={{0,1},{2,3},{4,5},{6,7},{8,9},{10,11},{12,13},{14,15},{16,17},{18,... | collective-permute-start | bytes 294920 | tf_op jit(solution)/shard_map/ppermute | solution.py:25
  139.1 14.5 %collective-permute-start.32 = (bf16[2,192,128]{2,1,0:T(8,128)(2,1)S(1)}, bf16[2,192,128]{2,1,0:T(8,128)(2,1)S(1)}, u32[]{:S(2)}, u32[]{:S(2)}) collective-permute-start(bf16[2,192,128]{2,1,0:T(8,128)(2,1)S(1)} %pad_maximum_fusion.refs_3_), channel_id=1, source_target_pairs={{2,1},{0,3},{6,5},{4,7},{10,9},{8,11},{14,13},{12,15},{18,17},{16,... | collective-permute-start | bytes 294920 | tf_op jit(solution)/shard_map/ppermute | solution.py:25
  (8 other events, 25.9 us)

commit v7 on v6

--- a/solution.py
+++ b/solution.py
@@ -115,27 +115,18 @@
             out_ref[...] = (own[rows, :].astype(F32) + other[rows, :].astype(F32)).astype(BF)
 
 
-def cut_body(own_any, other_any, capacity_ref, message_ref, keep_ref, own, other, sems, *, first, last):
+def cut_body(own_any, other_any, capacity_ref, message_ref, own, other, sems, *, first):
     @pl.when(bit(0) == 1)
     def _():
         fetch([(own_any, own), (other_any, other)], sems)
         inner = capacity_ref.shape[2]
-        count = own.shape[0] // 2
-        part = (own.shape[1] - last) // 2
-
-        def total(rows, low, high):
-            return (own[rows, low:high].astype(F32) + other[rows, low:high].astype(F32)).astype(BF)
-
-        message_ref[:, :first] = total(slice(None), 0, first)
+        for low, high, at in ((0, first, 0), (first, own.shape[1], first + inner)):
+            total = own[:, low:high].astype(F32) + other[:, low:high].astype(F32)
+            message_ref[:, at : at + high - low] = total.astype(BF)
         message_ref[:, first : first + inner] = capacity_ref[0]
-        message_ref[:, first + inner : last + inner] = total(slice(None), first, last)
-        for place, out_ref, at in ((bit(1), keep_ref, 0), (1 - bit(1), message_ref, last + inner)):
-            rows = rows_of(place, count)
-            out_ref[:count, at:] = total(rows, last, last + part)
-            out_ref[count:, at:] = total(rows, last + part, last + 2 * part)
-
-
-def static_body(own_any, other_any, keep_ref, capacity_ref, *refs, cut, width, outs, kept):
+
+
+def static_body(own_any, other_any, capacity_ref, *refs, cut, width, outs):
     out_refs, (own, other, sems) = refs[:outs], refs[outs:]
 
     @pl.when(bit(0) == 1)
@@ -155,38 +146,8 @@
         if width:
             message_ref[:, :width] = total(cut, cut + width)
         message_ref[:, width : width + inner] = capacity_ref[0]
-        end = own.shape[1] - kept
-        if end > cut + width:
-            message_ref[:, width + inner : end - cut + inner] = total(cut + width, end)
-        if kept:
-            rest = keep_ref[...].astype(F32) + other[:, end:].astype(F32)
-            message_ref[:, end - cut + inner :] = rest.astype(BF)
-
-
-def tail_body(own_any, other_any, out_ref, own, other, sems, *, cut):
-    @pl.when(bit(0) == 1)
-    def _():
-        fetch([(own_any, own), (other_any, other)], sems)
-        out_ref[...] = (own[:, cut:].astype(F32) + other[:, cut:].astype(F32)).astype(BF)
-
-
-def join_body(own_ref, other_ref, capacity_ref, message_ref, *, width):
-    @pl.when(bit(0) == 1)
-    def _():
-        inner = capacity_ref.shape[2]
-        part = own_ref.shape[1]
-        count = own_ref.shape[0] // 2
-        message_ref[:, width : width + inner] = capacity_ref[0]
-        for place, ref in ((bit(1), own_ref), (1 - bit(1), other_ref)):
-            rows = rows_of(place, count)
-            for half in range(2):
-                low, high = half * part, (half + 1) * part
-                middle = min(max(low, width), high)
-                block = ref[half * count : (half + 1) * count, :]
-                if middle > low:
-                    message_ref[rows, low:middle] = block[:, : middle - low]
-                if high > middle:
-                    message_ref[rows, middle + inner : high + inner] = block[:, middle - low :]
+        if own.shape[1] > cut + width:
+            message_ref[:, width + inner :] = total(cut + width, own.shape[1])
 
 
 def step_body(own_ref, other_ref, static_ref, *out_refs, level):
@@ -246,23 +207,21 @@
         [VMEM, VMEM, level_block(project_rows, 0)],
     )
     static_other, sums = lax.optimization_barrier((static_other, sums))
-    stacked = lax.all_gather(
-        sums, AXIS, axis_index_groups=[[d, d + 1] for d in range(0, size, 2)], tiled=True
-    )
     def blocks(low, high):
         return sum(levels - 1 - level for level in range(low, min(high, levels - 1))) * rank
 
-    split = 4
-    rest = blocks(split, levels) // 2
-    message, keep = call(
-        lambda *refs: cut_body(*refs, first=blocks(1, 2), last=blocks(1, split)),
-        [sds((rank, blocks(1, split) + inner + rest), BF), sds((rank, rest), BF)],
+    (message,) = call(
+        lambda *refs: cut_body(*refs, first=blocks(1, 2)),
+        [sds((rank, pairs * rank + inner), BF)],
         [static, static_other, capacity],
         [ANY, ANY, level_block(capacity, 1)],
         [like(static), like(static), dma((2,))],
     )
-    stacked, message = lax.optimization_barrier((stacked, message))
     static_got = swap(message, mask_of(1), 1)
+    sums, message = lax.optimization_barrier((sums, message))
+    stacked = lax.all_gather(
+        sums, AXIS, axis_index_groups=[[d, d + 1] for d in range(0, size, 2)], tiled=True
+    )
     zero, sums = call(
         first_body,
         [sds((rank, columns), BF), sds((columns, (levels - 1) * rank), BF)],
@@ -308,45 +267,24 @@
     gathered = []
     early = levels - 3
     for level in range(1, levels):
-        if level == split - 1:
-            other = swap(send, mask_of(level), 0)
-        plain = level == split - 1 and rest > 0
         outs = [sds((2 * rank, blocks(level, level + 1) + inner), BF)]
-        if level < levels - 1 and not plain:
-            late = rest if level < split else blocks(level + 2, levels)
-            outs.append(sds((rank, blocks(level + 1, max(split, level + 2) if level < split else level + 2) + inner + late), BF))
+        if level < levels - 1:
+            outs.append(sds((rank, blocks(level + 1, levels) + inner), BF))
         results = call(
             lambda *refs, l=level, n=len(outs): static_body(
-                *refs, cut=blocks(l, l + 1) + inner, width=blocks(l + 1, l + 2), outs=n, kept=rest if l == 1 else 0
+                *refs, cut=blocks(l, l + 1) + inner, width=blocks(l + 1, l + 2), outs=n
             ),
             outs,
-            [message, static_got, keep, capacity],
-            [ANY, ANY, VMEM, level_block(capacity, min(level + 1, levels - 1))],
+            [message, static_got, capacity],
+            [ANY, ANY, level_block(capacity, min(level + 1, levels - 1))],
             [like(message), like(message), dma((2,))],
         )
         static_block = to_core(results[0], 0)
-        if plain:
-            static_got, other, static_block = lax.optimization_barrier((static_got, other, static_block))
-            (tail,) = call(
-                lambda *refs, c=blocks(level, level + 1) + inner: tail_body(*refs, cut=c),
-                [sds((rank, rest), BF)],
-                [message, static_got],
-                [ANY, ANY],
-                [like(message), like(message), dma((2,))],
-            )
-            (message,) = call(
-                lambda *refs: join_body(*refs, width=blocks(split, split + 1)),
-                [sds((rank, 2 * rest + inner), BF)],
-                [tail, swap(tail, 2, 1), capacity],
-                [VMEM, VMEM, level_block(capacity, split)],
-            )
-        elif level < levels - 1:
+        if level < levels - 1:
             message = results[1]
-        if level < levels - 1:
             static_got = swap(message, mask_of(level + 1), 1)
 
-        if level != split - 1:
-            other = swap(send, mask_of(level), 0)
+        other = swap(send, mask_of(level), 0)
         width = (levels - 1 - level) * rank
         outs = [sds((half, 2 * rank if level == 1 else rank), BF)]
         if width:
@@ -360,7 +298,7 @@
         gathered.append(results[0])
         if width:
             own = results[1]
-            if level < split - 1:
+            if level < 3:
                 own, static_got = lax.optimization_barrier((own, static_got))
             send = own
         if level == early:

time: 156 us -> 150 us (0.962)
  the two profiles are of different devices: /device:TPU:1 before, /device:TPU:8 now
where the time goes in v7:
time: 150 us
  waiting for transfers between devices  75.7 us (50%)
  starting transfers between devices  55.9 us (37%)
  Pallas kernels  8.92 us (6%)
  blocking collectives  5.76 us (4%)
  local copies, waits for them, and re-layouts  2.67 us (2%)
    ppermute x18, waiting for transfers between devices, swap(): return lax.ppermute(value, AXIS, pairs)  43.7 us
    ppermute x18, starting transfers between devices, swap(): return lax.ppermute(value, AXIS, pairs)  34.1 us
    ppermute x14, waiting for transfers between devices, to_core(): return lax.ppermute(value, AXIS, pairs)  32 us
    ppermute x14, starting transfers between devices, to_core(): return lax.ppermute(value, AXIS, pairs)  21.8 us
    pallas_call x23, Pallas kernels, call(): pl.pallas_call(body, out_shape=outs, grid=grid, in_specs=specs, out_specs...  8.92 us
    all_gather x1, blocking collectives, on_device(): lax.all_gather(sums, AXIS, axis_index_groups=[[d, d + 1] for d in range(0...  5.76 us
  transfers between devices with their start and end apart: 32, of which 15 were waited for; matrix products, arithmetic and copies ran while one was open for 0% of the time, Pallas kernels for 4%

profile of v7, /device:TPU:8, one launch (start us, length us, event | category | flops | bytes accessed | tf_op | source)
XLA Modules:
  0.0 149.6 jit_solution(9019101576416570184)
XLA Ops:
  3.7 1.9 %collective-permute-start = (bf16[128,3584]{1,0:T(8,128)(2,1)S(1)}, bf16[128,3584]{1,0:T(8,128)(2,1)S(1)}, u32[]{:S(2)}, u32[]{:S(2)}) collective-permute-start(bf16[128,3584]{1,0:T(8,128)(2,1)S(1)} %shard_map.56.refs_0_), channel_id=1, source_target_pairs={{0,1},{2,3},{4,5},{6,7},{8,9},{10,11},{12,13},{14,15},{16,17},{18,... | collective-permute-start | bytes 2752520 | tf_op jit(solution)/shard_map/ppermute | solution.py:25
  6.3 1.4 collective-permute-done.refs_1_
  8.6 5.8 %all_gather.3.stacked_ref = bf16[256,384]{1,0:T(8,128)(2,1)S(1)} all-gather(bf16[128,384]{1,0:T(8,128)(2,1)S(1)} %get-tuple-element.53), channel_id=1, replica_groups={{0,1},{2,3},{4,5},{6,7},{8,9},{10,11},{12,13},{14,15},{16,17},{18,19},{..., dimensions={0}, use_global_device_ids=true | all-gather | bytes 294912 | tf_op jit(solution)/shard_map/all_gather | solution.py:222
  14.3 1.4 shard_map.58
  20.2 2.2 %collective-permute-start.2 = (bf16[192,1024]{1,0:T(8,128)(2,1)S(1)}, bf16[192,1024]{1,0:T(8,128)(2,1)S(1)}, u32[]{:S(2)}, u32[]{:S(2)}) collective-permute-start(bf16[192,1024]{1,0:T(8,128)(2,1)S(1)} %get-tuple-element.56), channel_id=1, source_target_pairs={{0,2},{2,0},{4,6},{6,4},{8,10},{10,8},{12,14},{14,12},{16,18},{18,... | collective-permute-start | bytes 1179656 | tf_op jit(solution)/shard_map/ppermute | solution.py:20
  22.4 7.5 %collective-permute-done.2.refs_1_ = bf16[192,1024]{1,0:T(8,128)(2,1)S(1)} collective-permute-done((bf16[192,1024]{1,0:T(8,128)(2,1)S(1)}, bf16[192,1024]{1,0:T(8,128)(2,1)S(1)}, u32[]{:S(2)}, u32[]{:S(2)}) %collective-permute-start.2) | collective-permute-done | bytes 393248 | tf_op jit(solution)/shard_map/ppermute | solution.py:20
  29.9 3.8 %collective-permute-done.4.refs_2_ = bf16[256,1152]{1,0:T(8,128)(2,1)S(1)} collective-permute-done((bf16[256,1152]{1,0:T(8,128)(2,1)S(1)}, bf16[256,1152]{1,0:T(8,128)(2,1)S(1)}, u32[]{:S(2)}, u32[]{:S(2)}) %collective-permute-start.4) | collective-permute-done | bytes 589856 | tf_op jit(solution)/shard_map/ppermute | solution.py:25
  36.2 2.3 %collective-permute-start.6 = (bf16[192,896]{1,0:T(8,128)(2,1)S(1)}, bf16[192,896]{1,0:T(8,128)(2,1)S(1)}, u32[]{:S(2)}, u32[]{:S(2)}) collective-permute-start(bf16[192,896]{1,0:T(8,128)(2,1)S(1)} %get-tuple-element.62.refs_0_), channel_id=1, source_target_pairs={{0,4},{2,6},{4,0},{6,2},{8,12},{10,14},{12,8},{14,10},{16,20},{18,... | collective-permute-start | bytes 1032200 | tf_op jit(solution)/shard_map/ppermute | solution.py:20
  38.5 15.2 %collective-permute-done.6.refs_1_ = bf16[192,896]{1,0:T(8,128)(2,1)S(1)} collective-permute-done((bf16[192,896]{1,0:T(8,128)(2,1)S(1)}, bf16[192,896]{1,0:T(8,128)(2,1)S(1)}, u32[]{:S(2)}, u32[]{:S(2)}) %collective-permute-start.6) | collective-permute-done | bytes 344096 | tf_op jit(solution)/shard_map/ppermute | solution.py:20
  53.7 11.1 %collective-permute-done.7.refs_2_ = bf16[256,1024]{1,0:T(8,128)(2,1)S(1)} collective-permute-done((bf16[256,1024]{1,0:T(8,128)(2,1)S(1)}, bf16[256,1024]{1,0:T(8,128)(2,1)S(1)}, u32[]{:S(2)}, u32[]{:S(2)}) %collective-permute-start.7) | collective-permute-done | bytes 524320 | tf_op jit(solution)/shard_map/ppermute | solution.py:25
  67.3 2.2 %collective-permute-start.9 = (bf16[192,768]{1,0:T(8,128)(2,1)S(1)}, bf16[192,768]{1,0:T(8,128)(2,1)S(1)}, u32[]{:S(2)}, u32[]{:S(2)}) collective-permute-start(bf16[192,768]{1,0:T(8,128)(2,1)S(1)} %get-tuple-element.68.refs_0_), channel_id=1, source_target_pairs={{0,12},{2,14},{4,8},{6,10},{8,4},{10,6},{12,0},{14,2},{16,28},{18,... | collective-permute-start | bytes 884744 | tf_op jit(solution)/shard_map/ppermute | solution.py:20
  70.2 1.3 collective-permute-start.13
  71.5 9.2 %collective-permute-done.9.refs_1_ = bf16[192,768]{1,0:T(8,128)(2,1)S(1)} collective-permute-done((bf16[192,768]{1,0:T(8,128)(2,1)S(1)}, bf16[192,768]{1,0:T(8,128)(2,1)S(1)}, u32[]{:S(2)}, u32[]{:S(2)}) %collective-permute-start.9) | collective-permute-done | bytes 294944 | tf_op jit(solution)/shard_map/ppermute | solution.py:20
  80.7 4.1 %collective-permute-done.10.refs_2_ = bf16[256,896]{1,0:T(8,128)(2,1)S(1)} collective-permute-done((bf16[256,896]{1,0:T(8,128)(2,1)S(1)}, bf16[256,896]{1,0:T(8,128)(2,1)S(1)}, u32[]{:S(2)}, u32[]{:S(2)}) %collective-permute-start.10) | collective-permute-done | bytes 458784 | tf_op jit(solution)/shard_map/ppermute | solution.py:25
  85.3 3.6 %collective-permute-start.11 = (bf16[192,640]{1,0:T(8,128)(2,1)S(1)}, bf16[192,640]{1,0:T(8,128)(2,1)S(1)}, u32[]{:S(2)}, u32[]{:S(2)}) collective-permute-start(bf16[192,640]{1,0:T(8,128)(2,1)S(1)} %get-tuple-element.72.refs_0_), channel_id=1, source_target_pairs={{0,16},{2,18},{4,20},{6,22},{8,24},{10,26},{12,28},{14,30},{16,0},... | collective-permute-start | bytes 737288 | tf_op jit(solution)/shard_map/ppermute | solution.py:20
  91.0 2.4 %collective-permute-done.11.refs_1_ = bf16[192,640]{1,0:T(8,128)(2,1)S(1)} collective-permute-done((bf16[192,640]{1,0:T(8,128)(2,1)S(1)}, bf16[192,640]{1,0:T(8,128)(2,1)S(1)}, u32[]{:S(2)}, u32[]{:S(2)}) %collective-permute-start.11) | collective-permute-done | bytes 245792 | tf_op jit(solution)/shard_map/ppermute | solution.py:20
  93.4 2.7 %collective-permute-done.13.refs_2_ = bf16[256,768]{1,0:T(8,128)(2,1)S(1)} collective-permute-done((bf16[256,768]{1,0:T(8,128)(2,1)S(1)}, bf16[256,768]{1,0:T(8,128)(2,1)S(1)}, u32[]{:S(2)}, u32[]{:S(2)}) %collective-permute-start.13) | collective-permute-done | bytes 393248 | tf_op jit(solution)/shard_map/ppermute | solution.py:25
  96.5 2.2 %collective-permute-start.14 = (bf16[192,512]{1,0:T(8,128)(2,1)S(1)}, bf16[192,512]{1,0:T(8,128)(2,1)S(1)}, u32[]{:S(2)}, u32[]{:S(2)}) collective-permute-start(bf16[192,512]{1,0:T(8,128)(2,1)S(1)} %get-tuple-element.76.refs_0_), channel_id=1, source_target_pairs={{0,32},{2,34},{4,36},{6,38},{8,40},{10,42},{12,44},{14,46},{16,48}... | collective-permute-start | bytes 589832 | tf_op jit(solution)/shard_map/ppermute | solution.py:20
  102.8 4.9 %collective-permute-done.16.refs_2_ = bf16[256,640]{1,0:T(8,128)(2,1)S(1)} collective-permute-done((bf16[256,640]{1,0:T(8,128)(2,1)S(1)}, bf16[256,640]{1,0:T(8,128)(2,1)S(1)}, u32[]{:S(2)}, u32[]{:S(2)}) %collective-permute-start.16) | collective-permute-done | bytes 327712 | tf_op jit(solution)/shard_map/ppermute | solution.py:25
  108.1 4.3 %collective-permute-start.17 = (bf16[192,384]{1,0:T(8,128)(2,1)S(1)}, bf16[192,384]{1,0:T(8,128)(2,1)S(1)}, u32[]{:S(2)}, u32[]{:S(2)}) collective-permute-start(bf16[192,384]{1,0:T(8,128)(2,1)S(1)} %get-tuple-element.80.refs_0_), channel_id=1, source_target_pairs={{0,96},{2,98},{4,100},{6,102},{8,104},{10,106},{12,108},{14,110},{... | collective-permute-start | bytes 442376 | tf_op jit(solution)/shard_map/ppermute | solution.py:20
  112.4 3.2 %collective-permute-done.19.refs_2_ = bf16[256,512]{1,0:T(8,128)(2,1)S(1)} collective-permute-done((bf16[256,512]{1,0:T(8,128)(2,1)S(1)}, bf16[256,512]{1,0:T(8,128)(2,1)S(1)}, u32[]{:S(2)}, u32[]{:S(2)}) %collective-permute-start.19) | collective-permute-done | bytes 262176 | tf_op jit(solution)/shard_map/ppermute | solution.py:25
  115.6 3.0 %collective-permute-done.17.refs_1_ = bf16[192,384]{1,0:T(8,128)(2,1)S(1)} collective-permute-done((bf16[192,384]{1,0:T(8,128)(2,1)S(1)}, bf16[192,384]{1,0:T(8,128)(2,1)S(1)}, u32[]{:S(2)}, u32[]{:S(2)}) %collective-permute-start.17) | collective-permute-done | bytes 147488 | tf_op jit(solution)/shard_map/ppermute | solution.py:20
  119.0 3.4 %collective-permute-start.20 = (bf16[192,256]{1,0:T(8,128)(2,1)S(1)}, bf16[192,256]{1,0:T(8,128)(2,1)S(1)}, u32[]{:S(2)}, u32[]{:S(2)}) collective-permute-start(bf16[192,256]{1,0:T(8,128)(2,1)S(1)} %get-tuple-element.84.refs_0_), channel_id=1, source_target_pairs={{0,128},{2,130},{4,132},{6,134},{8,136},{10,138},{12,140},{14,142}... | collective-permute-start | bytes 294920 | tf_op jit(solution)/shard_map/ppermute | solution.py:20
  122.4 1.9 %collective-permute-start.23 = (bf16[6,192,128]{2,1,0:T(8,128)(2,1)S(1)}, bf16[6,192,128]{2,1,0:T(8,128)(2,1)S(1)}, u32[]{:S(2)}, u32[]{:S(2)}) collective-permute-start(bf16[6,192,128]{2,1,0:T(8,128)(2,1)S(1)} %get-tuple-element.89), channel_id=1, source_target_pairs={{0,2},{2,0},{4,6},{6,4},{8,10},{10,8},{12,14},{14,12},{16,18},{18,... | collective-permute-start | bytes 884744 | tf_op jit(solution)/shard_map/ppermute | solution.py:20
  126.1 4.3 %collective-permute-start.25 = (bf16[6,192,128]{2,1,0:T(8,128)(2,1)S(1)}, bf16[6,192,128]{2,1,0:T(8,128)(2,1)S(1)}, u32[]{:S(2)}, u32[]{:S(2)}) collective-permute-start(bf16[6,192,128]{2,1,0:T(8,128)(2,1)S(1)} %get-tuple-element.89), channel_id=1, source_target_pairs={{2,1},{0,3},{6,5},{4,7},{10,9},{8,11},{14,13},{12,15},{18,17},{16,... | collective-permute-start | bytes 884744 | tf_op jit(solution)/shard_map/ppermute | solution.py:25
  130.4 1.3 collective-permute-start.24
  131.7 4.0 %collective-permute-start.26 = (bf16[192,128]{1,0:T(8,128)(2,1)S(1)}, bf16[192,128]{1,0:T(8,128)(2,1)S(1)}, u32[]{:S(2)}, u32[]{:S(2)}) collective-permute-start(bf16[192,128]{1,0:T(8,128)(2,1)S(1)} %get-tuple-element.91.refs_0_), channel_id=1, source_target_pairs={{0,384},{2,386},{4,388},{6,390},{8,392},{10,394},{12,396},{14,398}... | collective-permute-start | bytes 147464 | tf_op jit(solution)/shard_map/ppermute | solution.py:20
  135.8 3.2 %collective-permute-done.26.refs_1_ = bf16[192,128]{1,0:T(8,128)(2,1)S(1)} collective-permute-done((bf16[192,128]{1,0:T(8,128)(2,1)S(1)}, bf16[192,128]{1,0:T(8,128)(2,1)S(1)}, u32[]{:S(2)}, u32[]{:S(2)}) %collective-permute-start.26) | collective-permute-done | bytes 49184 | tf_op jit(solution)/shard_map/ppermute | solution.py:20
  139.2 1.3 collective-permute-start.31
  140.5 1.3 collective-permute-start.30
  141.8 2.3 %collective-permute-start.29 = (bf16[2,192,128]{2,1,0:T(8,128)(2,1)S(1)}, bf16[2,192,128]{2,1,0:T(8,128)(2,1)S(1)}, u32[]{:S(2)}, u32[]{:S(2)}) collective-permute-start(bf16[2,192,128]{2,1,0:T(8,128)(2,1)S(1)} %pad_maximum_fusion.refs_3_), channel_id=1, source_target_pairs={{0,2},{2,0},{4,6},{6,4},{8,10},{10,8},{12,14},{14,12},{16,18},{18,... | collective-permute-start | bytes 294920 | tf_op jit(solution)/shard_map/ppermute | solution.py:20
  145.0 3.3 %collective-permute-done.29.refs_4_ = bf16[2,192,128]{2,1,0:T(8,128)(2,1)S(1)} collective-permute-done((bf16[2,192,128]{2,1,0:T(8,128)(2,1)S(1)}, bf16[2,192,128]{2,1,0:T(8,128)(2,1)S(1)}, u32[]{:S(2)}, u32[]{:S(2)}) %collective-permute-start.29) | collective-permute-done | bytes 98336 | tf_op jit(solution)/shard_map/ppermute | solution.py:20
  (77 shorter events, 27.1 us)
Async XLA Ops:
  3.7 4.0 %collective-permute-start = (bf16[128,3584]{1,0:T(8,128)(2,1)S(1)}, bf16[128,3584]{1,0:T(8,128)(2,1)S(1)}, u32[]{:S(2)}, u32[]{:S(2)}) collective-permute-start(bf16[128,3584]{1,0:T(8,128)(2,1)S(1)} %shard_map.56.refs_0_), channel_id=1, source_target_pairs={{0,1},{2,3},{4,5},{6,7},{8,9},{10,11},{12,13},{14,15},{16,17},{18,... | collective-permute-start | bytes 2752520 | tf_op jit(solution)/shard_map/ppermute | solution.py:25
  7.7 9.3 %collective-permute-start.3 = (bf16[128,3840]{1,0:T(8,128)(2,1)S(1)}, bf16[128,3840]{1,0:T(8,128)(2,1)S(1)}, u32[]{:S(2)}, u32[]{:S(2)}) collective-permute-start(bf16[128,3840]{1,0:T(8,128)(2,1)S(1)} %shard_map.57.refs_0_), channel_id=1, source_target_pairs={{1,3},{3,1},{5,7},{7,5},{9,11},{11,9},{13,15},{15,13},{17,19},{19,... | collective-permute-start | bytes 2949128 | tf_op jit(solution)/shard_map/ppermute | solution.py:20
  15.7 4.2 %collective-permute-start.1 = (bf16[384,1024]{1,0:T(8,128)(2,1)S(1)}, bf16[384,1024]{1,0:T(8,128)(2,1)S(1)}, u32[]{:S(2)}, u32[]{:S(2)}) collective-permute-start(bf16[384,1024]{1,0:T(8,128)(2,1)S(1)} %get-tuple-element.54.own_any), channel_id=1, source_target_pairs={{1,0},{3,2},{5,4},{7,6},{9,8},{11,10},{13,12},{15,14},{17,16},{19,... | collective-permute-start | bytes 2359304 | tf_op jit(solution)/shard_map/ppermute | solution.py:25
  17.1 17.1 %collective-permute-start.5 = (bf16[128,2944]{1,0:T(8,128)(2,1)S(1)}, bf16[128,2944]{1,0:T(8,128)(2,1)S(1)}, u32[]{:S(2)}, u32[]{:S(2)}) collective-permute-start(bf16[128,2944]{1,0:T(8,128)(2,1)S(1)} %get-tuple-element.61.refs_0_), channel_id=1, source_target_pairs={{1,5},{3,7},{5,1},{7,3},{9,13},{11,15},{13,9},{15,11},{17,21},{19,... | collective-permute-start | bytes 2261000 | tf_op jit(solution)/shard_map/ppermute | solution.py:20
  17.8 15.9 %collective-permute-start.4 = (bf16[256,1152]{1,0:T(8,128)(2,1)S(1)}, bf16[256,1152]{1,0:T(8,128)(2,1)S(1)}, u32[]{:S(2)}, u32[]{:S(2)}) collective-permute-start(bf16[256,1152]{1,0:T(8,128)(2,1)S(1)} %get-tuple-element.58), channel_id=1, source_target_pairs={{1,0},{3,2},{5,4},{7,6},{9,8},{11,10},{13,12},{15,14},{17,16},{19,... | collective-permute-start | bytes 1769480 | tf_op jit(solution)/shard_map/ppermute | solution.py:25
  20.2 9.7 %collective-permute-start.2 = (bf16[192,1024]{1,0:T(8,128)(2,1)S(1)}, bf16[192,1024]{1,0:T(8,128)(2,1)S(1)}, u32[]{:S(2)}, u32[]{:S(2)}) collective-permute-start(bf16[192,1024]{1,0:T(8,128)(2,1)S(1)} %get-tuple-element.56), channel_id=1, source_target_pairs={{0,2},{2,0},{4,6},{6,4},{8,10},{10,8},{12,14},{14,12},{16,18},{18,... | collective-permute-start | bytes 1179656 | tf_op jit(solution)/shard_map/ppermute | solution.py:20
  34.2 31.1 %collective-permute-start.8 = (bf16[128,2176]{1,0:T(8,128)(2,1)S(1)}, bf16[128,2176]{1,0:T(8,128)(2,1)S(1)}, u32[]{:S(2)}, u32[]{:S(2)}) collective-permute-start(bf16[128,2176]{1,0:T(8,128)(2,1)S(1)} %get-tuple-element.67.refs_0_), channel_id=1, source_target_pairs={{1,13},{3,15},{5,9},{7,11},{9,5},{11,7},{13,1},{15,3},{17,29},{19,... | collective-permute-start | bytes 1671176 | tf_op jit(solution)/shard_map/ppermute | solution.py:20
  34.9 29.9 %collective-permute-start.7 = (bf16[256,1024]{1,0:T(8,128)(2,1)S(1)}, bf16[256,1024]{1,0:T(8,128)(2,1)S(1)}, u32[]{:S(2)}, u32[]{:S(2)}) collective-permute-start(bf16[256,1024]{1,0:T(8,128)(2,1)S(1)} %get-tuple-element.64), channel_id=1, source_target_pairs={{1,0},{3,2},{5,4},{7,6},{9,8},{11,10},{13,12},{15,14},{17,16},{19,... | collective-permute-start | bytes 1572872 | tf_op jit(solution)/shard_map/ppermute | solution.py:25
  36.2 17.5 %collective-permute-start.6 = (bf16[192,896]{1,0:T(8,128)(2,1)S(1)}, bf16[192,896]{1,0:T(8,128)(2,1)S(1)}, u32[]{:S(2)}, u32[]{:S(2)}) collective-permute-start(bf16[192,896]{1,0:T(8,128)(2,1)S(1)} %get-tuple-element.62.refs_0_), channel_id=1, source_target_pairs={{0,4},{2,6},{4,0},{6,2},{8,12},{10,14},{12,8},{14,10},{16,20},{18,... | collective-permute-start | bytes 1032200 | tf_op jit(solution)/shard_map/ppermute | solution.py:20
  65.3 4.2 %collective-permute-start.12 = (bf16[128,1536]{1,0:T(8,128)(2,1)S(1)}, bf16[128,1536]{1,0:T(8,128)(2,1)S(1)}, u32[]{:S(2)}, u32[]{:S(2)}) collective-permute-start(bf16[128,1536]{1,0:T(8,128)(2,1)S(1)} %get-tuple-element.73.refs_0_), channel_id=1, source_target_pairs={{1,17},{3,19},{5,21},{7,23},{9,25},{11,27},{13,29},{15,31},{17,1},... | collective-permute-start | bytes 1179656 | tf_op jit(solution)/shard_map/ppermute | solution.py:20
  66.0 18.9 %collective-permute-start.10 = (bf16[256,896]{1,0:T(8,128)(2,1)S(1)}, bf16[256,896]{1,0:T(8,128)(2,1)S(1)}, u32[]{:S(2)}, u32[]{:S(2)}) collective-permute-start(bf16[256,896]{1,0:T(8,128)(2,1)S(1)} %get-tuple-element.70), channel_id=1, source_target_pairs={{1,0},{3,2},{5,4},{7,6},{9,8},{11,10},{13,12},{15,14},{17,16},{19,... | collective-permute-start | bytes 1376264 | tf_op jit(solution)/shard_map/ppermute | solution.py:25
  67.3 13.5 %collective-permute-start.9 = (bf16[192,768]{1,0:T(8,128)(2,1)S(1)}, bf16[192,768]{1,0:T(8,128)(2,1)S(1)}, u32[]{:S(2)}, u32[]{:S(2)}) collective-permute-start(bf16[192,768]{1,0:T(8,128)(2,1)S(1)} %get-tuple-element.68.refs_0_), channel_id=1, source_target_pairs={{0,12},{2,14},{4,8},{6,10},{8,4},{10,6},{12,0},{14,2},{16,28},{18,... | collective-permute-start | bytes 884744 | tf_op jit(solution)/shard_map/ppermute | solution.py:20
  69.5 19.4 %collective-permute-start.15 = (bf16[128,1024]{1,0:T(8,128)(2,1)S(1)}, bf16[128,1024]{1,0:T(8,128)(2,1)S(1)}, u32[]{:S(2)}, u32[]{:S(2)}) collective-permute-start(bf16[128,1024]{1,0:T(8,128)(2,1)S(1)} %get-tuple-element.77.refs_0_), channel_id=1, source_target_pairs={{1,33},{3,35},{5,37},{7,39},{9,41},{11,43},{13,45},{15,47},{17,49}... | collective-permute-start | bytes 786440 | tf_op jit(solution)/shard_map/ppermute | solution.py:20
  70.2 25.8 %collective-permute-start.13 = (bf16[256,768]{1,0:T(8,128)(2,1)S(1)}, bf16[256,768]{1,0:T(8,128)(2,1)S(1)}, u32[]{:S(2)}, u32[]{:S(2)}) collective-permute-start(bf16[256,768]{1,0:T(8,128)(2,1)S(1)} %get-tuple-element.74), channel_id=1, source_target_pairs={{1,0},{3,2},{5,4},{7,6},{9,8},{11,10},{13,12},{15,14},{17,16},{19,... | collective-permute-start | bytes 1179656 | tf_op jit(solution)/shard_map/ppermute | solution.py:25
  85.3 8.1 %collective-permute-start.11 = (bf16[192,640]{1,0:T(8,128)(2,1)S(1)}, bf16[192,640]{1,0:T(8,128)(2,1)S(1)}, u32[]{:S(2)}, u32[]{:S(2)}) collective-permute-start(bf16[192,640]{1,0:T(8,128)(2,1)S(1)} %get-tuple-element.72.refs_0_), channel_id=1, source_target_pairs={{0,16},{2,18},{4,20},{6,22},{8,24},{10,26},{12,28},{14,30},{16,0},... | collective-permute-start | bytes 737288 | tf_op jit(solution)/shard_map/ppermute | solution.py:20
  89.0 9.7 %collective-permute-start.18 = (bf16[128,640]{1,0:T(8,128)(2,1)S(1)}, bf16[128,640]{1,0:T(8,128)(2,1)S(1)}, u32[]{:S(2)}, u32[]{:S(2)}) collective-permute-start(bf16[128,640]{1,0:T(8,128)(2,1)S(1)} %get-tuple-element.81.refs_0_), channel_id=1, source_target_pairs={{1,97},{3,99},{5,101},{7,103},{9,105},{11,107},{13,109},{15,111},{... | collective-permute-start | bytes 491528 | tf_op jit(solution)/shard_map/ppermute | solution.py:20
  89.7 18.0 %collective-permute-start.16 = (bf16[256,640]{1,0:T(8,128)(2,1)S(1)}, bf16[256,640]{1,0:T(8,128)(2,1)S(1)}, u32[]{:S(2)}, u32[]{:S(2)}) collective-permute-start(bf16[256,640]{1,0:T(8,128)(2,1)S(1)} %get-tuple-element.78), channel_id=1, source_target_pairs={{1,0},{3,2},{5,4},{7,6},{9,8},{11,10},{13,12},{15,14},{17,16},{19,... | collective-permute-start | bytes 983048 | tf_op jit(solution)/shard_map/ppermute | solution.py:25
  96.5 11.2 %collective-permute-start.14 = (bf16[192,512]{1,0:T(8,128)(2,1)S(1)}, bf16[192,512]{1,0:T(8,128)(2,1)S(1)}, u32[]{:S(2)}, u32[]{:S(2)}) collective-permute-start(bf16[192,512]{1,0:T(8,128)(2,1)S(1)} %get-tuple-element.76.refs_0_), channel_id=1, source_target_pairs={{0,32},{2,34},{4,36},{6,38},{8,40},{10,42},{12,44},{14,46},{16,48}... | collective-permute-start | bytes 589832 | tf_op jit(solution)/shard_map/ppermute | solution.py:20
  98.8 2.0 %collective-permute-start.21 = (bf16[128,384]{1,0:T(8,128)(2,1)S(1)}, bf16[128,384]{1,0:T(8,128)(2,1)S(1)}, u32[]{:S(2)}, u32[]{:S(2)}) collective-permute-start(bf16[128,384]{1,0:T(8,128)(2,1)S(1)} %get-tuple-element.85.refs_0_), channel_id=1, source_target_pairs={{1,129},{3,131},{5,133},{7,135},{9,137},{11,139},{13,141},{15,143}... | collective-permute-start | bytes 294920 | tf_op jit(solution)/shard_map/ppermute | solution.py:20
  99.5 16.1 %collective-permute-start.19 = (bf16[256,512]{1,0:T(8,128)(2,1)S(1)}, bf16[256,512]{1,0:T(8,128)(2,1)S(1)}, u32[]{:S(2)}, u32[]{:S(2)}) collective-permute-start(bf16[256,512]{1,0:T(8,128)(2,1)S(1)} %get-tuple-element.82), channel_id=1, source_target_pairs={{1,0},{3,2},{5,4},{7,6},{9,8},{11,10},{13,12},{15,14},{17,16},{19,... | collective-permute-start | bytes 786440 | tf_op jit(solution)/shard_map/ppermute | solution.py:25
  100.8 23.5 %collective-permute-start.27 = (bf16[128,256]{1,0:T(8,128)(2,1)S(1)}, bf16[128,256]{1,0:T(8,128)(2,1)S(1)}, u32[]{:S(2)}, u32[]{:S(2)}) collective-permute-start(bf16[128,256]{1,0:T(8,128)(2,1)S(1)} %get-tuple-element.92.refs_0_), channel_id=1, source_target_pairs={{1,385},{3,387},{5,389},{7,391},{9,393},{11,395},{13,397},{15,399}... | collective-permute-start | bytes 196616 | tf_op jit(solution)/shard_map/ppermute | solution.py:20
  101.5 24.2 %collective-permute-start.22 = (bf16[256,384]{1,0:T(8,128)(2,1)S(1)}, bf16[256,384]{1,0:T(8,128)(2,1)S(1)}, u32[]{:S(2)}, u32[]{:S(2)}) collective-permute-start(bf16[256,384]{1,0:T(8,128)(2,1)S(1)} %get-tuple-element.86), channel_id=1, source_target_pairs={{1,0},{3,2},{5,4},{7,6},{9,8},{11,10},{13,12},{15,14},{17,16},{19,... | collective-permute-start | bytes 589832 | tf_op jit(solution)/shard_map/ppermute | solution.py:25
  108.1 10.6 %collective-permute-start.17 = (bf16[192,384]{1,0:T(8,128)(2,1)S(1)}, bf16[192,384]{1,0:T(8,128)(2,1)S(1)}, u32[]{:S(2)}, u32[]{:S(2)}) collective-permute-start(bf16[192,384]{1,0:T(8,128)(2,1)S(1)} %get-tuple-element.80.refs_0_), channel_id=1, source_target_pairs={{0,96},{2,98},{4,100},{6,102},{8,104},{10,106},{12,108},{14,110},{... | collective-permute-start | bytes 442376 | tf_op jit(solution)/shard_map/ppermute | solution.py:20
  119.0 6.7 %collective-permute-start.20 = (bf16[192,256]{1,0:T(8,128)(2,1)S(1)}, bf16[192,256]{1,0:T(8,128)(2,1)S(1)}, u32[]{:S(2)}, u32[]{:S(2)}) collective-permute-start(bf16[192,256]{1,0:T(8,128)(2,1)S(1)} %get-tuple-element.84.refs_0_), channel_id=1, source_target_pairs={{0,128},{2,130},{4,132},{6,134},{8,136},{10,138},{12,140},{14,142}... | collective-permute-start | bytes 294920 | tf_op jit(solution)/shard_map/ppermute | solution.py:20
  122.4 19.4 %collective-permute-start.23 = (bf16[6,192,128]{2,1,0:T(8,128)(2,1)S(1)}, bf16[6,192,128]{2,1,0:T(8,128)(2,1)S(1)}, u32[]{:S(2)}, u32[]{:S(2)}) collective-permute-start(bf16[6,192,128]{2,1,0:T(8,128)(2,1)S(1)} %get-tuple-element.89), channel_id=1, source_target_pairs={{0,2},{2,0},{4,6},{6,4},{8,10},{10,8},{12,14},{14,12},{16,18},{18,... | collective-permute-start | bytes 884744 | tf_op jit(solution)/shard_map/ppermute | solution.py:20
  124.4 11.4 %collective-permute-start.28 = (bf16[256,256]{1,0:T(8,128)(2,1)S(1)}, bf16[256,256]{1,0:T(8,128)(2,1)S(1)}, u32[]{:S(2)}, u32[]{:S(2)}) collective-permute-start(bf16[256,256]{1,0:T(8,128)(2,1)S(1)} %shard_map.75), channel_id=1, source_target_pairs={{1,0},{3,2},{5,4},{7,6},{9,8},{11,10},{13,12},{15,14},{17,16},{19,... | collective-permute-start | bytes 393224 | tf_op jit(solution)/shard_map/ppermute | solution.py:25
  126.1 18.0 %collective-permute-start.25 = (bf16[6,192,128]{2,1,0:T(8,128)(2,1)S(1)}, bf16[6,192,128]{2,1,0:T(8,128)(2,1)S(1)}, u32[]{:S(2)}, u32[]{:S(2)}) collective-permute-start(bf16[6,192,128]{2,1,0:T(8,128)(2,1)S(1)} %get-tuple-element.89), channel_id=1, source_target_pairs={{2,1},{0,3},{6,5},{4,7},{10,9},{8,11},{14,13},{12,15},{18,17},{16,... | collective-permute-start | bytes 884744 | tf_op jit(solution)/shard_map/ppermute | solution.py:25
  130.4 13.7 %collective-permute-start.24 = (bf16[6,192,128]{2,1,0:T(8,128)(2,1)S(1)}, bf16[6,192,128]{2,1,0:T(8,128)(2,1)S(1)}, u32[]{:S(2)}, u32[]{:S(2)}) collective-permute-start(bf16[6,192,128]{2,1,0:T(8,128)(2,1)S(1)} %get-tuple-element.88.refs_7_), channel_id=1, source_target_pairs={{0,1},{2,3},{4,5},{6,7},{8,9},{10,11},{12,13},{14,15},{16,17},{18,... | collective-permute-start | bytes 884744 | tf_op jit(solution)/shard_map/ppermute | solution.py:25
  131.7 7.2 %collective-permute-start.26 = (bf16[192,128]{1,0:T(8,128)(2,1)S(1)}, bf16[192,128]{1,0:T(8,128)(2,1)S(1)}, u32[]{:S(2)}, u32[]{:S(2)}) collective-permute-start(bf16[192,128]{1,0:T(8,128)(2,1)S(1)} %get-tuple-element.91.refs_0_), channel_id=1, source_target_pairs={{0,384},{2,386},{4,388},{6,390},{8,392},{10,394},{12,396},{14,398}... | collective-permute-start | bytes 147464 | tf_op jit(solution)/shard_map/ppermute | solution.py:20
  139.2 5.8 %collective-permute-start.31 = (bf16[2,192,128]{2,1,0:T(8,128)(2,1)S(1)}, bf16[2,192,128]{2,1,0:T(8,128)(2,1)S(1)}, u32[]{:S(2)}, u32[]{:S(2)}) collective-permute-start(bf16[2,192,128]{2,1,0:T(8,128)(2,1)S(1)} %pad_maximum_fusion.refs_3_), channel_id=1, source_target_pairs={{2,1},{0,3},{6,5},{4,7},{10,9},{8,11},{14,13},{12,15},{18,17},{16,... | collective-permute-start | bytes 294920 | tf_op jit(solution)/shard_map/ppermute | solution.py:25
  140.5 4.5 %collective-permute-start.30 = (bf16[2,192,128]{2,1,0:T(8,128)(2,1)S(1)}, bf16[2,192,128]{2,1,0:T(8,128)(2,1)S(1)}, u32[]{:S(2)}, u32[]{:S(2)}) collective-permute-start(bf16[2,192,128]{2,1,0:T(8,128)(2,1)S(1)} %pad_maximum_fusion.refs_3_), channel_id=1, source_target_pairs={{0,1},{2,3},{4,5},{6,7},{8,9},{10,11},{12,13},{14,15},{16,17},{18,... | collective-permute-start | bytes 294920 | tf_op jit(solution)/shard_map/ppermute | solution.py:25
  141.8 6.5 %collective-permute-start.29 = (bf16[2,192,128]{2,1,0:T(8,128)(2,1)S(1)}, bf16[2,192,128]{2,1,0:T(8,128)(2,1)S(1)}, u32[]{:S(2)}, u32[]{:S(2)}) collective-permute-start(bf16[2,192,128]{2,1,0:T(8,128)(2,1)S(1)} %pad_maximum_fusion.refs_3_), channel_id=1, source_target_pairs={{0,2},{2,0},{4,6},{6,4},{8,10},{10,8},{12,14},{14,12},{16,18},{18,... | collective-permute-start | bytes 294920 | tf_op jit(solution)/shard_map/ppermute | solution.py:20
  (7 other events, 22.6 us)

commit v8 on v7

--- a/solution.py
+++ b/solution.py
@@ -304,11 +304,13 @@
         if level == early:
             near0, theirs = stacks(gathered)
             far0 = swap(theirs, 2, 0)
-        if level == early + 1:
-            near0, theirs, _ = lax.optimization_barrier((near0, theirs, gathered[-1]))
+        if level == levels - 1:
+            near0, theirs, last = lax.optimization_barrier((near0, theirs, gathered[-1]))
+            gathered[-1] = last
+            near_last, theirs_last = stacks(gathered[early:])
+            far_last = swap(theirs_last, 2, 0)
             state = spread_out(state, near0, theirs, far0, 1, zero)
-    near0, theirs = stacks(gathered[early:])
-    return spread_out(state, near0, theirs, swap(theirs, 2, 0), early + 1, None)
+    return spread_out(state, near_last, theirs_last, far_last, early + 1, None)
 
 
 def solution(mesh):

time: 150 us -> 147 us (0.980)
  starting transfers between devices: 55.9 us -> 54 us
    ppermute x14, starting transfers between devices: 21.8 us -> 18.8 us  [to_core(): return lax.ppermute(value, AXIS, pairs)]
  transfers between devices with their start and end apart: 32 -> 32, of which waited for: 15 -> 16; matrix products, arithmetic and copies ran while one was open for 0% -> 0% of each run, Pallas kernels for 4% -> 4%
where the time goes in v8:
time: 147 us; the launch traced here: 146 us
  waiting for transfers between devices  74.4 us (51%)
  starting transfers between devices  54 us (37%)
  Pallas kernels  8.9 us (6%)
  blocking collectives  5.76 us (4%)
  local copies, waits for them, and re-layouts  2.67 us (2%)
    ppermute x18, waiting for transfers between devices, swap(): return lax.ppermute(value, AXIS, pairs)  42.2 us
    ppermute x18, starting transfers between devices, swap(): return lax.ppermute(value, AXIS, pairs)  35.3 us
    ppermute x14, waiting for transfers between devices, to_core(): return lax.ppermute(value, AXIS, pairs)  32.1 us
    ppermute x14, starting transfers between devices, to_core(): return lax.ppermute(value, AXIS, pairs)  18.8 us
    pallas_call x23, Pallas kernels, call(): pl.pallas_call(body, out_shape=outs, grid=grid, in_specs=specs, out_specs...  8.9 us
    all_gather x1, blocking collectives, on_device(): lax.all_gather(sums, AXIS, axis_index_groups=[[d, d + 1] for d in range(0...  5.76 us
  transfers between devices with their start and end apart: 32, of which 16 were waited for; matrix products, arithmetic and copies ran while one was open for 0% of the time, Pallas kernels for 4%

profile of v8, /device:TPU:8, one launch (start us, length us, event | category | flops | bytes accessed | tf_op | source)
XLA Modules:
  0.0 146.4 jit_solution(7095880605178645205)
XLA Ops:
  3.7 1.9 %collective-permute-start = (bf16[128,3584]{1,0:T(8,128)(2,1)S(1)}, bf16[128,3584]{1,0:T(8,128)(2,1)S(1)}, u32[]{:S(2)}, u32[]{:S(2)}) collective-permute-start(bf16[128,3584]{1,0:T(8,128)(2,1)S(1)} %shard_map.56.refs_0_), channel_id=1, source_target_pairs={{0,1},{2,3},{4,5},{6,7},{8,9},{10,11},{12,13},{14,15},{16,17},{18,... | collective-permute-start | bytes 2752520 | tf_op jit(solution)/shard_map/ppermute | solution.py:25
  6.3 1.4 collective-permute-done.refs_1_
  8.6 5.8 %all_gather.3.stacked_ref = bf16[256,384]{1,0:T(8,128)(2,1)S(1)} all-gather(bf16[128,384]{1,0:T(8,128)(2,1)S(1)} %get-tuple-element.54), channel_id=1, replica_groups={{0,1},{2,3},{4,5},{6,7},{8,9},{10,11},{12,13},{14,15},{16,17},{18,19},{..., dimensions={0}, use_global_device_ids=true | all-gather | bytes 294912 | tf_op jit(solution)/shard_map/all_gather | solution.py:222
  14.3 1.4 shard_map.58
  20.2 2.2 %collective-permute-start.2 = (bf16[192,1024]{1,0:T(8,128)(2,1)S(1)}, bf16[192,1024]{1,0:T(8,128)(2,1)S(1)}, u32[]{:S(2)}, u32[]{:S(2)}) collective-permute-start(bf16[192,1024]{1,0:T(8,128)(2,1)S(1)} %get-tuple-element.57), channel_id=1, source_target_pairs={{0,2},{2,0},{4,6},{6,4},{8,10},{10,8},{12,14},{14,12},{16,18},{18,... | collective-permute-start | bytes 1179656 | tf_op jit(solution)/shard_map/ppermute | solution.py:20
  22.4 7.5 %collective-permute-done.2.refs_1_ = bf16[192,1024]{1,0:T(8,128)(2,1)S(1)} collective-permute-done((bf16[192,1024]{1,0:T(8,128)(2,1)S(1)}, bf16[192,1024]{1,0:T(8,128)(2,1)S(1)}, u32[]{:S(2)}, u32[]{:S(2)}) %collective-permute-start.2) | collective-permute-done | bytes 393248 | tf_op jit(solution)/shard_map/ppermute | solution.py:20
  29.9 3.8 %collective-permute-done.4.refs_2_ = bf16[256,1152]{1,0:T(8,128)(2,1)S(1)} collective-permute-done((bf16[256,1152]{1,0:T(8,128)(2,1)S(1)}, bf16[256,1152]{1,0:T(8,128)(2,1)S(1)}, u32[]{:S(2)}, u32[]{:S(2)}) %collective-permute-start.4) | collective-permute-done | bytes 589856 | tf_op jit(solution)/shard_map/ppermute | solution.py:25
  36.2 2.3 %collective-permute-start.6 = (bf16[192,896]{1,0:T(8,128)(2,1)S(1)}, bf16[192,896]{1,0:T(8,128)(2,1)S(1)}, u32[]{:S(2)}, u32[]{:S(2)}) collective-permute-start(bf16[192,896]{1,0:T(8,128)(2,1)S(1)} %get-tuple-element.63.refs_0_), channel_id=1, source_target_pairs={{0,4},{2,6},{4,0},{6,2},{8,12},{10,14},{12,8},{14,10},{16,20},{18,... | collective-permute-start | bytes 1032200 | tf_op jit(solution)/shard_map/ppermute | solution.py:20
  38.5 15.2 %collective-permute-done.6.refs_1_ = bf16[192,896]{1,0:T(8,128)(2,1)S(1)} collective-permute-done((bf16[192,896]{1,0:T(8,128)(2,1)S(1)}, bf16[192,896]{1,0:T(8,128)(2,1)S(1)}, u32[]{:S(2)}, u32[]{:S(2)}) %collective-permute-start.6) | collective-permute-done | bytes 344096 | tf_op jit(solution)/shard_map/ppermute | solution.py:20
  53.7 11.1 %collective-permute-done.7.refs_2_ = bf16[256,1024]{1,0:T(8,128)(2,1)S(1)} collective-permute-done((bf16[256,1024]{1,0:T(8,128)(2,1)S(1)}, bf16[256,1024]{1,0:T(8,128)(2,1)S(1)}, u32[]{:S(2)}, u32[]{:S(2)}) %collective-permute-start.7) | collective-permute-done | bytes 524320 | tf_op jit(solution)/shard_map/ppermute | solution.py:25
  66.0 1.3 collective-permute-start.10
  67.3 2.2 %collective-permute-start.9 = (bf16[192,768]{1,0:T(8,128)(2,1)S(1)}, bf16[192,768]{1,0:T(8,128)(2,1)S(1)}, u32[]{:S(2)}, u32[]{:S(2)}) collective-permute-start(bf16[192,768]{1,0:T(8,128)(2,1)S(1)} %get-tuple-element.69.refs_0_), channel_id=1, source_target_pairs={{0,12},{2,14},{4,8},{6,10},{8,4},{10,6},{12,0},{14,2},{16,28},{18,... | collective-permute-start | bytes 884744 | tf_op jit(solution)/shard_map/ppermute | solution.py:20
  71.5 9.2 %collective-permute-done.9.refs_1_ = bf16[192,768]{1,0:T(8,128)(2,1)S(1)} collective-permute-done((bf16[192,768]{1,0:T(8,128)(2,1)S(1)}, bf16[192,768]{1,0:T(8,128)(2,1)S(1)}, u32[]{:S(2)}, u32[]{:S(2)}) %collective-permute-start.9) | collective-permute-done | bytes 294944 | tf_op jit(solution)/shard_map/ppermute | solution.py:20
  80.7 4.1 %collective-permute-done.10.refs_2_ = bf16[256,896]{1,0:T(8,128)(2,1)S(1)} collective-permute-done((bf16[256,896]{1,0:T(8,128)(2,1)S(1)}, bf16[256,896]{1,0:T(8,128)(2,1)S(1)}, u32[]{:S(2)}, u32[]{:S(2)}) %collective-permute-start.10) | collective-permute-done | bytes 458784 | tf_op jit(solution)/shard_map/ppermute | solution.py:25
  85.3 3.6 %collective-permute-start.11 = (bf16[192,640]{1,0:T(8,128)(2,1)S(1)}, bf16[192,640]{1,0:T(8,128)(2,1)S(1)}, u32[]{:S(2)}, u32[]{:S(2)}) collective-permute-start(bf16[192,640]{1,0:T(8,128)(2,1)S(1)} %get-tuple-element.73.refs_0_), channel_id=1, source_target_pairs={{0,16},{2,18},{4,20},{6,22},{8,24},{10,26},{12,28},{14,30},{16,0},... | collective-permute-start | bytes 737288 | tf_op jit(solution)/shard_map/ppermute | solution.py:20
  91.7 1.6 %collective-permute-done.11.refs_1_ = bf16[192,640]{1,0:T(8,128)(2,1)S(1)} collective-permute-done((bf16[192,640]{1,0:T(8,128)(2,1)S(1)}, bf16[192,640]{1,0:T(8,128)(2,1)S(1)}, u32[]{:S(2)}, u32[]{:S(2)}) %collective-permute-start.11) | collective-permute-done | bytes 245792 | tf_op jit(solution)/shard_map/ppermute | solution.py:20
  93.4 2.7 %collective-permute-done.13.refs_2_ = bf16[256,768]{1,0:T(8,128)(2,1)S(1)} collective-permute-done((bf16[256,768]{1,0:T(8,128)(2,1)S(1)}, bf16[256,768]{1,0:T(8,128)(2,1)S(1)}, u32[]{:S(2)}, u32[]{:S(2)}) %collective-permute-start.13) | collective-permute-done | bytes 393248 | tf_op jit(solution)/shard_map/ppermute | solution.py:25
  96.5 2.2 %collective-permute-start.14 = (bf16[192,512]{1,0:T(8,128)(2,1)S(1)}, bf16[192,512]{1,0:T(8,128)(2,1)S(1)}, u32[]{:S(2)}, u32[]{:S(2)}) collective-permute-start(bf16[192,512]{1,0:T(8,128)(2,1)S(1)} %get-tuple-element.77.refs_0_), channel_id=1, source_target_pairs={{0,32},{2,34},{4,36},{6,38},{8,40},{10,42},{12,44},{14,46},{16,48}... | collective-permute-start | bytes 589832 | tf_op jit(solution)/shard_map/ppermute | solution.py:20
  103.4 4.3 %collective-permute-done.16.refs_2_ = bf16[256,640]{1,0:T(8,128)(2,1)S(1)} collective-permute-done((bf16[256,640]{1,0:T(8,128)(2,1)S(1)}, bf16[256,640]{1,0:T(8,128)(2,1)S(1)}, u32[]{:S(2)}, u32[]{:S(2)}) %collective-permute-start.16) | collective-permute-done | bytes 327712 | tf_op jit(solution)/shard_map/ppermute | solution.py:25
  108.1 4.3 %collective-permute-start.17 = (bf16[192,384]{1,0:T(8,128)(2,1)S(1)}, bf16[192,384]{1,0:T(8,128)(2,1)S(1)}, u32[]{:S(2)}, u32[]{:S(2)}) collective-permute-start(bf16[192,384]{1,0:T(8,128)(2,1)S(1)} %get-tuple-element.81.refs_0_), channel_id=1, source_target_pairs={{0,96},{2,98},{4,100},{6,102},{8,104},{10,106},{12,108},{14,110},{... | collective-permute-start | bytes 442376 | tf_op jit(solution)/shard_map/ppermute | solution.py:20
  112.4 4.0 %collective-permute-done.19.refs_2_ = bf16[256,512]{1,0:T(8,128)(2,1)S(1)} collective-permute-done((bf16[256,512]{1,0:T(8,128)(2,1)S(1)}, bf16[256,512]{1,0:T(8,128)(2,1)S(1)}, u32[]{:S(2)}, u32[]{:S(2)}) %collective-permute-start.19) | collective-permute-done | bytes 262176 | tf_op jit(solution)/shard_map/ppermute | solution.py:25
  116.4 2.3 %collective-permute-done.17.refs_1_ = bf16[192,384]{1,0:T(8,128)(2,1)S(1)} collective-permute-done((bf16[192,384]{1,0:T(8,128)(2,1)S(1)}, bf16[192,384]{1,0:T(8,128)(2,1)S(1)}, u32[]{:S(2)}, u32[]{:S(2)}) %collective-permute-start.17) | collective-permute-done | bytes 147488 | tf_op jit(solution)/shard_map/ppermute | solution.py:20
  119.0 3.4 %collective-permute-start.20 = (bf16[192,256]{1,0:T(8,128)(2,1)S(1)}, bf16[192,256]{1,0:T(8,128)(2,1)S(1)}, u32[]{:S(2)}, u32[]{:S(2)}) collective-permute-start(bf16[192,256]{1,0:T(8,128)(2,1)S(1)} %get-tuple-element.85.refs_0_), channel_id=1, source_target_pairs={{0,128},{2,130},{4,132},{6,134},{8,136},{10,138},{12,140},{14,142}... | collective-permute-start | bytes 294920 | tf_op jit(solution)/shard_map/ppermute | solution.py:20
  122.5 1.9 %collective-permute-start.26 = (bf16[6,192,128]{2,1,0:T(8,128)(2,1)S(1)}, bf16[6,192,128]{2,1,0:T(8,128)(2,1)S(1)}, u32[]{:S(2)}, u32[]{:S(2)}) collective-permute-start(bf16[6,192,128]{2,1,0:T(8,128)(2,1)S(1)} %get-tuple-element.91), channel_id=1, source_target_pairs={{0,2},{2,0},{4,6},{6,4},{8,10},{10,8},{12,14},{14,12},{16,18},{18,... | collective-permute-start | bytes 884744 | tf_op jit(solution)/shard_map/ppermute | solution.py:20
  125.9 4.7 %collective-permute-start.23 = (bf16[192,128]{1,0:T(8,128)(2,1)S(1)}, bf16[192,128]{1,0:T(8,128)(2,1)S(1)}, u32[]{:S(2)}, u32[]{:S(2)}) collective-permute-start(bf16[192,128]{1,0:T(8,128)(2,1)S(1)} %get-tuple-element.88.refs_0_), channel_id=1, source_target_pairs={{0,384},{2,386},{4,388},{6,390},{8,392},{10,394},{12,396},{14,398}... | collective-permute-start | bytes 147464 | tf_op jit(solution)/shard_map/ppermute | solution.py:20
  130.6 2.5 %collective-permute-done.23.refs_1_ = bf16[192,128]{1,0:T(8,128)(2,1)S(1)} collective-permute-done((bf16[192,128]{1,0:T(8,128)(2,1)S(1)}, bf16[192,128]{1,0:T(8,128)(2,1)S(1)}, u32[]{:S(2)}, u32[]{:S(2)}) %collective-permute-start.23) | collective-permute-done | bytes 49184 | tf_op jit(solution)/shard_map/ppermute | solution.py:20
  133.3 1.3 collective-permute-start.28
  134.6 1.3 collective-permute-start.27
  135.9 1.3 collective-permute-start.31
  137.2 1.3 collective-permute-start.30
  138.6 2.8 %collective-permute-start.29 = (bf16[2,192,128]{2,1,0:T(8,128)(2,1)S(1)}, bf16[2,192,128]{2,1,0:T(8,128)(2,1)S(1)}, u32[]{:S(2)}, u32[]{:S(2)}) collective-permute-start(bf16[2,192,128]{2,1,0:T(8,128)(2,1)S(1)} %pad_maximum_fusion.refs_3_), channel_id=1, source_target_pairs={{0,2},{2,0},{4,6},{6,4},{8,10},{10,8},{12,14},{14,12},{16,18},{18,... | collective-permute-start | bytes 294920 | tf_op jit(solution)/shard_map/ppermute | solution.py:20
  142.3 2.8 %collective-permute-done.29.refs_4_ = bf16[2,192,128]{2,1,0:T(8,128)(2,1)S(1)} collective-permute-done((bf16[2,192,128]{2,1,0:T(8,128)(2,1)S(1)}, bf16[2,192,128]{2,1,0:T(8,128)(2,1)S(1)}, u32[]{:S(2)}, u32[]{:S(2)}) %collective-permute-start.29) | collective-permute-done | bytes 98336 | tf_op jit(solution)/shard_map/ppermute | solution.py:20
  (77 shorter events, 28.2 us)
Async XLA Ops:
  3.7 4.0 %collective-permute-start = (bf16[128,3584]{1,0:T(8,128)(2,1)S(1)}, bf16[128,3584]{1,0:T(8,128)(2,1)S(1)}, u32[]{:S(2)}, u32[]{:S(2)}) collective-permute-start(bf16[128,3584]{1,0:T(8,128)(2,1)S(1)} %shard_map.56.refs_0_), channel_id=1, source_target_pairs={{0,1},{2,3},{4,5},{6,7},{8,9},{10,11},{12,13},{14,15},{16,17},{18,... | collective-permute-start | bytes 2752520 | tf_op jit(solution)/shard_map/ppermute | solution.py:25
  7.7 9.3 %collective-permute-start.3 = (bf16[128,3840]{1,0:T(8,128)(2,1)S(1)}, bf16[128,3840]{1,0:T(8,128)(2,1)S(1)}, u32[]{:S(2)}, u32[]{:S(2)}) collective-permute-start(bf16[128,3840]{1,0:T(8,128)(2,1)S(1)} %shard_map.57.refs_0_), channel_id=1, source_target_pairs={{1,3},{3,1},{5,7},{7,5},{9,11},{11,9},{13,15},{15,13},{17,19},{19,... | collective-permute-start | bytes 2949128 | tf_op jit(solution)/shard_map/ppermute | solution.py:20
  15.7 4.2 %collective-permute-start.1 = (bf16[384,1024]{1,0:T(8,128)(2,1)S(1)}, bf16[384,1024]{1,0:T(8,128)(2,1)S(1)}, u32[]{:S(2)}, u32[]{:S(2)}) collective-permute-start(bf16[384,1024]{1,0:T(8,128)(2,1)S(1)} %get-tuple-element.55.own_any), channel_id=1, source_target_pairs={{1,0},{3,2},{5,4},{7,6},{9,8},{11,10},{13,12},{15,14},{17,16},{19,... | collective-permute-start | bytes 2359304 | tf_op jit(solution)/shard_map/ppermute | solution.py:25
  17.1 17.1 %collective-permute-start.5 = (bf16[128,2944]{1,0:T(8,128)(2,1)S(1)}, bf16[128,2944]{1,0:T(8,128)(2,1)S(1)}, u32[]{:S(2)}, u32[]{:S(2)}) collective-permute-start(bf16[128,2944]{1,0:T(8,128)(2,1)S(1)} %get-tuple-element.62.refs_0_), channel_id=1, source_target_pairs={{1,5},{3,7},{5,1},{7,3},{9,13},{11,15},{13,9},{15,11},{17,21},{19,... | collective-permute-start | bytes 2261000 | tf_op jit(solution)/shard_map/ppermute | solution.py:20
  17.8 15.9 %collective-permute-start.4 = (bf16[256,1152]{1,0:T(8,128)(2,1)S(1)}, bf16[256,1152]{1,0:T(8,128)(2,1)S(1)}, u32[]{:S(2)}, u32[]{:S(2)}) collective-permute-start(bf16[256,1152]{1,0:T(8,128)(2,1)S(1)} %get-tuple-element.59), channel_id=1, source_target_pairs={{1,0},{3,2},{5,4},{7,6},{9,8},{11,10},{13,12},{15,14},{17,16},{19,... | collective-permute-start | bytes 1769480 | tf_op jit(solution)/shard_map/ppermute | solution.py:25
  20.2 9.7 %collective-permute-start.2 = (bf16[192,1024]{1,0:T(8,128)(2,1)S(1)}, bf16[192,1024]{1,0:T(8,128)(2,1)S(1)}, u32[]{:S(2)}, u32[]{:S(2)}) collective-permute-start(bf16[192,1024]{1,0:T(8,128)(2,1)S(1)} %get-tuple-element.57), channel_id=1, source_target_pairs={{0,2},{2,0},{4,6},{6,4},{8,10},{10,8},{12,14},{14,12},{16,18},{18,... | collective-permute-start | bytes 1179656 | tf_op jit(solution)/shard_map/ppermute | solution.py:20
  34.2 31.1 %collective-permute-start.8 = (bf16[128,2176]{1,0:T(8,128)(2,1)S(1)}, bf16[128,2176]{1,0:T(8,128)(2,1)S(1)}, u32[]{:S(2)}, u32[]{:S(2)}) collective-permute-start(bf16[128,2176]{1,0:T(8,128)(2,1)S(1)} %get-tuple-element.68.refs_0_), channel_id=1, source_target_pairs={{1,13},{3,15},{5,9},{7,11},{9,5},{11,7},{13,1},{15,3},{17,29},{19,... | collective-permute-start | bytes 1671176 | tf_op jit(solution)/shard_map/ppermute | solution.py:20
  34.9 29.9 %collective-permute-start.7 = (bf16[256,1024]{1,0:T(8,128)(2,1)S(1)}, bf16[256,1024]{1,0:T(8,128)(2,1)S(1)}, u32[]{:S(2)}, u32[]{:S(2)}) collective-permute-start(bf16[256,1024]{1,0:T(8,128)(2,1)S(1)} %get-tuple-element.65), channel_id=1, source_target_pairs={{1,0},{3,2},{5,4},{7,6},{9,8},{11,10},{13,12},{15,14},{17,16},{19,... | collective-permute-start | bytes 1572872 | tf_op jit(solution)/shard_map/ppermute | solution.py:25
  36.2 17.5 %collective-permute-start.6 = (bf16[192,896]{1,0:T(8,128)(2,1)S(1)}, bf16[192,896]{1,0:T(8,128)(2,1)S(1)}, u32[]{:S(2)}, u32[]{:S(2)}) collective-permute-start(bf16[192,896]{1,0:T(8,128)(2,1)S(1)} %get-tuple-element.63.refs_0_), channel_id=1, source_target_pairs={{0,4},{2,6},{4,0},{6,2},{8,12},{10,14},{12,8},{14,10},{16,20},{18,... | collective-permute-start | bytes 1032200 | tf_op jit(solution)/shard_map/ppermute | solution.py:20
  65.3 4.2 %collective-permute-start.12 = (bf16[128,1536]{1,0:T(8,128)(2,1)S(1)}, bf16[128,1536]{1,0:T(8,128)(2,1)S(1)}, u32[]{:S(2)}, u32[]{:S(2)}) collective-permute-start(bf16[128,1536]{1,0:T(8,128)(2,1)S(1)} %get-tuple-element.74.refs_0_), channel_id=1, source_target_pairs={{1,17},{3,19},{5,21},{7,23},{9,25},{11,27},{13,29},{15,31},{17,1},... | collective-permute-start | bytes 1179656 | tf_op jit(solution)/shard_map/ppermute | solution.py:20
  66.0 18.9 %collective-permute-start.10 = (bf16[256,896]{1,0:T(8,128)(2,1)S(1)}, bf16[256,896]{1,0:T(8,128)(2,1)S(1)}, u32[]{:S(2)}, u32[]{:S(2)}) collective-permute-start(bf16[256,896]{1,0:T(8,128)(2,1)S(1)} %get-tuple-element.71), channel_id=1, source_target_pairs={{1,0},{3,2},{5,4},{7,6},{9,8},{11,10},{13,12},{15,14},{17,16},{19,... | collective-permute-start | bytes 1376264 | tf_op jit(solution)/shard_map/ppermute | solution.py:25
  67.3 13.5 %collective-permute-start.9 = (bf16[192,768]{1,0:T(8,128)(2,1)S(1)}, bf16[192,768]{1,0:T(8,128)(2,1)S(1)}, u32[]{:S(2)}, u32[]{:S(2)}) collective-permute-start(bf16[192,768]{1,0:T(8,128)(2,1)S(1)} %get-tuple-element.69.refs_0_), channel_id=1, source_target_pairs={{0,12},{2,14},{4,8},{6,10},{8,4},{10,6},{12,0},{14,2},{16,28},{18,... | collective-permute-start | bytes 884744 | tf_op jit(solution)/shard_map/ppermute | solution.py:20
  69.5 19.4 %collective-permute-start.15 = (bf16[128,1024]{1,0:T(8,128)(2,1)S(1)}, bf16[128,1024]{1,0:T(8,128)(2,1)S(1)}, u32[]{:S(2)}, u32[]{:S(2)}) collective-permute-start(bf16[128,1024]{1,0:T(8,128)(2,1)S(1)} %get-tuple-element.78.refs_0_), channel_id=1, source_target_pairs={{1,33},{3,35},{5,37},{7,39},{9,41},{11,43},{13,45},{15,47},{17,49}... | collective-permute-start | bytes 786440 | tf_op jit(solution)/shard_map/ppermute | solution.py:20
  70.2 25.8 %collective-permute-start.13 = (bf16[256,768]{1,0:T(8,128)(2,1)S(1)}, bf16[256,768]{1,0:T(8,128)(2,1)S(1)}, u32[]{:S(2)}, u32[]{:S(2)}) collective-permute-start(bf16[256,768]{1,0:T(8,128)(2,1)S(1)} %get-tuple-element.75), channel_id=1, source_target_pairs={{1,0},{3,2},{5,4},{7,6},{9,8},{11,10},{13,12},{15,14},{17,16},{19,... | collective-permute-start | bytes 1179656 | tf_op jit(solution)/shard_map/ppermute | solution.py:25
  85.3 8.1 %collective-permute-start.11 = (bf16[192,640]{1,0:T(8,128)(2,1)S(1)}, bf16[192,640]{1,0:T(8,128)(2,1)S(1)}, u32[]{:S(2)}, u32[]{:S(2)}) collective-permute-start(bf16[192,640]{1,0:T(8,128)(2,1)S(1)} %get-tuple-element.73.refs_0_), channel_id=1, source_target_pairs={{0,16},{2,18},{4,20},{6,22},{8,24},{10,26},{12,28},{14,30},{16,0},... | collective-permute-start | bytes 737288 | tf_op jit(solution)/shard_map/ppermute | solution.py:20
  89.0 2.0 %collective-permute-start.18 = (bf16[128,640]{1,0:T(8,128)(2,1)S(1)}, bf16[128,640]{1,0:T(8,128)(2,1)S(1)}, u32[]{:S(2)}, u32[]{:S(2)}) collective-permute-start(bf16[128,640]{1,0:T(8,128)(2,1)S(1)} %get-tuple-element.82.refs_0_), channel_id=1, source_target_pairs={{1,97},{3,99},{5,101},{7,103},{9,105},{11,107},{13,109},{15,111},{... | collective-permute-start | bytes 491528 | tf_op jit(solution)/shard_map/ppermute | solution.py:20
  89.7 18.0 %collective-permute-start.16 = (bf16[256,640]{1,0:T(8,128)(2,1)S(1)}, bf16[256,640]{1,0:T(8,128)(2,1)S(1)}, u32[]{:S(2)}, u32[]{:S(2)}) collective-permute-start(bf16[256,640]{1,0:T(8,128)(2,1)S(1)} %get-tuple-element.79), channel_id=1, source_target_pairs={{1,0},{3,2},{5,4},{7,6},{9,8},{11,10},{13,12},{15,14},{17,16},{19,... | collective-permute-start | bytes 983048 | tf_op jit(solution)/shard_map/ppermute | solution.py:25
  91.0 9.0 %collective-permute-start.21 = (bf16[128,384]{1,0:T(8,128)(2,1)S(1)}, bf16[128,384]{1,0:T(8,128)(2,1)S(1)}, u32[]{:S(2)}, u32[]{:S(2)}) collective-permute-start(bf16[128,384]{1,0:T(8,128)(2,1)S(1)} %get-tuple-element.86.refs_0_), channel_id=1, source_target_pairs={{1,129},{3,131},{5,133},{7,135},{9,137},{11,139},{13,141},{15,143}... | collective-permute-start | bytes 294920 | tf_op jit(solution)/shard_map/ppermute | solution.py:20
  96.5 11.2 %collective-permute-start.14 = (bf16[192,512]{1,0:T(8,128)(2,1)S(1)}, bf16[192,512]{1,0:T(8,128)(2,1)S(1)}, u32[]{:S(2)}, u32[]{:S(2)}) collective-permute-start(bf16[192,512]{1,0:T(8,128)(2,1)S(1)} %get-tuple-element.77.refs_0_), channel_id=1, source_target_pairs={{0,32},{2,34},{4,36},{6,38},{8,40},{10,42},{12,44},{14,46},{16,48}... | collective-permute-start | bytes 589832 | tf_op jit(solution)/shard_map/ppermute | solution.py:20
  98.7 17.6 %collective-permute-start.19 = (bf16[256,512]{1,0:T(8,128)(2,1)S(1)}, bf16[256,512]{1,0:T(8,128)(2,1)S(1)}, u32[]{:S(2)}, u32[]{:S(2)}) collective-permute-start(bf16[256,512]{1,0:T(8,128)(2,1)S(1)} %get-tuple-element.83), channel_id=1, source_target_pairs={{1,0},{3,2},{5,4},{7,6},{9,8},{11,10},{13,12},{15,14},{17,16},{19,... | collective-permute-start | bytes 786440 | tf_op jit(solution)/shard_map/ppermute | solution.py:25
  100.1 2.0 %collective-permute-start.24 = (bf16[128,256]{1,0:T(8,128)(2,1)S(1)}, bf16[128,256]{1,0:T(8,128)(2,1)S(1)}, u32[]{:S(2)}, u32[]{:S(2)}) collective-permute-start(bf16[128,256]{1,0:T(8,128)(2,1)S(1)} %get-tuple-element.89.refs_0_), channel_id=1, source_target_pairs={{1,385},{3,387},{5,389},{7,391},{9,393},{11,395},{13,397},{15,399}... | collective-permute-start | bytes 196616 | tf_op jit(solution)/shard_map/ppermute | solution.py:20
  100.8 23.6 %collective-permute-start.22 = (bf16[256,384]{1,0:T(8,128)(2,1)S(1)}, bf16[256,384]{1,0:T(8,128)(2,1)S(1)}, u32[]{:S(2)}, u32[]{:S(2)}) collective-permute-start(bf16[256,384]{1,0:T(8,128)(2,1)S(1)} %get-tuple-element.87), channel_id=1, source_target_pairs={{1,0},{3,2},{5,4},{7,6},{9,8},{11,10},{13,12},{15,14},{17,16},{19,... | collective-permute-start | bytes 589832 | tf_op jit(solution)/shard_map/ppermute | solution.py:25
  102.1 28.4 %collective-permute-start.25 = (bf16[256,256]{1,0:T(8,128)(2,1)S(1)}, bf16[256,256]{1,0:T(8,128)(2,1)S(1)}, u32[]{:S(2)}, u32[]{:S(2)}) collective-permute-start(bf16[256,256]{1,0:T(8,128)(2,1)S(1)} %shard_map.74), channel_id=1, source_target_pairs={{1,0},{3,2},{5,4},{7,6},{9,8},{11,10},{13,12},{15,14},{17,16},{19,... | collective-permute-start | bytes 393224 | tf_op jit(solution)/shard_map/ppermute | solution.py:25
  108.1 10.6 %collective-permute-start.17 = (bf16[192,384]{1,0:T(8,128)(2,1)S(1)}, bf16[192,384]{1,0:T(8,128)(2,1)S(1)}, u32[]{:S(2)}, u32[]{:S(2)}) collective-permute-start(bf16[192,384]{1,0:T(8,128)(2,1)S(1)} %get-tuple-element.81.refs_0_), channel_id=1, source_target_pairs={{0,96},{2,98},{4,100},{6,102},{8,104},{10,106},{12,108},{14,110},{... | collective-permute-start | bytes 442376 | tf_op jit(solution)/shard_map/ppermute | solution.py:20
  119.0 6.5 %collective-permute-start.20 = (bf16[192,256]{1,0:T(8,128)(2,1)S(1)}, bf16[192,256]{1,0:T(8,128)(2,1)S(1)}, u32[]{:S(2)}, u32[]{:S(2)}) collective-permute-start(bf16[192,256]{1,0:T(8,128)(2,1)S(1)} %get-tuple-element.85.refs_0_), channel_id=1, source_target_pairs={{0,128},{2,130},{4,132},{6,134},{8,136},{10,138},{12,140},{14,142}... | collective-permute-start | bytes 294920 | tf_op jit(solution)/shard_map/ppermute | solution.py:20
  122.5 16.1 %collective-permute-start.26 = (bf16[6,192,128]{2,1,0:T(8,128)(2,1)S(1)}, bf16[6,192,128]{2,1,0:T(8,128)(2,1)S(1)}, u32[]{:S(2)}, u32[]{:S(2)}) collective-permute-start(bf16[6,192,128]{2,1,0:T(8,128)(2,1)S(1)} %get-tuple-element.91), channel_id=1, source_target_pairs={{0,2},{2,0},{4,6},{6,4},{8,10},{10,8},{12,14},{14,12},{16,18},{18,... | collective-permute-start | bytes 884744 | tf_op jit(solution)/shard_map/ppermute | solution.py:20
  125.9 7.2 %collective-permute-start.23 = (bf16[192,128]{1,0:T(8,128)(2,1)S(1)}, bf16[192,128]{1,0:T(8,128)(2,1)S(1)}, u32[]{:S(2)}, u32[]{:S(2)}) collective-permute-start(bf16[192,128]{1,0:T(8,128)(2,1)S(1)} %get-tuple-element.88.refs_0_), channel_id=1, source_target_pairs={{0,384},{2,386},{4,388},{6,390},{8,392},{10,394},{12,396},{14,398}... | collective-permute-start | bytes 147464 | tf_op jit(solution)/shard_map/ppermute | solution.py:20
  133.3 8.1 %collective-permute-start.28 = (bf16[6,192,128]{2,1,0:T(8,128)(2,1)S(1)}, bf16[6,192,128]{2,1,0:T(8,128)(2,1)S(1)}, u32[]{:S(2)}, u32[]{:S(2)}) collective-permute-start(bf16[6,192,128]{2,1,0:T(8,128)(2,1)S(1)} %get-tuple-element.91), channel_id=1, source_target_pairs={{2,1},{0,3},{6,5},{4,7},{10,9},{8,11},{14,13},{12,15},{18,17},{16,... | collective-permute-start | bytes 884744 | tf_op jit(solution)/shard_map/ppermute | solution.py:25
  134.6 6.8 %collective-permute-start.27 = (bf16[6,192,128]{2,1,0:T(8,128)(2,1)S(1)}, bf16[6,192,128]{2,1,0:T(8,128)(2,1)S(1)}, u32[]{:S(2)}, u32[]{:S(2)}) collective-permute-start(bf16[6,192,128]{2,1,0:T(8,128)(2,1)S(1)} %get-tuple-element.90.refs_7_), channel_id=1, source_target_pairs={{0,1},{2,3},{4,5},{6,7},{8,9},{10,11},{12,13},{14,15},{16,17},{18,... | collective-permute-start | bytes 884744 | tf_op jit(solution)/shard_map/ppermute | solution.py:25
  135.9 6.3 %collective-permute-start.31 = (bf16[2,192,128]{2,1,0:T(8,128)(2,1)S(1)}, bf16[2,192,128]{2,1,0:T(8,128)(2,1)S(1)}, u32[]{:S(2)}, u32[]{:S(2)}) collective-permute-start(bf16[2,192,128]{2,1,0:T(8,128)(2,1)S(1)} %pad_maximum_fusion.refs_3_), channel_id=1, source_target_pairs={{2,1},{0,3},{6,5},{4,7},{10,9},{8,11},{14,13},{12,15},{18,17},{16,... | collective-permute-start | bytes 294920 | tf_op jit(solution)/shard_map/ppermute | solution.py:25
  137.2 5.0 %collective-permute-start.30 = (bf16[2,192,128]{2,1,0:T(8,128)(2,1)S(1)}, bf16[2,192,128]{2,1,0:T(8,128)(2,1)S(1)}, u32[]{:S(2)}, u32[]{:S(2)}) collective-permute-start(bf16[2,192,128]{2,1,0:T(8,128)(2,1)S(1)} %pad_maximum_fusion.refs_3_), channel_id=1, source_target_pairs={{0,1},{2,3},{4,5},{6,7},{8,9},{10,11},{12,13},{14,15},{16,17},{18,... | collective-permute-start | bytes 294920 | tf_op jit(solution)/shard_map/ppermute | solution.py:25
  138.6 6.5 %collective-permute-start.29 = (bf16[2,192,128]{2,1,0:T(8,128)(2,1)S(1)}, bf16[2,192,128]{2,1,0:T(8,128)(2,1)S(1)}, u32[]{:S(2)}, u32[]{:S(2)}) collective-permute-start(bf16[2,192,128]{2,1,0:T(8,128)(2,1)S(1)} %pad_maximum_fusion.refs_3_), channel_id=1, source_target_pairs={{0,2},{2,0},{4,6},{6,4},{8,10},{10,8},{12,14},{14,12},{16,18},{18,... | collective-permute-start | bytes 294920 | tf_op jit(solution)/shard_map/ppermute | solution.py:20
  (7 other events, 22.6 us)
